TPU v7x, 32 devices: a whole 2x2x4 slice. The times are simulated.
32 devices in a mesh: group: 2 (over x), leaf: 16 (over z, y, core).
Axes of the slice: x: 2, y: 2, z: 4, core: 2. Of those that a mesh axis runs over, the one named last changes fastest.
Arguments:
- points: bfloat16 [32768, 64], P(('group', 'leaf')), may hold values from -6 to 6
- weights: bfloat16 [32768, 128], P(('group', 'leaf')), may hold values from -6 to 6
- interp: bfloat16 [32768, 256], P(('group', 'leaf')), may hold values from -0.1875 to 0.1875
- cluster_interp: bfloat16 [8192, 512], P(('group', 'leaf')), may hold values from -0.09375 to 0.09375
- skeleton_rows: int32 [32, 256], P(('group', 'leaf')), may hold values from 0 to 1023, as said below
- near_flags: int32 [32, 5], P(('group', 'leaf')), may hold values from 0 to 1, as said below
- cluster_rows: int32 [2, 512], P('group'), may hold values from 0 to 4095, as said below
Outputs:
- potential: bfloat16 [32768, 128], P(('group', 'leaf'))
Inputs may be any that keep to these rules, and one draw needn't show every extreme that they name: `skeleton_rows`: within a row the values are distinct. `near_flags`: the middle column is 1; a column is 0 where the leaf it names lies outside the leaf's group. `cluster_rows`: within a row the values are distinct.
All inputs are finite; a program needn't handle non-finite values.
Results may differ from a plain program's by a relative error of at most 0.0063.
Values may be sent and summed in bfloat16 or wider, within the bound.
No kernel may reach another device: no remote copies, remote signals or barrier semaphores. Data moves between devices by JAX's collectives and lax.ppermute only.
A program may use at most 64 MiB of HBM per device.

v0:
```python
import jax
import jax.numpy as jnp
from jax import lax
from jax.sharding import PartitionSpec as P

block_rows = 2048


def from_behind(value, axis, by):
    length = lax.axis_size(axis)
    pairs = [(i, i + by) for i in range(length) if 0 <= i + by < length]
    return lax.ppermute(value, axis, pairs)


def kernel_tile(targets, sources):
    target_sq_norm_values = jnp.sum(jnp.square(targets.astype(jnp.float32)), axis=1)
    source_norm = jnp.sum(jnp.square(sources.astype(jnp.float32)), axis=1)
    inner_term = lax.dot_general(
        targets, sources, (((1,), (1,)), ((), ())), preferred_element_type=jnp.float32
    )
    scaled = (target_sq_norm_values[:, None] + source_norm[None, :] - 2.0 * inner_term) * (
        2.0 / targets.shape[1]
    )
    return jnp.exp(-scaled).astype(jnp.bfloat16)


def tile_product(targets, sources, source_weights):
    return jnp.dot(
        kernel_tile(targets, sources), source_weights, preferred_element_type=jnp.float32
    )


def add_blocks(running, centres, source_points, source_mass, kept_fn):
    row_total = source_points.shape[0]
    block_size = block_rows if row_total % block_rows == 0 else row_total
    block_count = row_total // block_size

    def one_block(partial_sum, block_index):
        block_start = block_index * block_size
        block_points = lax.dynamic_slice_in_dim(source_points, block_start, block_size, 0)
        block_mass = lax.dynamic_slice_in_dim(source_mass, block_start, block_size, 0)
        kept_rows = kept_fn(block_start + jnp.arange(block_size, dtype=jnp.int32))
        return (
            partial_sum + tile_product(centres, block_points, block_mass * kept_rows[:, None]),
            None,
        )

    running, unused = lax.scan(one_block, running, jnp.arange(block_count, dtype=jnp.int32))
    return running


def on_device(points, weights, interp, cluster_interp, skeleton_rows, near_flags, cluster_rows):
    leaf_here = lax.axis_index("leaf")
    group_here = lax.axis_index("group")
    skeleton_count = interp.shape[1]
    feature_count = points.shape[1]
    flag_count = near_flags.shape[1]
    near_reach = (flag_count - 1) // 2
    nearby_row = near_flags[0]
    skeleton = points[skeleton_rows[0]]
    skeleton_charges = jnp.einsum(
        "ps,pr->sr", interp, weights, preferred_element_type=jnp.float32
    ).astype(jnp.bfloat16)
    near_field = jnp.zeros(weights.shape, jnp.float32)
    for column in range(flag_count):
        offset = column - near_reach
        if offset == 0:
            source_points, source_weights = (points, weights)
        else:
            source_points, source_weights = from_behind((points, weights), "leaf", -offset)
        flag_value = nearby_row[column]
        near_field = near_field + flag_value.astype(jnp.float32) * tile_product(
            points, source_points, source_weights
        )
    offsets = jnp.arange(flag_count, dtype=jnp.int32) - near_reach

    def not_listed(row_ids):
        distance = row_ids // skeleton_count - leaf_here
        listed = jnp.sum(
            (distance[:, None] == offsets[None, :]).astype(jnp.int32) * nearby_row[None, :], axis=1
        )
        return (1 - listed).astype(jnp.bfloat16)

    empty_field = jnp.zeros((skeleton_count, weights.shape[1]), jnp.float32)
    pieces = (
        lax.all_gather(skeleton, "leaf", axis=0, tiled=True),
        lax.all_gather(skeleton_charges, "leaf", axis=0, tiled=True),
    )
    sibling = add_blocks(empty_field, skeleton, pieces[0], pieces[1], not_listed)
    cluster_count = cluster_rows.shape[0]
    member_ids = jnp.transpose(cluster_rows).reshape(-1)
    row_total = member_ids.shape[0]
    row_ids = jnp.arange(row_total, dtype=jnp.int32)
    own_rows = row_ids % cluster_count == leaf_here // 16
    own_point = own_rows & (member_ids // skeleton_count == leaf_here % 16)
    selector = (
        (
            (member_ids % skeleton_count)[:, None]
            == jnp.arange(skeleton_count, dtype=jnp.int32)[None, :]
        )
        & own_point[:, None]
    ).astype(jnp.bfloat16)
    picked = jnp.dot(selector, skeleton, preferred_element_type=jnp.float32)
    own_cluster = jnp.einsum(
        "sk,sr->kr", cluster_interp, skeleton_charges, preferred_element_type=jnp.float32
    )
    spread = jnp.repeat(own_cluster, cluster_count, axis=0) * own_rows[:, None].astype(jnp.float32)
    partial_term = jnp.concatenate([picked, spread], axis=1)
    received = lax.psum_scatter(partial_term, "leaf", scatter_dimension=0, tiled=True)
    cluster_points = received[:, :feature_count].astype(jnp.bfloat16)
    cluster_mass = received[:, feature_count:].astype(jnp.bfloat16)

    def far_rows(row_ids_far):
        return (row_ids_far // row_total != group_here).astype(jnp.bfloat16)

    grouped_points, group_mass = (
        lax.all_gather(cluster_points, "leaf", axis=0, tiled=True),
        lax.all_gather(cluster_mass, "leaf", axis=0, tiled=True),
    )
    pieces = (
        lax.all_gather(grouped_points, "group", axis=0, tiled=True),
        lax.all_gather(group_mass, "group", axis=0, tiled=True),
    )
    distant = add_blocks(empty_field, skeleton, pieces[0], pieces[1], far_rows)
    coarse_field = (sibling + distant).astype(jnp.bfloat16)
    return (near_field + jnp.dot(interp, coarse_field, preferred_element_type=jnp.float32)).astype(
        jnp.bfloat16
    )


def solution(mesh):
    placed = (
        P(("group", "leaf"), None),
        P(("group", "leaf"), None),
        P(("group", "leaf"), None),
        P(("group", "leaf"), None),
        P(("group", "leaf"), None),
        P(("group", "leaf"), None),
        P("group", None),
    )
    return jax.shard_map(
        on_device, mesh=mesh, in_specs=placed, out_specs=P(("group", "leaf"), None), check_vma=False
    )
```

profile of v0, /device:TPU:0, one launch (start us, length us, event | category | flops | bytes accessed | tf_op | source)
XLA Modules:
  0.0 150.3 jit_solution(17988207851937787434)
XLA Ops:
  6.5 0.8 add_select_fusion.3
  7.3 0.7 fusion.71
  8.0 1.1 copy.16
  9.1 0.7 compare_select_fusion
  9.8 0.9 gather_fusion
  10.7 0.3 convolution_convert_fusion
  11.0 0.7 fusion.58
  11.8 0.2 fusion.49
  12.1 1.0 copy.21
  13.2 1.3 collective-permute-start.6
  14.5 1.3 collective-permute-start.7
  15.8 1.3 collective-permute-start.4
  17.1 1.3 collective-permute-start.5
  18.4 3.7 %collective-permute-start.2 = (bf16[1024,64]{0,1:T(8,128)(2,1)S(1)}, bf16[1024,64]{0,1:T(8,128)(2,1)S(1)}, u32[]{:S(2)}, u32[]{:S(2)}) collective-permute-start(bf16[1024,64]{0,1:T(8,128)(2,1)S(1)} %copy-done.2), channel_id=1, source_target_pairs={{0,1},{1,2},{2,3},{3,4},{4,5},{5,6},{6,7},{7,8},{8,9},{9,10},{10,1... | collective-permute-start | bytes 393224 | tf_op jit(solution)/shard_map/ppermute | solution.py:12
  22.1 30.7 %all-gather = bf16[4096,64]{1,0:T(8,128)(2,1)S(1)} all-gather(bf16[256,64]{1,0:T(8,128)(2,1)S(1)} %gather_fusion), channel_id=2, replica_groups=mesh['group'=2,'leaf'=16] {'leaf'}, dimensions={0}, use_global_device_ids=true | all-gather | bytes 557056 | tf_op jit(solution)/shard_map/all_gather | solution.py:86
  52.8 0.6 fusion.84
  54.1 2.4 %fusion.40 = f32[1024,128]{1,0:T(8,128)} fusion(bf16[1024,128]{1,0:T(8,128)(2,1)S(1)} %copy-done.3, bf16[1024,64]{0,1:T(8,128)(2,1)S(1)} %copy-done.2, f32[1024]{0:T(1024)S(1)} %multiply_reduce_fusion.7, f32[]{:T(128)} %bitcast.2), kind=kOutput, calls=%fused_computation.57 | convolution fusion | flops 409075712 | bytes 921604 | tf_op jit(solution)/shard_map/dot_general | solution.py:28
  56.5 0.1 multiply_reduce_fusion.8
  59.1 3.0 %collective-permute-start.3 = (bf16[1024,128]{1,0:T(8,128)(2,1)S(1)}, bf16[1024,128]{1,0:T(8,128)(2,1)}, u32[]{:S(2)}, u32[]{:S(2)}) collective-permute-start(bf16[1024,128]{1,0:T(8,128)(2,1)S(1)} %copy-done.3), channel_id=1, source_target_pairs={{0,1},{1,2},{2,3},{3,4},{4,5},{5,6},{6,7},{7,8},{8,9},{9,10},{10,1... | collective-permute-start | bytes 786440 | tf_op jit(solution)/shard_map/ppermute | solution.py:12
  62.1 1.3 collective-permute-start
  63.5 3.7 %collective-permute-start.1 = (bf16[1024,128]{1,0:T(8,128)(2,1)S(1)}, bf16[1024,128]{1,0:T(8,128)(2,1)S(1)}, u32[]{:S(2)}, u32[]{:S(2)}) collective-permute-start(bf16[1024,128]{1,0:T(8,128)(2,1)S(1)} %copy-done.3), channel_id=1, source_target_pairs={{0,2},{1,3},{2,4},{3,5},{4,6},{5,7},{6,8},{7,9},{8,10},{9,11},{10,... | collective-permute-start | bytes 786440 | tf_op jit(solution)/shard_map/ppermute | solution.py:12
  67.3 2.4 %fusion.38 = f32[1024,128]{1,0:T(8,128)} fusion(bf16[1024,128]{1,0:T(8,128)(2,1)S(1)} %collective-permute-done.7, bf16[1024,64]{0,1:T(8,128)(2,1)S(1)} %copy-done.2, bf16[1024,64]{0,1:T(8,128)(2,1)S(1)} %collective-permute-done.6, f32[1024]{0:T(1024)S(1)} %multiply_reduce_fusion.3, f32[1024]{0:T(1024)S(1)} %multiply_reduce_fusion.7, f32[]{:T(128)} %bitcast.4), kind=kOutput, calls=%fused_computation.55 | convolution fusion | flops 409075712 | bytes 1056772 | tf_op jit(solution)/shard_map/dot_general | solution.py:28
  69.6 2.4 %fusion.39 = f32[1024,128]{1,0:T(8,128)} fusion(bf16[1024,128]{1,0:T(8,128)(2,1)S(1)} %collective-permute-done.5, bf16[1024,64]{0,1:T(8,128)(2,1)S(1)} %copy-done.2, bf16[1024,64]{0,1:T(8,128)(2,1)S(1)} %collective-permute-done.4, f32[1024]{0:T(1024)S(1)} %multiply_reduce_fusion.4, f32[1024]{0:T(1024)S(1)} %multiply_reduce_fusion.7, f32[]{:T(128)} %bitcast.3), kind=kOutput, calls=%fused_computation.56 | convolution fusion | flops 409075712 | bytes 1056772 | tf_op jit(solution)/shard_map/dot_general | solution.py:28
  72.0 3.3 %fusion.41 = f32[1024,128]{1,0:T(8,128)} fusion(bf16[1024,128]{1,0:T(8,128)(2,1)} %collective-permute-done.3, bf16[1024,64]{0,1:T(8,128)(2,1)S(1)} %copy-done.2, bf16[1024,64]{0,1:T(8,128)(2,1)S(1)} %collective-permute-done.2, f32[1024]{0:T(1024)S(1)} %multiply_reduce_fusion.5, f32[1024]{0:T(1024)S(1)} %multiply_reduce_fusion.7, f32[]{:T(128)} %bitcast.1), kind=kOutput, calls=%fused_computation.58 | convolution fusion | flops 409075712 | bytes 1056772 | tf_op jit(solution)/shard_map/dot_general | solution.py:28
  75.3 0.9 slice.38
  76.2 0.1 copy.24
  76.4 0.8 slice.37
  77.1 0.1 copy.23
  77.2 0.1 copy.17
  77.3 21.3 %all_gather.20 = bf16[512,64]{1,0:T(8,128)(2,1)S(1)} all-gather(bf16[32,64]{1,0:T(8,128)(2,1)S(1)} %copy.17), channel_id=1, replica_groups=mesh['group'=2,'leaf'=16] {'leaf'}, dimensions={0}, use_global_device_ids=true | all-gather | bytes 69632 | tf_op jit(solution)/shard_map/all_gather | solution.py:117
  98.6 6.4 %all_gather.21 = bf16[1024,64]{1,0:T(8,128)(2,1)S(1)} all-gather(bf16[512,64]{1,0:T(8,128)(2,1)S(1)} %all_gather.20), channel_id=1, replica_groups=mesh['group'=2,'leaf'=16] {'group'}, dimensions={0}, use_global_device_ids=true | all-gather | bytes 196608 | tf_op jit(solution)/shard_map/all_gather | solution.py:121
  105.0 17.8 %all_gather.22 = bf16[512,128]{1,0:T(8,128)(2,1)S(1)} all-gather(bf16[32,128]{1,0:T(8,128)(2,1)S(1)} %copy.18), channel_id=1, replica_groups=mesh['group'=2,'leaf'=16] {'leaf'}, dimensions={0}, use_global_device_ids=true | all-gather | bytes 139264 | tf_op jit(solution)/shard_map/all_gather | solution.py:118
  122.9 6.6 %all_gather.23 = bf16[1024,128]{1,0:T(8,128)(2,1)S(1)} all-gather(bf16[512,128]{1,0:T(8,128)(2,1)S(1)} %all_gather.22), channel_id=1, replica_groups=mesh['group'=2,'leaf'=16] {'group'}, dimensions={0}, use_global_device_ids=true | all-gather | bytes 393216 | tf_op jit(solution)/shard_map/all_gather | solution.py:122
  129.5 0.2 multiply_reduce_fusion.2
  129.7 8.5 %while.17 = (s32[]{:T(128)}, f32[256,128]{1,0:T(8,128)S(1)}, bf16[256,64]{1,0:T(8,128)(2,1)S(1)}, s32[2]{0:T(128)S(1)}, bf16[4096,64]{1,0:T(8,128)(2,1)S(1)}, /*...) while((s32[]{:T(128)}, f32[256,128]{1,0:T(8,128)S(1)}, ...), condition=%wide.region_9.0_spmd.clone, body=%wide.region_5.9_spmd.clone.sunk | while | flops 206094096 | bytes 1732352 | solution.py:48
  129.8 0.6 dynamic_slice.44
  131.0 0.3 multiply_reduce_fusion.11
  131.5 0.1 multiply_reduce_fusion.12
  131.6 2.4 %fusion.119 = f32[256,128]{1,0:T(8,128)S(1)} fusion(bf16[256,64]{1,0:T(8,128)(2,1)S(1)} %get-tuple-element.263, f32[2048]{0:T(1024)S(1)} %multiply_reduce_fusion.11, f32[256]{0:T(256)S(1)} %multiply_reduce_fusion.12, bf16[4096,128]{1,0:T(8,128)(2,1)} %get-tuple-element.266, s32[]{:T(128)S(6)} %select_n.112, ...), kind=kOutput, calls=%fused_computation.10.clone.1 | convolution fusion | flops 205586432 | bytes 1391104 | tf_op jit(solution)/shard_map/while/body/eval_jaxpr/dot_general | solution.py:28
  134.0 0.6 dynamic_slice.44
  135.2 0.3 multiply_reduce_fusion.11
  135.7 0.1 multiply_reduce_fusion.12
  135.9 2.4 %fusion.119 = f32[256,128]{1,0:T(8,128)S(1)} fusion(bf16[256,64]{1,0:T(8,128)(2,1)S(1)} %get-tuple-element.263, f32[2048]{0:T(1024)S(1)} %multiply_reduce_fusion.11, f32[256]{0:T(256)S(1)} %multiply_reduce_fusion.12, bf16[4096,128]{1,0:T(8,128)(2,1)} %get-tuple-element.266, s32[]{:T(128)S(6)} %select_n.112, ...), kind=kOutput, calls=%fused_computation.10.clone.1 | convolution fusion | flops 205586432 | bytes 1391104 | tf_op jit(solution)/shard_map/while/body/eval_jaxpr/dot_general | solution.py:28
  138.2 0.5 fusion.51
  138.8 0.3 convolution_bitcast_fusion
  139.1 0.7 copy-done.7
  139.8 0.2 copy-done.8
  140.0 3.5 %fusion.48 = bf16[1024,128]{1,0:T(8,128)(2,1)} fusion(f32[1024,128]{1,0:T(8,128)S(1)} %convolution_bitcast_fusion, f32[1024,128]{1,0:T(8,128)S(1)} %copy-done.8, f32[1024,128]{1,0:T(8,128)} %fusion.39, f32[1024,128]{1,0:T(8,128)S(1)} %copy-done.7, f32[1024,128]{1,0:T(8,128)} %fusion.41, bf16[1024,128]{1,0:T(8,128)(2,1)S(1)} %collective-permute-done.1, ...), kind=kOutput, calls=%fused_computation.65 | convolution fusion | flops 409862144 | bytes 3416068 | tf_op jit(solution)/shard_map/dot_general | solution.py:28
  (49 shorter events, 0.7 us)
Async XLA Ops:
  6.5 4.1 %copy-start = (bf16[1024,256]{1,0:T(8,128)(2,1)S(1)}, bf16[1024,256]{1,0:T(8,128)(2,1)}, u32[]{:S(2)}) copy-start(bf16[1024,256]{1,0:T(8,128)(2,1)} %param.11) | copy-start | bytes 1572868
  6.5 4.1 %copy-start.3 = (bf16[1024,128]{1,0:T(8,128)(2,1)S(1)}, bf16[1024,128]{1,0:T(8,128)(2,1)}, u32[]{:S(2)}) copy-start(bf16[1024,128]{1,0:T(8,128)(2,1)} %param.10) | copy-start | bytes 786436
  6.5 68.8 %reduce-scatter.4.cloned.1.call-start = ((), (), s32[]{:S(2)}) async-start(), calls=%async_computation.2 | async-start | bytes 557056
  8.0 3.8 %copy-start.4 = (bf16[256,512]{1,0:T(8,128)(2,1)S(1)}, bf16[256,512]{1,0:T(8,128)(2,1)}, u32[]{:S(2)}) copy-start(bf16[256,512]{1,0:T(8,128)(2,1)} %param.12) | copy-start | bytes 786436
  11.0 2.0 %copy-start.1 = (bf16[256,128]{1,0:T(8,128)(2,1)}, bf16[256,128]{1,0:T(8,128)(2,1)S(1)}, u32[]{:S(2)}) copy-start(bf16[256,128]{1,0:T(8,128)(2,1)S(1)} %convolution_convert_fusion) | copy-start | bytes 196612
  12.0 1.1 copy-start.2
  13.1 39.7 %copy-start.5 = (s32[1,5]{1,0:T(1,128)S(1)}, s32[1,5]{1,0:T(1,128)}, u32[]{:S(2)}) copy-start(s32[1,5]{1,0:T(1,128)} %param.14) | copy-start | bytes 64
  13.1 116.6 %all-gather.3.cloned.1.call-start = ((), (), s32[]{:S(2)}) async-start(), calls=%async_computation.1 | async-start | bytes 1114112 | tf_op jit(solution)/shard_map/all_gather | solution.py:87
  13.2 45.9 %collective-permute-start.6 = (bf16[1024,64]{0,1:T(8,128)(2,1)S(1)}, bf16[1024,64]{0,1:T(8,128)(2,1)S(1)}, u32[]{:S(2)}, u32[]{:S(2)}) collective-permute-start(bf16[1024,64]{0,1:T(8,128)(2,1)S(1)} %copy-done.2), channel_id=1, source_target_pairs={{2,0},{3,1},{4,2},{5,3},{6,4},{7,5},{8,6},{9,7},{10,8},{11,9},{12,... | collective-permute-start | bytes 393224 | tf_op jit(solution)/shard_map/ppermute | solution.py:12
  14.5 52.8 %collective-permute-start.7 = (bf16[1024,128]{1,0:T(8,128)(2,1)S(1)}, bf16[1024,128]{1,0:T(8,128)(2,1)S(1)}, u32[]{:S(2)}, u32[]{:S(2)}) collective-permute-start(bf16[1024,128]{1,0:T(8,128)(2,1)S(1)} %copy-done.3), channel_id=1, source_target_pairs={{2,0},{3,1},{4,2},{5,3},{6,4},{7,5},{8,6},{9,7},{10,8},{11,9},{12,... | collective-permute-start | bytes 786440 | tf_op jit(solution)/shard_map/ppermute | solution.py:12
  15.8 46.3 %collective-permute-start.4 = (bf16[1024,64]{0,1:T(8,128)(2,1)S(1)}, bf16[1024,64]{0,1:T(8,128)(2,1)S(1)}, u32[]{:S(2)}, u32[]{:S(2)}) collective-permute-start(bf16[1024,64]{0,1:T(8,128)(2,1)S(1)} %copy-done.2), channel_id=1, source_target_pairs={{1,0},{2,1},{3,2},{4,3},{5,4},{6,5},{7,6},{8,7},{9,8},{10,9},{11,1... | collective-permute-start | bytes 393224 | tf_op jit(solution)/shard_map/ppermute | solution.py:12
  17.1 52.6 %collective-permute-start.5 = (bf16[1024,128]{1,0:T(8,128)(2,1)S(1)}, bf16[1024,128]{1,0:T(8,128)(2,1)S(1)}, u32[]{:S(2)}, u32[]{:S(2)}) collective-permute-start(bf16[1024,128]{1,0:T(8,128)(2,1)S(1)} %copy-done.3), channel_id=1, source_target_pairs={{1,0},{2,1},{3,2},{4,3},{5,4},{6,5},{7,6},{8,7},{9,8},{10,9},{11,1... | collective-permute-start | bytes 786440 | tf_op jit(solution)/shard_map/ppermute | solution.py:12
  18.4 45.1 %collective-permute-start.2 = (bf16[1024,64]{0,1:T(8,128)(2,1)S(1)}, bf16[1024,64]{0,1:T(8,128)(2,1)S(1)}, u32[]{:S(2)}, u32[]{:S(2)}) collective-permute-start(bf16[1024,64]{0,1:T(8,128)(2,1)S(1)} %copy-done.2), channel_id=1, source_target_pairs={{0,1},{1,2},{2,3},{3,4},{4,5},{5,6},{6,7},{7,8},{8,9},{9,10},{10,1... | collective-permute-start | bytes 393224 | tf_op jit(solution)/shard_map/ppermute | solution.py:12
  59.1 12.9 %collective-permute-start.3 = (bf16[1024,128]{1,0:T(8,128)(2,1)S(1)}, bf16[1024,128]{1,0:T(8,128)(2,1)}, u32[]{:S(2)}, u32[]{:S(2)}) collective-permute-start(bf16[1024,128]{1,0:T(8,128)(2,1)S(1)} %copy-done.3), channel_id=1, source_target_pairs={{0,1},{1,2},{2,3},{3,4},{4,5},{5,6},{6,7},{7,8},{8,9},{9,10},{10,1... | collective-permute-start | bytes 786440 | tf_op jit(solution)/shard_map/ppermute | solution.py:12
  62.1 5.1 %collective-permute-start = (bf16[1024,64]{0,1:T(8,128)(2,1)S(1)}, bf16[1024,64]{0,1:T(8,128)(2,1)S(1)}, u32[]{:S(2)}, u32[]{:S(2)}) collective-permute-start(bf16[1024,64]{0,1:T(8,128)(2,1)S(1)} %copy-done.2), channel_id=1, source_target_pairs={{0,2},{1,3},{2,4},{3,5},{4,6},{5,7},{6,8},{7,9},{8,10},{9,11},{10,... | collective-permute-start | bytes 393224 | tf_op jit(solution)/shard_map/ppermute | solution.py:12
  63.5 75.6 %collective-permute-start.1 = (bf16[1024,128]{1,0:T(8,128)(2,1)S(1)}, bf16[1024,128]{1,0:T(8,128)(2,1)S(1)}, u32[]{:S(2)}, u32[]{:S(2)}) collective-permute-start(bf16[1024,128]{1,0:T(8,128)(2,1)S(1)} %copy-done.3), channel_id=1, source_target_pairs={{0,2},{1,3},{2,4},{3,5},{4,6},{5,7},{6,8},{7,9},{8,10},{9,11},{10,... | collective-permute-start | bytes 786440 | tf_op jit(solution)/shard_map/ppermute | solution.py:12
  75.3 54.4 %copy-start.6 = (f32[256,128]{1,0:T(8,128)S(1)}, f32[256,128]{1,0:T(8,128)}, u32[]{:S(2)}) copy-start(f32[256,128]{1,0:T(8,128)} %custom-call) | copy-start | bytes 393220
  138.8 1.0 copy-start.7
  138.8 1.2 copy-start.8
Sparse Core Ops, SparseCore 0:
  13.2 59.0 reduce-scatter.3
  74.7 37.3 all-gather.2
where the time goes:
time: 151 us; the launch traced here: 150 us
  blocking collectives  82.8 us (55%)
  matrix products  20.8 us (14%)
  starting transfers between devices  16.8 us (11%)
  between operations  16.8 us (11%)
  local copies, waits for them, and re-layouts  7.73 us (5%)
  other arithmetic  3.86 us (3%)
    all_gather x1, blocking collectives, on_device(): lax.all_gather(skeleton, 'leaf', axis=0, tiled=True)  30.7 us
    all_gather x1, blocking collectives, on_device(): lax.all_gather(cluster_points, 'leaf', axis=0, tiled=True)  21.3 us
    dot_general x8, matrix products, tile_product(): jnp.dot(kernel_tile(targets, sources), source_weights, preferred_element_...  19.2 us
    all_gather x1, blocking collectives, on_device(): lax.all_gather(cluster_mass, 'leaf', axis=0, tiled=True)  17.8 us
    ppermute x8, starting transfers between devices, from_behind(): return lax.ppermute(value, axis, pairs)  16.8 us
    all_gather x1, blocking collectives, on_device(): lax.all_gather(group_mass, 'group', axis=0, tiled=True)  6.59 us
    all_gather x1, blocking collectives, on_device(): lax.all_gather(grouped_points, 'group', axis=0, tiled=True)  6.41 us
    unnamed x22, local copies, waits for them, and re-layouts  3.27 us
  transfers between devices with their start and end apart: 10, of which 0 were waited for; matrix products, arithmetic and copies ran while one was open for 14% of the time, Pallas kernels for 0%

commit v1 on v0

v1 whole, which is shorter than its diff:
```python
import functools
import math

import jax
import jax.numpy as jnp
from jax import lax
from jax.experimental import pallas as pl
from jax.experimental.pallas import tpu as pltpu
from jax.sharding import PartitionSpec as P

BF16 = jnp.bfloat16
F32 = jnp.float32
VMEM_BYTES = 24 * 1024 * 1024
TARGET_ROWS = 256
SOURCE_ROWS = 512


def vmem():
    return pl.BlockSpec(memory_space=pltpu.VMEM)


def smem():
    return pl.BlockSpec(memory_space=pltpu.SMEM)


def call(body, outs, ins, scratch=(), flops=0, moved=0):
    specs, args = [], []
    for item in ins:
        if isinstance(item, tuple):
            specs.append(smem())
            args.append(item[0])
        else:
            specs.append(vmem())
            args.append(item)
    return pl.pallas_call(
        body,
        out_shape=[jax.ShapeDtypeStruct(shape, dtype) for shape, dtype in outs],
        in_specs=specs,
        out_specs=[vmem() for _ in outs],
        scratch_shapes=[pltpu.VMEM(shape, dtype) for shape, dtype in scratch],
        compiler_params=pltpu.CompilerParams(vmem_limit_bytes=VMEM_BYTES),
        cost_estimate=pl.CostEstimate(flops=flops, bytes_accessed=moved, transcendentals=0),
    )(*args)


def dot_nt(a, b):
    return lax.dot_general(a, b, (((1,), (1,)), ((), ())), preferred_element_type=F32)


def dot_tn(a, b):
    return lax.dot_general(a, b, (((0,), (0,)), ((), ())), preferred_element_type=F32)


def dot_nn(a, b):
    return jnp.dot(a, b, preferred_element_type=F32)


def pack_halves(values):
    half = values.shape[0] // 2
    return jnp.concatenate([values[:half], values[half:]], axis=1)


def extended(values, features, as_target):
    lane = lax.broadcasted_iota(jnp.int32, values.shape, 1)
    kept = jnp.where(lane < features, values, 0.0)
    norm = -0.5 * jnp.sum(kept * kept, axis=1, keepdims=True)
    high = norm.astype(BF16).astype(F32)
    rest = norm - high
    middle = rest.astype(BF16).astype(F32)
    low = rest - middle
    first = features if as_target else features + 3
    ones = features + 3 if as_target else features
    out = jnp.where((lane >= ones) & (lane < ones + 3), 1.0, kept)
    out = jnp.where(lane == first, high, out)
    out = jnp.where(lane == first + 1, middle, out)
    out = jnp.where(lane == first + 2, low, out)
    return out.astype(BF16)


def extended_halves(packed, features, as_target):
    wide = packed.astype(F32)
    return (
        extended(wide, features, as_target),
        extended(pltpu.roll(wide, features, 1), features, as_target),
    )


def exponent_scale(features):
    return 4.0 / features * math.log2(math.e)


def kernel_values(targets, sources, features):
    return jnp.exp2(dot_nt(targets, sources) * exponent_scale(features)).astype(BF16)


def product(targets, source_ref, mass_ref, first, rows, features, mass_first=0):
    total = None
    step = min(SOURCE_ROWS, rows)
    for start in range(0, rows, step):
        tile = kernel_values(targets, source_ref[first + start : first + start + step, :], features)
        term = dot_nn(tile, mass_ref[mass_first + start : mass_first + start + step, :])
        total = term if total is None else total + term
    return total


def xor_exchange(value, axis, mask):
    return lax.ppermute(value, axis, [(i, i ^ mask) for i in range(lax.axis_size(axis))])


def pack_kernel(points_ref, weights_ref, halo_ref):
    half = points_ref.shape[0] // 2
    halo_ref[:half, :] = pack_halves(points_ref[...].astype(F32)).astype(BF16)
    halo_ref[half:, :] = weights_ref[...]


def skeleton_kernel(
    points_ref, weights_ref, interp_ref, ci_ref, rows_ref, ids_ref, sv_ref, sum_ref, send_ref, u_ref, c_ref
):
    leaf = lax.axis_index("leaf")
    points, skeleton_count = points_ref.shape[0], interp_ref.shape[1]
    cluster_count, picked = ids_ref.shape
    members = lax.axis_size("leaf") // cluster_count
    core = leaf % 2
    one = (
        lax.broadcasted_iota(jnp.int32, (points, skeleton_count), 0) == rows_ref[...]
    ).astype(F32).astype(BF16)
    skeleton = dot_tn(one, points_ref[...])
    charges = dot_tn(interp_ref[...], weights_ref[...]).astype(BF16)
    half = skeleton_count // 2
    sv_ref[:half, :] = pack_halves(skeleton).astype(BF16)
    sv_ref[half:, :] = charges
    u_ref[...] = dot_tn(ci_ref[...], charges)
    ids = ids_ref[pl.ds(leaf // members, 1), :] - (leaf % members) * skeleton_count
    chosen = (
        lax.broadcasted_iota(jnp.int32, (skeleton_count, picked), 0) == ids
    ).astype(F32).astype(BF16)
    cluster = dot_tn(chosen, skeleton.astype(BF16))
    part = picked // 2
    c_ref[: part // 2, :] = pack_halves(cluster[:part])
    c_ref[part // 2 :, :] = pack_halves(cluster[part:])
    sum_ref[:part, :] = u_ref[pl.ds(core * part, part), :]
    sum_ref[part:, :] = c_ref[pl.ds(core * (part // 2), part // 2), :]
    send_ref[:part, :] = u_ref[pl.ds((1 - core) * part, part), :].astype(BF16)
    send_ref[part:, :] = c_ref[pl.ds((1 - core) * (part // 2), part // 2), :].astype(BF16)


def first_add_kernel(flags_ref, sum_ref, got_ref, sv_ref, new_ref, send_ref):
    rows = sum_ref.shape[0]
    half = send_ref.shape[0] - 16 - rows
    total = sum_ref[...] + got_ref[...].astype(F32)
    new_ref[...] = total
    send_ref[:rows, :] = total.astype(BF16)
    send_ref[rows : rows + half, :] = sv_ref[:half, :]
    lane = lax.broadcasted_iota(jnp.int32, (16, send_ref.shape[1]), 1)
    row = jnp.zeros(lane.shape, F32)
    for column in range(flags_ref.shape[1]):
        row = jnp.where(lane == column, flags_ref[0, column].astype(F32), row)
    send_ref[rows + half :, :] = row.astype(BF16)


def add_kernel(sum_ref, got_ref, new_ref, send_ref):
    rows = sum_ref.shape[0]
    total = sum_ref[...] + got_ref[:rows, :].astype(F32)
    new_ref[...] = total
    send_ref[...] = total.astype(BF16)


def near_tile(targets_ref, halo_ref, source_ref, near_ref, features):
    half = source_ref.shape[0] // 2
    low, high = extended_halves(halo_ref[:half, :], features, False)
    source_ref[:half, :] = low
    source_ref[half:, :] = high
    for start in range(0, targets_ref.shape[0], TARGET_ROWS):
        rows = slice(start, start + TARGET_ROWS)
        near_ref[rows, :] += product(
            targets_ref[rows, :], source_ref, halo_ref, 0, 2 * half, features, half
        )


def near_kernel(stage, features, flags_ref, own_ref, across_ref, *refs):
    leaf = lax.axis_index("leaf")
    core, chip = leaf % 2, (leaf // 2) % 2
    reach = (flags_ref.shape[1] - 1) // 2
    side, beside = 1 - 2 * core, 1 - 2 * chip
    if stage == 0:
        targets_ref, near_ref, source_ref = refs
        half = targets_ref.shape[0] // 2
        low, high = extended_halves(own_ref[:half, :], features, True)
        targets_ref[:half, :] = low
        targets_ref[half:, :] = high
        near_ref[...] = jnp.zeros_like(near_ref)
        distances, here = (0, side), core == core
    else:
        targets_ref, before_ref, near_ref, source_ref = refs
        near_ref[...] = before_ref[...]
        distances = (2 * beside if stage == 1 else -2 * beside, -side)
        here = core != chip if stage == 1 else core == chip

    @pl.when(flags_ref[0, reach + distances[0]] != 0)
    def _():
        near_tile(targets_ref, own_ref, source_ref, near_ref, features)

    @pl.when((flags_ref[0, reach + distances[1]] != 0) & here)
    def _():
        near_tile(targets_ref, across_ref, source_ref, near_ref, features)


def sibling_kernel(masks, reduced, features, flags_ref, got_ref, *refs):
    pieces, refs = refs[: len(masks)], refs[len(masks) :]
    own_ref, send_ref, low_ref, high_ref, mine_ref, other_ref, targets_ref = refs
    leaf = lax.axis_index("leaf")
    columns = flags_ref.shape[1]
    reach = (columns - 1) // 2
    half = pieces[0].shape[0] // 3
    got_rows = got_ref.shape[0]
    other_points = got_ref[got_rows - 16 - half : got_rows - 16, :]
    other_flags = got_ref[got_rows - 16 :, :].astype(F32)[:1, :]
    lane = lax.broadcasted_iota(jnp.int32, other_flags.shape, 1)
    total = len(masks) * half
    for position, (mask, piece) in enumerate(zip(masks, pieces)):
        source = leaf ^ mask
        rows = slice(position * half, (position + 1) * half)
        later = slice(total + position * half, total + (position + 1) * half)
        low, high = extended_halves(piece[:half, :], features, False)
        low_ref[rows, :] = low
        high_ref[rows, :] = high
        mine = source - leaf + reach
        listed = flags_ref[0, jnp.clip(mine, 0, columns - 1)]
        kept = jnp.where((mine >= 0) & (mine < columns), 1 - listed, 1).astype(F32)
        flagged = jnp.where(lane == source - (leaf ^ reduced) + reach, other_flags, 0.0)
        kept_other = 1.0 - jnp.sum(flagged, axis=1, keepdims=True)
        mass = piece[half:, :].astype(F32)
        for ref, factor in ((mine_ref, kept), (other_ref, kept_other)):
            scaled = (mass * factor).astype(BF16)
            ref[rows, :] = scaled[:half]
            ref[later, :] = scaled[half:]
    for start, packed in ((0, pieces[0][:half, :]), (2 * half, other_points)):
        low, high = extended_halves(packed, features, True)
        targets_ref[start : start + half, :] = low
        targets_ref[start + half : start + 2 * half, :] = high
    for start, mass_ref, out_ref in ((0, mine_ref, own_ref), (2 * half, other_ref, send_ref)):
        targets = targets_ref[start : start + 2 * half, :]
        field = product(targets, low_ref, mass_ref, 0, total, features)
        field += product(targets, high_ref, mass_ref, 0, total, features, total)
        out_ref[...] = field.astype(out_ref.dtype)


def final_kernel(count, features, near_ref, interp_ref, sv_ref, own_ref, got_ref, *refs):
    packs, (out_ref, low_ref, high_ref, mass_ref) = refs[:count], refs[count:]
    half = packs[0].shape[0] // 3
    skeleton_half = sv_ref.shape[0] // 3
    total = count * half
    for position, pack in enumerate(packs):
        rows = slice(position * half, (position + 1) * half)
        later = slice(total + position * half, total + (position + 1) * half)
        low, high = extended_halves(pack[2 * half :, :], features, False)
        low_ref[rows, :] = low
        high_ref[rows, :] = high
        mass_ref[rows, :] = pack[:half, :]
        mass_ref[later, :] = pack[half : 2 * half, :]
    targets = jnp.concatenate(extended_halves(sv_ref[:skeleton_half, :], features, True), axis=0)
    field = own_ref[...] + got_ref[...].astype(F32)
    field += product(targets, low_ref, mass_ref, 0, total, features)
    field += product(targets, high_ref, mass_ref, 0, total, features, total)
    coarse = field.astype(BF16)
    out_ref[...] = (near_ref[...] + dot_nn(interp_ref[...], coarse)).astype(out_ref.dtype)


def on_device(points, weights, interp, cluster_interp, skeleton_rows, near_flags, cluster_rows):
    leaves, groups = lax.axis_size("leaf"), lax.axis_size("group")
    leaf_points, features = points.shape
    columns = weights.shape[1]
    skeletons = interp.shape[1]
    cluster_count, picked = cluster_rows.shape
    members = leaves // cluster_count
    core_mask, chip_mask, reduced = 1, 2, 4
    half, sk_half, part = leaf_points // 2, skeletons // 2, picked // 2
    sum_rows = part + part // 2
    flags = (near_flags,)
    tile_flops = 2 * leaf_points * leaf_points * (2 * features + columns)

    (halo,) = call(pack_kernel, [((half + leaf_points, columns), BF16)], [points, weights], moved=10**6)
    halo_beside = xor_exchange(halo, "leaf", chip_mask)
    halo_core = xor_exchange(halo, "leaf", core_mask)

    skeleton, cluster_sum, cluster_send = call(
        skeleton_kernel,
        [((sk_half * 3, columns), BF16), ((sum_rows, columns), F32), ((sum_rows, columns), BF16)],
        [points, weights, interp, cluster_interp, skeleton_rows, cluster_rows],
        scratch=[((picked, columns), F32), ((part, columns), F32)],
        flops=4 * leaf_points * skeletons * columns,
        moved=2 * 10**6,
    )

    pieces = {0: skeleton}
    mask = leaves // 2
    while mask >= 1:
        if mask != reduced:
            for known in sorted(pieces):
                pieces[known | mask] = xor_exchange(pieces[known], "leaf", mask)
        mask //= 2

    got = xor_exchange(cluster_send, "leaf", core_mask)
    cluster_sum, cluster_send = call(
        first_add_kernel,
        [((sum_rows, columns), F32), ((sum_rows + sk_half + 16, columns), BF16)],
        [flags, cluster_sum, got, skeleton],
        moved=10**6,
    )
    partner = got = xor_exchange(cluster_send, "leaf", reduced)
    mask = chip_mask
    while mask < members:
        if mask != reduced:
            cluster_sum, cluster_send = call(
                add_kernel,
                [((sum_rows, columns), F32), ((sum_rows, columns), BF16)],
                [cluster_sum, got],
                moved=10**6,
            )
            got = xor_exchange(cluster_send, "leaf", mask)
        mask *= 2
    cluster_sum, cluster_send = call(
        add_kernel,
        [((sum_rows, columns), F32), ((sum_rows, columns), BF16)],
        [cluster_sum, got],
        moved=10**6,
    )
    own_group = [cluster_send]
    while mask < leaves:
        own_group += [xor_exchange(pack, "leaf", mask) for pack in own_group]
        mask *= 2
    packs = []
    for shift in range(1, groups):
        pairs = [(i, (i + shift) % groups) for i in range(groups)]
        packs += [lax.ppermute(pack, "group", pairs) for pack in own_group]
    packs += [xor_exchange(pack, "leaf", core_mask) for pack in packs]

    near_outs = ((leaf_points, columns), F32)
    tile_scratch = [((leaf_points, columns), BF16)]
    targets, near = call(
        functools.partial(near_kernel, 0, features),
        [((leaf_points, columns), BF16), near_outs],
        [flags, halo, halo_core],
        scratch=tile_scratch,
        flops=2 * tile_flops,
        moved=3 * 10**6,
    )
    near_step = functools.partial(
        call, outs=[near_outs], scratch=tile_scratch, flops=3 * tile_flops // 2, moved=3 * 10**6
    )
    halo_across = xor_exchange(halo_beside, "leaf", core_mask)
    (near,) = near_step(
        functools.partial(near_kernel, 1, features),
        ins=[flags, halo_beside, halo_across, targets, near],
    )
    ahead = [(i, i + 4) for i in range(leaves - 4) if i & chip_mask == 0]
    behind = [(i, i - 4) for i in range(4, leaves) if i & chip_mask != 0]
    halo_far = lax.ppermute(halo_beside, "leaf", ahead + behind)
    halo_far_across = xor_exchange(halo_far, "leaf", core_mask)
    (near,) = near_step(
        functools.partial(near_kernel, 2, features),
        ins=[flags, halo_far, halo_far_across, targets, near],
    )

    masks = sorted(pieces)
    sources = len(masks) * sk_half
    field, field_send = call(
        functools.partial(sibling_kernel, masks, reduced, features),
        [((skeletons, columns), F32), ((skeletons, columns), BF16)],
        [flags, partner] + [pieces[m] for m in masks],
        scratch=[((sources, columns), BF16)] * 2
        + [((2 * sources, columns), BF16)] * 2
        + [((2 * skeletons, columns), BF16)],
        flops=4 * skeletons * 2 * sources * (2 * features + columns),
        moved=2 * 10**6,
    )
    field_got = xor_exchange(field_send, "leaf", reduced)

    sources = len(packs) * (part // 2)
    (potential,) = call(
        functools.partial(final_kernel, len(packs), features),
        [((leaf_points, columns), BF16)],
        [near, interp, skeleton, field, field_got] + packs,
        scratch=[((sources, columns), BF16)] * 2 + [((2 * sources, columns), BF16)],
        flops=2 * skeletons * 2 * sources * (2 * features + columns),
        moved=2 * 10**6,
    )
    return potential


def solution(mesh):
    placed = (P(("group", "leaf"), None),) * 6 + (P("group", None),)
    return jax.shard_map(
        on_device, mesh=mesh, in_specs=placed, out_specs=P(("group", "leaf"), None), check_vma=False
    )
```

time: 151 us -> 62.8 us (0.42)
  the two profiles are of different devices: /device:TPU:0 before, /device:TPU:5 now
where the time goes in v1:
time: 62.8 us; the launch traced here: 62.1 us
  waiting for transfers between devices  23.7 us (38%)
  Pallas kernels  18.5 us (29%)
  starting transfers between devices  18.5 us (29%)
  local copies, waits for them, and re-layouts  1.15 us (2%)
    ppermute x17, waiting for transfers between devices, xor_exchange(): lax.ppermute(value, axis, [(i, i ^ mask) for i in range(lax.axis_size(axi...  23.7 us
    pallas_call x11, Pallas kernels, call(): pl.pallas_call(body, out_shape=[jax.ShapeDtypeStruct(shape, dtype) for sh...  18.5 us
    ppermute x17, starting transfers between devices, xor_exchange(): lax.ppermute(value, axis, [(i, i ^ mask) for i in range(lax.axis_size(axi...  16 us
    ppermute x1, starting transfers between devices, on_device(): halo_far = lax.ppermute(halo_beside, 'leaf', ahead + behind)  1.28 us
  transfers between devices with their start and end apart: 19, of which 6 were waited for; matrix products, arithmetic and copies ran while one was open for 0% of the time, Pallas kernels for 27%

profile of v1, /device:TPU:5, one launch (start us, length us, event | category | flops | bytes accessed | tf_op | source)
XLA Modules:
  0.0 62.1 jit_solution(8903830940001108583)
XLA Ops:
  0.0 1.1 %copy.8.points_ref = bf16[1024,64]{1,0:T(8,128)(2,1)S(1)} copy(bf16[1024,64]{0,1:T(8,128)(2,1)} %param.7) | data formatting | bytes 262144 | tf_op args[0]
  1.1 0.0 copy-start
  1.1 0.0 copy-start.2
  1.2 0.0 copy-start.3
  1.2 0.0 copy-start.4
  1.2 0.1 shard_map.73.own_ref
  1.3 0.1 collective-permute-start
  1.4 10.0 %collective-permute-done.own_ref = bf16[1536,128]{1,0:T(8,128)(2,1)S(1)} collective-permute-done((bf16[1536,128]{1,0:T(8,128)(2,1)S(1)}, bf16[1536,128]{1,0:T(8,128)(2,1)S(1)}, u32[]{:S(2)}, u32[]{:S(2)}) %collective-permute-start) | collective-permute-done | bytes 393248 | tf_op jit(solution)/shard_map/ppermute | solution.py:107
  11.3 1.3 %collective-permute-start.1 = (bf16[1536,128]{1,0:T(8,128)(2,1)S(1)}, bf16[1536,128]{1,0:T(8,128)(2,1)S(1)}, u32[]{:S(2)}, u32[]{:S(2)}) collective-permute-start(bf16[1536,128]{1,0:T(8,128)(2,1)S(1)} %collective-permute-done.own_ref), channel_id=1, source_target_pairs={{0,4},{1,5},{4,8},{5,9},{8,12},{9,13},{6,2},{7,3},{10,6},{11,7},{1... | collective-permute-start | bytes 1179656 | tf_op jit(solution)/shard_map/ppermute | solution.py:358
  12.7 0.8 %shard_map.77 = (bf16[384,128]{1,0:T(8,128)(2,1)S(1)}, f32[384,128]{1,0:T(8,128)S(1)}, bf16[384,128]{1,0:T(8,128)(2,1)S(1)}) custom-call(bf16[1024,64]{1,0:T(8,128)(2,1)S(1)} %copy.8.points_ref, bf16[1024,128]{1,0:T(8,128)(2,1)S(1)} %copy-done.1, bf16[1024,256]{1,0:T(8,128)(2,1)S(1)} %copy-done, bf16[256,512]{1,0:T(8,128)(2,1)S(1)} %copy-done.2, ...), custom_call_target="tpu_custom_call" | custom-call | flops 134217728 | bytes 2000000 | tf_op jit(solution)/shard_map/pallas_call | solution.py:35
  13.5 1.6 %collective-permute-start.5 = (bf16[384,128]{1,0:T(8,128)(2,1)S(1)}, bf16[384,128]{1,0:T(8,128)(2,1)S(1)}, u32[]{:S(2)}, u32[]{:S(2)}) collective-permute-start(bf16[384,128]{1,0:T(8,128)(2,1)S(1)} %get-tuple-element.23), channel_id=1, source_target_pairs={{0,1},{1,0},{2,3},{3,2},{4,5},{5,4},{6,7},{7,6},{8,9},{9,8},{10,11... | collective-permute-start | bytes 294920 | tf_op jit(solution)/shard_map/ppermute | solution.py:107
  15.1 3.4 %collective-permute-start.10 = (bf16[384,128]{1,0:T(8,128)(2,1)S(1)}, bf16[384,128]{1,0:T(8,128)(2,1)S(1)}, u32[]{:S(2)}, u32[]{:S(2)}) collective-permute-start(bf16[384,128]{1,0:T(8,128)(2,1)S(1)} %get-tuple-element.21.sv_ref.refs_0_), channel_id=1, source_target_pairs={{0,8},{1,9},{2,10},{3,11},{4,12},{5,13},{6,14},{7,15},{8,0},{9,1},... | collective-permute-start | bytes 294920 | tf_op jit(solution)/shard_map/ppermute | solution.py:107
  18.5 1.4 %collective-permute-start.8 = (bf16[384,128]{1,0:T(8,128)(2,1)S(1)}, bf16[384,128]{1,0:T(8,128)(2,1)S(1)}, u32[]{:S(2)}, u32[]{:S(2)}) collective-permute-start(bf16[384,128]{1,0:T(8,128)(2,1)S(1)} %get-tuple-element.21.sv_ref.refs_0_), channel_id=1, source_target_pairs={{0,2},{1,3},{2,0},{3,1},{4,6},{5,7},{6,4},{7,5},{8,10},{9,11},{10,... | collective-permute-start | bytes 294920 | tf_op jit(solution)/shard_map/ppermute | solution.py:107
  19.8 0.0 collective-permute-done.5.got_ref
  19.8 0.6 shard_map.78
  20.4 0.1 collective-permute-start.6
  20.5 0.7 %collective-permute-start.7 = (bf16[384,128]{1,0:T(8,128)(2,1)S(1)}, bf16[384,128]{1,0:T(8,128)(2,1)S(1)}, u32[]{:S(2)}, u32[]{:S(2)}) collective-permute-start(bf16[384,128]{1,0:T(8,128)(2,1)S(1)} %get-tuple-element.21.sv_ref.refs_0_), channel_id=1, source_target_pairs={{0,1},{1,0},{2,3},{3,2},{4,5},{5,4},{6,7},{7,6},{8,9},{9,8},{10,11... | collective-permute-start | bytes 294920 | tf_op jit(solution)/shard_map/ppermute | solution.py:107
  21.2 5.0 %collective-permute-done.10.refs_4_ = bf16[384,128]{1,0:T(8,128)(2,1)S(1)} collective-permute-done((bf16[384,128]{1,0:T(8,128)(2,1)S(1)}, bf16[384,128]{1,0:T(8,128)(2,1)S(1)}, u32[]{:S(2)}, u32[]{:S(2)}) %collective-permute-start.10) | collective-permute-done | bytes 98336 | tf_op jit(solution)/shard_map/ppermute | solution.py:107
  26.2 2.9 %collective-permute-start.3 = (bf16[1536,128]{1,0:T(8,128)(2,1)S(1)}, bf16[1536,128]{1,0:T(8,128)(2,1)S(1)}, u32[]{:S(2)}, u32[]{:S(2)}) collective-permute-start(bf16[1536,128]{1,0:T(8,128)(2,1)S(1)} %shard_map.73.own_ref), channel_id=1, source_target_pairs={{0,1},{1,0},{2,3},{3,2},{4,5},{5,4},{6,7},{7,6},{8,9},{9,8},{10,11... | collective-permute-start | bytes 1179656 | tf_op jit(solution)/shard_map/ppermute | solution.py:107
  29.0 0.0 collective-permute-done.8.refs_2_
  29.0 0.0 collective-permute-start.12
  29.0 0.0 collective-permute-done.7.refs_1_
  29.0 0.1 collective-permute-start.11
  29.1 0.0 collective-permute-done.6.got_ref
  29.1 0.6 %collective-permute-start.4 = (bf16[1536,128]{1,0:T(8,128)(2,1)S(1)}, bf16[1536,128]{1,0:T(8,128)(2,1)S(1)}, u32[]{:S(2)}, u32[]{:S(2)}) collective-permute-start(bf16[1536,128]{1,0:T(8,128)(2,1)S(1)} %collective-permute-done.own_ref), channel_id=1, source_target_pairs={{0,1},{1,0},{2,3},{3,2},{4,5},{5,4},{6,7},{7,6},{8,9},{9,8},{10,11... | collective-permute-start | bytes 1179656 | tf_op jit(solution)/shard_map/ppermute | solution.py:107
  29.8 3.7 %collective-permute-done.12.refs_6_ = bf16[384,128]{1,0:T(8,128)(2,1)S(1)} collective-permute-done((bf16[384,128]{1,0:T(8,128)(2,1)S(1)}, bf16[384,128]{1,0:T(8,128)(2,1)S(1)}, u32[]{:S(2)}, u32[]{:S(2)}) %collective-permute-start.12) | collective-permute-done | bytes 98336 | tf_op jit(solution)/shard_map/ppermute | solution.py:107
  33.5 0.2 collective-permute-start.15
  33.7 0.9 %collective-permute-start.2 = (bf16[1536,128]{1,0:T(8,128)(2,1)S(1)}, bf16[1536,128]{1,0:T(8,128)(2,1)S(1)}, u32[]{:S(2)}, u32[]{:S(2)}) collective-permute-start(bf16[1536,128]{1,0:T(8,128)(2,1)S(1)} %collective-permute-done.1.own_ref), channel_id=1, source_target_pairs={{0,1},{1,0},{2,3},{3,2},{4,5},{5,4},{6,7},{7,6},{8,9},{9,8},{10,11... | collective-permute-start | bytes 1179656 | tf_op jit(solution)/shard_map/ppermute | solution.py:107
  34.5 0.1 collective-permute-start.9
  34.6 2.3 %collective-permute-done.15.got_ref = bf16[384,128]{1,0:T(8,128)(2,1)S(1)} collective-permute-done((bf16[384,128]{1,0:T(8,128)(2,1)S(1)}, bf16[384,128]{1,0:T(8,128)(2,1)S(1)}, u32[]{:S(2)}, u32[]{:S(2)}) %collective-permute-start.15) | collective-permute-done | bytes 98336 | tf_op jit(solution)/shard_map/ppermute | solution.py:107
  36.9 1.9 %collective-permute-start.13 = (bf16[384,128]{1,0:T(8,128)(2,1)S(1)}, bf16[384,128]{1,0:T(8,128)(2,1)S(1)}, u32[]{:S(2)}, u32[]{:S(2)}) collective-permute-start(bf16[384,128]{1,0:T(8,128)(2,1)S(1)} %collective-permute-done.12.refs_6_), channel_id=1, source_target_pairs={{0,1},{1,0},{2,3},{3,2},{4,5},{5,4},{6,7},{7,6},{8,9},{9,8},{10,11... | collective-permute-start | bytes 294920 | tf_op jit(solution)/shard_map/ppermute | solution.py:107
  38.9 0.0 collective-permute-done.9.refs_3_
  38.9 0.4 collective-permute-start.16
  39.3 0.5 collective-permute-done.13.refs_7_
  39.8 2.7 %shard_map.79 = (f32[256,128]{1,0:T(8,128)S(1)}, bf16[256,128]{1,0:T(8,128)(2,1)S(1)}) custom-call(s32[1,5]{1,0:T(1,128)S(1)} %copy-done.5, bf16[528,128]{1,0:T(8,128)(2,1)S(1)} %collective-permute-done.6.got_ref, bf16[384,128]{1,0:T(8,128)(2,1)S(1)} %get-tuple-element.21.sv_ref.refs_0_, bf16[384,128]{1,0:T(8,128)(2,1)S(1)} %collective-permute-done.7.refs_1_, ...), custom_call_target="tpu_custom_call" | custom-call | flops 536870912 | bytes 2000000 | tf_op jit(solution)/shard_map/pallas_call | solution.py:35
  42.5 1.6 %collective-permute-start.14 = (bf16[256,128]{1,0:T(8,128)(2,1)S(1)}, bf16[256,128]{1,0:T(8,128)(2,1)S(1)}, u32[]{:S(2)}, u32[]{:S(2)}) collective-permute-start(bf16[256,128]{1,0:T(8,128)(2,1)S(1)} %get-tuple-element.26), channel_id=1, source_target_pairs={{0,4},{1,5},{2,6},{3,7},{4,0},{5,1},{6,2},{7,3},{8,12},{9,13},{10,... | collective-permute-start | bytes 196616 | tf_op jit(solution)/shard_map/ppermute | solution.py:107
  44.2 2.2 %collective-permute-done.16.got_ref = bf16[384,128]{1,0:T(8,128)(2,1)S(1)} collective-permute-done((bf16[384,128]{1,0:T(8,128)(2,1)S(1)}, bf16[384,128]{1,0:T(8,128)(2,1)S(1)}, u32[]{:S(2)}, u32[]{:S(2)}) %collective-permute-start.16) | collective-permute-done | bytes 98336 | tf_op jit(solution)/shard_map/ppermute | solution.py:107
  46.4 0.7 %shard_map.82 = (f32[384,128]{1,0:T(8,128)}, bf16[384,128]{1,0:T(8,128)(2,1)S(1)}) custom-call(f32[384,128]{1,0:T(8,128)S(1)} %get-tuple-element.30.sum_ref, bf16[384,128]{1,0:T(8,128)(2,1)S(1)} %collective-permute-done.16.got_ref), custom_call_target="tpu_custom_call" | custom-call | bytes 1000000 | tf_op jit(solution)/shard_map/pallas_call | solution.py:35
  47.1 1.2 %collective-permute-start.17 = (bf16[384,128]{1,0:T(8,128)(2,1)S(1)}, bf16[384,128]{1,0:T(8,128)(2,1)S(1)}, u32[]{:S(2)}, u32[]{:S(2)}) collective-permute-start(bf16[384,128]{1,0:T(8,128)(2,1)S(1)} %get-tuple-element.32), channel_id=1, source_target_pairs={{0,16},{16,0},{1,17},{17,1},{2,18},{18,2},{3,19},{19,3},{4,20},{20... | collective-permute-start | bytes 294920 | tf_op jit(solution)/shard_map/ppermute | solution.py:335
  48.3 0.0 collective-permute-done.3.across_ref
  48.3 4.7 %shard_map.74 = (bf16[1024,128]{1,0:T(8,128)(2,1)S(1)}, f32[1024,128]{1,0:T(8,128)S(1)}) custom-call(s32[1,5]{1,0:T(1,128)S(1)} %copy-done.5, bf16[1536,128]{1,0:T(8,128)(2,1)S(1)} %shard_map.73.own_ref, bf16[1536,128]{1,0:T(8,128)(2,1)S(1)} %collective-permute-done.3.across_ref), custom_call_target="tpu_custom_call" | custom-call | flops 1073741824 | bytes 3000000 | tf_op jit(solution)/shard_map/pallas_call | solution.py:35
  53.1 0.0 collective-permute-done.17.refs_0_
  53.1 0.1 collective-permute-start.18
  53.1 0.0 collective-permute-done.4.across_ref
  53.2 2.5 %shard_map.75.refs_1_ = f32[1024,128]{1,0:T(8,128)S(1)} custom-call(s32[1,5]{1,0:T(1,128)S(1)} %copy-done.5, bf16[1536,128]{1,0:T(8,128)(2,1)S(1)} %collective-permute-done.own_ref, bf16[1536,128]{1,0:T(8,128)(2,1)S(1)} %collective-permute-done.4.across_ref, bf16[1024,128]{1,0:T(8,128)(2,1)S(1)} %get-tuple-element.19.refs_0_, ...), custom_call_target="tpu_custom_call" | custom-call | flops 805306368 | bytes 3000000 | tf_op jit(solution)/shard_map/pallas_call | solution.py:35
  55.7 4.6 %shard_map.76.near_ref = f32[1024,128]{1,0:T(8,128)S(1)} custom-call(s32[1,5]{1,0:T(1,128)S(1)} %copy-done.5, bf16[1536,128]{1,0:T(8,128)(2,1)S(1)} %collective-permute-done.1.own_ref, bf16[1536,128]{1,0:T(8,128)(2,1)S(1)} %collective-permute-done.2.across_ref, bf16[1024,128]{1,0:T(8,128)(2,1)S(1)} %get-tuple-element.19.refs_0_, ...), custom_call_target="tpu_custom_call" | custom-call | flops 805306368 | bytes 3000000 | tf_op jit(solution)/shard_map/pallas_call | solution.py:35
  60.3 0.0 collective-permute-done.14.got_ref
  60.3 1.8 %shard_map.83 = bf16[1024,128]{1,0:T(8,128)(2,1)} custom-call(f32[1024,128]{1,0:T(8,128)S(1)} %shard_map.76.near_ref, bf16[1024,256]{1,0:T(8,128)(2,1)S(1)} %copy-done, bf16[384,128]{1,0:T(8,128)(2,1)S(1)} %get-tuple-element.21.sv_ref.refs_0_, f32[256,128]{1,0:T(8,128)S(1)} %get-tuple-element.25.own_ref, ...), custom_call_target="tpu_custom_call" | custom-call | flops 67108864 | bytes 2000000 | tf_op jit(solution)/shard_map/pallas_call | solution.py:35
  (14 shorter events, 0.1 us)
Async XLA Ops:
  0.0 1.1 %copy-start.1 = (bf16[1024,128]{1,0:T(8,128)(2,1)S(1)}, bf16[1024,128]{1,0:T(8,128)(2,1)}, u32[]{:S(2)}) copy-start(bf16[1024,128]{1,0:T(8,128)(2,1)} %weights_ref.3) | copy-start | bytes 786436
  1.1 11.5 %copy-start = (bf16[1024,256]{1,0:T(8,128)(2,1)S(1)}, bf16[1024,256]{1,0:T(8,128)(2,1)}, u32[]{:S(2)}) copy-start(bf16[1024,256]{1,0:T(8,128)(2,1)} %interp_ref.3) | copy-start | bytes 1572868
  1.1 11.5 %copy-start.2 = (bf16[256,512]{1,0:T(8,128)(2,1)S(1)}, bf16[256,512]{1,0:T(8,128)(2,1)}, u32[]{:S(2)}) copy-start(bf16[256,512]{1,0:T(8,128)(2,1)} %ci_ref.1) | copy-start | bytes 786436
  1.2 11.5 %copy-start.3 = (s32[1,512]{1,0:T(1,128)S(1)}, s32[1,512]{1,0:T(1,128)}, u32[]{:S(2)}) copy-start(s32[1,512]{1,0:T(1,128)} %ids_ref.1) | copy-start | bytes 6148
  1.2 11.5 %copy-start.4 = (s32[1,256]{1,0:T(1,128)S(1)}, s32[1,256]{1,0:T(1,128)}, u32[]{:S(2)}) copy-start(s32[1,256]{1,0:T(1,128)} %rows_ref.1) | copy-start | bytes 3076
  1.3 10.0 %collective-permute-start = (bf16[1536,128]{1,0:T(8,128)(2,1)S(1)}, bf16[1536,128]{1,0:T(8,128)(2,1)S(1)}, u32[]{:S(2)}, u32[]{:S(2)}) collective-permute-start(bf16[1536,128]{1,0:T(8,128)(2,1)S(1)} %shard_map.73.own_ref), channel_id=1, source_target_pairs={{0,2},{1,3},{2,0},{3,1},{4,6},{5,7},{6,4},{7,5},{8,10},{9,11},{10,... | collective-permute-start | bytes 1179656 | tf_op jit(solution)/shard_map/ppermute | solution.py:107
  11.3 22.3 %collective-permute-start.1 = (bf16[1536,128]{1,0:T(8,128)(2,1)S(1)}, bf16[1536,128]{1,0:T(8,128)(2,1)S(1)}, u32[]{:S(2)}, u32[]{:S(2)}) collective-permute-start(bf16[1536,128]{1,0:T(8,128)(2,1)S(1)} %collective-permute-done.own_ref), channel_id=1, source_target_pairs={{0,4},{1,5},{4,8},{5,9},{8,12},{9,13},{6,2},{7,3},{10,6},{11,7},{1... | collective-permute-start | bytes 1179656 | tf_op jit(solution)/shard_map/ppermute | solution.py:358
  13.5 6.4 %collective-permute-start.5 = (bf16[384,128]{1,0:T(8,128)(2,1)S(1)}, bf16[384,128]{1,0:T(8,128)(2,1)S(1)}, u32[]{:S(2)}, u32[]{:S(2)}) collective-permute-start(bf16[384,128]{1,0:T(8,128)(2,1)S(1)} %get-tuple-element.23), channel_id=1, source_target_pairs={{0,1},{1,0},{2,3},{3,2},{4,5},{5,4},{6,7},{7,6},{8,9},{9,8},{10,11... | collective-permute-start | bytes 294920 | tf_op jit(solution)/shard_map/ppermute | solution.py:107
  15.1 4.8 %copy-start.5 = (s32[1,5]{1,0:T(1,128)S(1)}, s32[1,5]{1,0:T(1,128)}, u32[]{:S(2)}) copy-start(s32[1,5]{1,0:T(1,128)} %flags_ref.9) | copy-start | bytes 64
  15.1 11.1 %collective-permute-start.10 = (bf16[384,128]{1,0:T(8,128)(2,1)S(1)}, bf16[384,128]{1,0:T(8,128)(2,1)S(1)}, u32[]{:S(2)}, u32[]{:S(2)}) collective-permute-start(bf16[384,128]{1,0:T(8,128)(2,1)S(1)} %get-tuple-element.21.sv_ref.refs_0_), channel_id=1, source_target_pairs={{0,8},{1,9},{2,10},{3,11},{4,12},{5,13},{6,14},{7,15},{8,0},{9,1},... | collective-permute-start | bytes 294920 | tf_op jit(solution)/shard_map/ppermute | solution.py:107
  18.5 10.6 %collective-permute-start.8 = (bf16[384,128]{1,0:T(8,128)(2,1)S(1)}, bf16[384,128]{1,0:T(8,128)(2,1)S(1)}, u32[]{:S(2)}, u32[]{:S(2)}) collective-permute-start(bf16[384,128]{1,0:T(8,128)(2,1)S(1)} %get-tuple-element.21.sv_ref.refs_0_), channel_id=1, source_target_pairs={{0,2},{1,3},{2,0},{3,1},{4,6},{5,7},{6,4},{7,5},{8,10},{9,11},{10,... | collective-permute-start | bytes 294920 | tf_op jit(solution)/shard_map/ppermute | solution.py:107
  20.4 8.7 %collective-permute-start.6 = (bf16[528,128]{1,0:T(8,128)(2,1)S(1)}, bf16[528,128]{1,0:T(8,128)(2,1)S(1)}, u32[]{:S(2)}, u32[]{:S(2)}) collective-permute-start(bf16[528,128]{1,0:T(8,128)(2,1)S(1)} %get-tuple-element.24), channel_id=1, source_target_pairs={{0,4},{1,5},{2,6},{3,7},{4,0},{5,1},{6,2},{7,3},{8,12},{9,13},{10,... | collective-permute-start | bytes 405512 | tf_op jit(solution)/shard_map/ppermute | solution.py:107
  20.5 8.6 %collective-permute-start.7 = (bf16[384,128]{1,0:T(8,128)(2,1)S(1)}, bf16[384,128]{1,0:T(8,128)(2,1)S(1)}, u32[]{:S(2)}, u32[]{:S(2)}) collective-permute-start(bf16[384,128]{1,0:T(8,128)(2,1)S(1)} %get-tuple-element.21.sv_ref.refs_0_), channel_id=1, source_target_pairs={{0,1},{1,0},{2,3},{3,2},{4,5},{5,4},{6,7},{7,6},{8,9},{9,8},{10,11... | collective-permute-start | bytes 294920 | tf_op jit(solution)/shard_map/ppermute | solution.py:107
  26.2 22.2 %collective-permute-start.3 = (bf16[1536,128]{1,0:T(8,128)(2,1)S(1)}, bf16[1536,128]{1,0:T(8,128)(2,1)S(1)}, u32[]{:S(2)}, u32[]{:S(2)}) collective-permute-start(bf16[1536,128]{1,0:T(8,128)(2,1)S(1)} %shard_map.73.own_ref), channel_id=1, source_target_pairs={{0,1},{1,0},{2,3},{3,2},{4,5},{5,4},{6,7},{7,6},{8,9},{9,8},{10,11... | collective-permute-start | bytes 1179656 | tf_op jit(solution)/shard_map/ppermute | solution.py:107
  29.0 4.4 %collective-permute-start.12 = (bf16[384,128]{1,0:T(8,128)(2,1)S(1)}, bf16[384,128]{1,0:T(8,128)(2,1)S(1)}, u32[]{:S(2)}, u32[]{:S(2)}) collective-permute-start(bf16[384,128]{1,0:T(8,128)(2,1)S(1)} %collective-permute-done.10.refs_4_), channel_id=1, source_target_pairs={{0,2},{1,3},{2,0},{3,1},{4,6},{5,7},{6,4},{7,5},{8,10},{9,11},{10,... | collective-permute-start | bytes 294920 | tf_op jit(solution)/shard_map/ppermute | solution.py:107
  29.0 5.5 %collective-permute-start.11 = (bf16[384,128]{1,0:T(8,128)(2,1)S(1)}, bf16[384,128]{1,0:T(8,128)(2,1)S(1)}, u32[]{:S(2)}, u32[]{:S(2)}) collective-permute-start(bf16[384,128]{1,0:T(8,128)(2,1)S(1)} %collective-permute-done.10.refs_4_), channel_id=1, source_target_pairs={{0,1},{1,0},{2,3},{3,2},{4,5},{5,4},{6,7},{7,6},{8,9},{9,8},{10,11... | collective-permute-start | bytes 294920 | tf_op jit(solution)/shard_map/ppermute | solution.py:107
  29.1 24.0 %collective-permute-start.4 = (bf16[1536,128]{1,0:T(8,128)(2,1)S(1)}, bf16[1536,128]{1,0:T(8,128)(2,1)S(1)}, u32[]{:S(2)}, u32[]{:S(2)}) collective-permute-start(bf16[1536,128]{1,0:T(8,128)(2,1)S(1)} %collective-permute-done.own_ref), channel_id=1, source_target_pairs={{0,1},{1,0},{2,3},{3,2},{4,5},{5,4},{6,7},{7,6},{8,9},{9,8},{10,11... | collective-permute-start | bytes 1179656 | tf_op jit(solution)/shard_map/ppermute | solution.py:107
  33.5 3.5 %collective-permute-start.15 = (bf16[384,128]{1,0:T(8,128)(2,1)S(1)}, bf16[384,128]{1,0:T(8,128)(2,1)S(1)}, u32[]{:S(2)}, u32[]{:S(2)}) collective-permute-start(bf16[384,128]{1,0:T(8,128)(2,1)S(1)} %get-tuple-element.29), channel_id=1, source_target_pairs={{0,2},{1,3},{2,0},{3,1},{4,6},{5,7},{6,4},{7,5},{8,10},{9,11},{10,... | collective-permute-start | bytes 294920 | tf_op jit(solution)/shard_map/ppermute | solution.py:107
  33.7 22.0 %collective-permute-start.2 = (bf16[1536,128]{1,0:T(8,128)(2,1)S(1)}, bf16[1536,128]{1,0:T(8,128)(2,1)S(1)}, u32[]{:S(2)}, u32[]{:S(2)}) collective-permute-start(bf16[1536,128]{1,0:T(8,128)(2,1)S(1)} %collective-permute-done.1.own_ref), channel_id=1, source_target_pairs={{0,1},{1,0},{2,3},{3,2},{4,5},{5,4},{6,7},{7,6},{8,9},{9,8},{10,11... | collective-permute-start | bytes 1179656 | tf_op jit(solution)/shard_map/ppermute | solution.py:107
  34.5 4.4 %collective-permute-start.9 = (bf16[384,128]{1,0:T(8,128)(2,1)S(1)}, bf16[384,128]{1,0:T(8,128)(2,1)S(1)}, u32[]{:S(2)}, u32[]{:S(2)}) collective-permute-start(bf16[384,128]{1,0:T(8,128)(2,1)S(1)} %collective-permute-done.8.refs_2_), channel_id=1, source_target_pairs={{0,1},{1,0},{2,3},{3,2},{4,5},{5,4},{6,7},{7,6},{8,9},{9,8},{10,11... | collective-permute-start | bytes 294920 | tf_op jit(solution)/shard_map/ppermute | solution.py:107
  36.9 2.9 %collective-permute-start.13 = (bf16[384,128]{1,0:T(8,128)(2,1)S(1)}, bf16[384,128]{1,0:T(8,128)(2,1)S(1)}, u32[]{:S(2)}, u32[]{:S(2)}) collective-permute-start(bf16[384,128]{1,0:T(8,128)(2,1)S(1)} %collective-permute-done.12.refs_6_), channel_id=1, source_target_pairs={{0,1},{1,0},{2,3},{3,2},{4,5},{5,4},{6,7},{7,6},{8,9},{9,8},{10,11... | collective-permute-start | bytes 294920 | tf_op jit(solution)/shard_map/ppermute | solution.py:107
  38.9 7.5 %collective-permute-start.16 = (bf16[384,128]{1,0:T(8,128)(2,1)S(1)}, bf16[384,128]{1,0:T(8,128)(2,1)S(1)}, u32[]{:S(2)}, u32[]{:S(2)}) collective-permute-start(bf16[384,128]{1,0:T(8,128)(2,1)S(1)} %get-tuple-element.31), channel_id=1, source_target_pairs={{0,8},{1,9},{2,10},{3,11},{4,12},{5,13},{6,14},{7,15},{8,0},{9,1},... | collective-permute-start | bytes 294920 | tf_op jit(solution)/shard_map/ppermute | solution.py:107
  42.5 17.7 %collective-permute-start.14 = (bf16[256,128]{1,0:T(8,128)(2,1)S(1)}, bf16[256,128]{1,0:T(8,128)(2,1)S(1)}, u32[]{:S(2)}, u32[]{:S(2)}) collective-permute-start(bf16[256,128]{1,0:T(8,128)(2,1)S(1)} %get-tuple-element.26), channel_id=1, source_target_pairs={{0,4},{1,5},{2,6},{3,7},{4,0},{5,1},{6,2},{7,3},{8,12},{9,13},{10,... | collective-permute-start | bytes 196616 | tf_op jit(solution)/shard_map/ppermute | solution.py:107
  47.1 6.0 %collective-permute-start.17 = (bf16[384,128]{1,0:T(8,128)(2,1)S(1)}, bf16[384,128]{1,0:T(8,128)(2,1)S(1)}, u32[]{:S(2)}, u32[]{:S(2)}) collective-permute-start(bf16[384,128]{1,0:T(8,128)(2,1)S(1)} %get-tuple-element.32), channel_id=1, source_target_pairs={{0,16},{16,0},{1,17},{17,1},{2,18},{18,2},{3,19},{19,3},{4,20},{20... | collective-permute-start | bytes 294920 | tf_op jit(solution)/shard_map/ppermute | solution.py:335
  53.1 7.2 %collective-permute-start.18 = (bf16[384,128]{1,0:T(8,128)(2,1)S(1)}, bf16[384,128]{1,0:T(8,128)(2,1)S(1)}, u32[]{:S(2)}, u32[]{:S(2)}) collective-permute-start(bf16[384,128]{1,0:T(8,128)(2,1)S(1)} %collective-permute-done.17.refs_0_), channel_id=1, source_target_pairs={{0,1},{1,0},{2,3},{3,2},{4,5},{5,4},{6,7},{7,6},{8,9},{9,8},{10,11... | collective-permute-start | bytes 294920 | tf_op jit(solution)/shard_map/ppermute | solution.py:107

commit v2 on v1

--- a/solution.py
+++ b/solution.py
@@ -19,28 +19,29 @@
     return pl.BlockSpec(memory_space=pltpu.VMEM)
 
 
-def smem():
-    return pl.BlockSpec(memory_space=pltpu.SMEM)
-
-
-def call(body, outs, ins, scratch=(), flops=0, moved=0):
-    specs, args = [], []
-    for item in ins:
-        if isinstance(item, tuple):
-            specs.append(smem())
-            args.append(item[0])
-        else:
-            specs.append(vmem())
-            args.append(item)
+def call(body, outs, ins, scratch=(), after=(), flops=0, moved=0):
+    waits = len(after)
     return pl.pallas_call(
-        body,
+        lambda *refs: body(*refs[waits:]),
         out_shape=[jax.ShapeDtypeStruct(shape, dtype) for shape, dtype in outs],
-        in_specs=specs,
+        in_specs=[pl.BlockSpec(memory_space=pl.ANY) for _ in after] + [vmem() for _ in ins],
         out_specs=[vmem() for _ in outs],
         scratch_shapes=[pltpu.VMEM(shape, dtype) for shape, dtype in scratch],
         compiler_params=pltpu.CompilerParams(vmem_limit_bytes=VMEM_BYTES),
         cost_estimate=pl.CostEstimate(flops=flops, bytes_accessed=moved, transcendentals=0),
-    )(*args)
+    )(*after, *ins)
+
+
+def hand_on(value, *after):
+    anywhere = pl.BlockSpec(memory_space=pl.ANY)
+    return pl.pallas_call(
+        lambda *refs: None,
+        out_shape=jax.ShapeDtypeStruct(value.shape, value.dtype),
+        in_specs=[anywhere] * (1 + len(after)),
+        out_specs=anywhere,
+        input_output_aliases={0: 0},
+        cost_estimate=pl.CostEstimate(flops=0, bytes_accessed=0, transcendentals=0),
+    )(value, *after)
 
 
 def dot_nt(a, b):
@@ -108,23 +109,37 @@
 
 
 def pack_kernel(points_ref, weights_ref, halo_ref):
-    half = points_ref.shape[0] // 2
-    halo_ref[:half, :] = pack_halves(points_ref[...].astype(F32)).astype(BF16)
+    features, rows = points_ref.shape
+    half = rows // 2
+    spread = (features, 2 * features)
+    row = lax.broadcasted_iota(jnp.int32, spread, 0)
+    lane = lax.broadcasted_iota(jnp.int32, spread, 1)
+    left = (row == lane).astype(F32).astype(BF16)
+    right = (row + features == lane).astype(F32).astype(BF16)
+    packed = dot_tn(points_ref[:, :half], left) + dot_tn(points_ref[:, half:], right)
+    halo_ref[:half, :] = packed.astype(BF16)
     halo_ref[half:, :] = weights_ref[...]
+
+
+def flag_of(flags_ref, distance):
+    columns = flags_ref.shape[1]
+    lane = lax.broadcasted_iota(jnp.int32, (1, columns), 1)
+    here = lane == distance + (columns - 1) // 2
+    return jnp.sum(jnp.where(here, flags_ref[...], 0).astype(F32), axis=1, keepdims=True)
 
 
 def skeleton_kernel(
     points_ref, weights_ref, interp_ref, ci_ref, rows_ref, ids_ref, sv_ref, sum_ref, send_ref, u_ref, c_ref
 ):
     leaf = lax.axis_index("leaf")
-    points, skeleton_count = points_ref.shape[0], interp_ref.shape[1]
+    points, skeleton_count = points_ref.shape[1], interp_ref.shape[1]
     cluster_count, picked = ids_ref.shape
     members = lax.axis_size("leaf") // cluster_count
     core = leaf % 2
     one = (
         lax.broadcasted_iota(jnp.int32, (points, skeleton_count), 0) == rows_ref[...]
     ).astype(F32).astype(BF16)
-    skeleton = dot_tn(one, points_ref[...])
+    skeleton = lax.dot_general(one, points_ref[...], (((0,), (1,)), ((), ())), preferred_element_type=F32)
     charges = dot_tn(interp_ref[...], weights_ref[...]).astype(BF16)
     half = skeleton_count // 2
     sv_ref[:half, :] = pack_halves(skeleton).astype(BF16)
@@ -151,11 +166,11 @@
     new_ref[...] = total
     send_ref[:rows, :] = total.astype(BF16)
     send_ref[rows : rows + half, :] = sv_ref[:half, :]
-    lane = lax.broadcasted_iota(jnp.int32, (16, send_ref.shape[1]), 1)
-    row = jnp.zeros(lane.shape, F32)
-    for column in range(flags_ref.shape[1]):
-        row = jnp.where(lane == column, flags_ref[0, column].astype(F32), row)
-    send_ref[rows + half :, :] = row.astype(BF16)
+    columns = flags_ref.shape[1]
+    row = lax.broadcasted_iota(jnp.int32, (columns, send_ref.shape[1]), 0)
+    lane = lax.broadcasted_iota(jnp.int32, (columns, send_ref.shape[1]), 1)
+    spread = dot_nn(flags_ref[...].astype(F32), (row == lane).astype(F32))
+    send_ref[rows + half :, :] = jnp.broadcast_to(spread, (16, send_ref.shape[1])).astype(BF16)
 
 
 def add_kernel(sum_ref, got_ref, new_ref, send_ref):
@@ -165,14 +180,14 @@
     send_ref[...] = total.astype(BF16)
 
 
-def near_tile(targets_ref, halo_ref, source_ref, near_ref, features):
+def near_tile(targets_ref, halo_ref, source_ref, near_ref, flag, features):
     half = source_ref.shape[0] // 2
     low, high = extended_halves(halo_ref[:half, :], features, False)
     source_ref[:half, :] = low
     source_ref[half:, :] = high
     for start in range(0, targets_ref.shape[0], TARGET_ROWS):
         rows = slice(start, start + TARGET_ROWS)
-        near_ref[rows, :] += product(
+        near_ref[rows, :] += flag * product(
             targets_ref[rows, :], source_ref, halo_ref, 0, 2 * half, features, half
         )
 
@@ -180,7 +195,6 @@
 def near_kernel(stage, features, flags_ref, own_ref, across_ref, *refs):
     leaf = lax.axis_index("leaf")
     core, chip = leaf % 2, (leaf // 2) % 2
-    reach = (flags_ref.shape[1] - 1) // 2
     side, beside = 1 - 2 * core, 1 - 2 * chip
     if stage == 0:
         targets_ref, near_ref, source_ref = refs
@@ -189,47 +203,52 @@
         targets_ref[:half, :] = low
         targets_ref[half:, :] = high
         near_ref[...] = jnp.zeros_like(near_ref)
-        distances, here = (0, side), core == core
+        distances = (0, side)
     else:
         targets_ref, before_ref, near_ref, source_ref = refs
         near_ref[...] = before_ref[...]
         distances = (2 * beside if stage == 1 else -2 * beside, -side)
-        here = core != chip if stage == 1 else core == chip
-
-    @pl.when(flags_ref[0, reach + distances[0]] != 0)
-    def _():
-        near_tile(targets_ref, own_ref, source_ref, near_ref, features)
-
-    @pl.when((flags_ref[0, reach + distances[1]] != 0) & here)
-    def _():
-        near_tile(targets_ref, across_ref, source_ref, near_ref, features)
-
-
-def sibling_kernel(masks, reduced, features, flags_ref, got_ref, *refs):
+    near_tile(targets_ref, own_ref, source_ref, near_ref, flag_of(flags_ref, distances[0]), features)
+
+    def second():
+        flag = flag_of(flags_ref, distances[1])
+        near_tile(targets_ref, across_ref, source_ref, near_ref, flag, features)
+
+    if stage == 0:
+        second()
+    else:
+        pl.when(core != chip if stage == 1 else core == chip)(second)
+
+
+def join_kernel(first_ref, second_ref, both_ref):
+    rows = first_ref.shape[0]
+    both_ref[:rows, :] = first_ref[...]
+    both_ref[rows:, :] = second_ref[...]
+
+
+def sibling_kernel(masks, reduced, features, skeletons, flags_ref, got_ref, *refs):
     pieces, refs = refs[: len(masks)], refs[len(masks) :]
     own_ref, send_ref, low_ref, high_ref, mine_ref, other_ref, targets_ref = refs
     leaf = lax.axis_index("leaf")
-    columns = flags_ref.shape[1]
-    reach = (columns - 1) // 2
-    half = pieces[0].shape[0] // 3
+    reach = (flags_ref.shape[1] - 1) // 2
+    half = skeletons // 2
     got_rows = got_ref.shape[0]
     other_points = got_ref[got_rows - 16 - half : got_rows - 16, :]
     other_flags = got_ref[got_rows - 16 :, :].astype(F32)[:1, :]
     lane = lax.broadcasted_iota(jnp.int32, other_flags.shape, 1)
-    total = len(masks) * half
-    for position, (mask, piece) in enumerate(zip(masks, pieces)):
+    flat = [(m, piece, 3 * half * i) for part, piece in zip(masks, pieces) for i, m in enumerate(part)]
+    total = len(flat) * half
+    for position, (mask, piece, start) in enumerate(flat):
         source = leaf ^ mask
         rows = slice(position * half, (position + 1) * half)
         later = slice(total + position * half, total + (position + 1) * half)
-        low, high = extended_halves(piece[:half, :], features, False)
+        low, high = extended_halves(piece[start : start + half, :], features, False)
         low_ref[rows, :] = low
         high_ref[rows, :] = high
-        mine = source - leaf + reach
-        listed = flags_ref[0, jnp.clip(mine, 0, columns - 1)]
-        kept = jnp.where((mine >= 0) & (mine < columns), 1 - listed, 1).astype(F32)
+        kept = 1.0 - flag_of(flags_ref, source - leaf)
         flagged = jnp.where(lane == source - (leaf ^ reduced) + reach, other_flags, 0.0)
         kept_other = 1.0 - jnp.sum(flagged, axis=1, keepdims=True)
-        mass = piece[half:, :].astype(F32)
+        mass = piece[start + half : start + 3 * half, :].astype(F32)
         for ref, factor in ((mine_ref, kept), (other_ref, kept_other)):
             scaled = (mass * factor).astype(BF16)
             ref[rows, :] = scaled[:half]
@@ -276,56 +295,100 @@
     core_mask, chip_mask, reduced = 1, 2, 4
     half, sk_half, part = leaf_points // 2, skeletons // 2, picked // 2
     sum_rows = part + part // 2
-    flags = (near_flags,)
+    flags, turned = near_flags, points.T
     tile_flops = 2 * leaf_points * leaf_points * (2 * features + columns)
 
-    (halo,) = call(pack_kernel, [((half + leaf_points, columns), BF16)], [points, weights], moved=10**6)
+    (halo,) = call(pack_kernel, [((half + leaf_points, columns), BF16)], [turned, weights], moved=10**6)
     halo_beside = xor_exchange(halo, "leaf", chip_mask)
     halo_core = xor_exchange(halo, "leaf", core_mask)
 
     skeleton, cluster_sum, cluster_send = call(
         skeleton_kernel,
         [((sk_half * 3, columns), BF16), ((sum_rows, columns), F32), ((sum_rows, columns), BF16)],
-        [points, weights, interp, cluster_interp, skeleton_rows, cluster_rows],
+        [turned, weights, interp, cluster_interp, skeleton_rows, cluster_rows],
         scratch=[((picked, columns), F32), ((part, columns), F32)],
+        after=[halo],
         flops=4 * leaf_points * skeletons * columns,
         moved=2 * 10**6,
     )
 
-    pieces = {0: skeleton}
-    mask = leaves // 2
-    while mask >= 1:
-        if mask != reduced:
-            for known in sorted(pieces):
-                pieces[known | mask] = xor_exchange(pieces[known], "leaf", mask)
-        mask //= 2
-
+    sum_outs = [((sum_rows, columns), F32), ((sum_rows, columns), BF16)]
     got = xor_exchange(cluster_send, "leaf", core_mask)
+    gathered, masks = skeleton, [0]
+    gather_masks = [1 << i for i in reversed(range(1, leaves.bit_length() - 1)) if 1 << i != reduced]
+    last_mask = gather_masks.pop()
+    first_got = xor_exchange(gathered, "leaf", gather_masks[0]) if gather_masks else None
     cluster_sum, cluster_send = call(
         first_add_kernel,
-        [((sum_rows, columns), F32), ((sum_rows + sk_half + 16, columns), BF16)],
+        [sum_outs[0], ((sum_rows + sk_half + 16, columns), BF16)],
         [flags, cluster_sum, got, skeleton],
         moved=10**6,
     )
     partner = got = xor_exchange(cluster_send, "leaf", reduced)
-    mask = chip_mask
-    while mask < members:
-        if mask != reduced:
-            cluster_sum, cluster_send = call(
-                add_kernel,
-                [((sum_rows, columns), F32), ((sum_rows, columns), BF16)],
-                [cluster_sum, got],
-                moved=10**6,
-            )
-            got = xor_exchange(cluster_send, "leaf", mask)
-        mask *= 2
-    cluster_sum, cluster_send = call(
-        add_kernel,
-        [((sum_rows, columns), F32), ((sum_rows, columns), BF16)],
-        [cluster_sum, got],
-        moved=10**6,
-    )
+
+    near_outs = ((leaf_points, columns), F32)
+    tile_scratch = [((leaf_points, columns), BF16)]
+    targets, near = call(
+        functools.partial(near_kernel, 0, features),
+        [((leaf_points, columns), BF16), near_outs],
+        [flags, halo, halo_core],
+        scratch=tile_scratch,
+        after=[cluster_send],
+        flops=2 * tile_flops,
+        moved=3 * 10**6,
+    )
+    near_step = functools.partial(
+        call, outs=[near_outs], scratch=tile_scratch, flops=3 * tile_flops // 2, moved=3 * 10**6
+    )
+
+    add_masks = [1 << i for i in range(1, members.bit_length() - 1) if 1 << i != reduced]
+    cluster_sum, cluster_send = call(add_kernel, sum_outs, [cluster_sum, got], after=[near], moved=10**6)
+    got = xor_exchange(cluster_send, "leaf", add_masks[0])
+
+    halo_beside = hand_on(halo_beside, cluster_send)
+    ahead = [(i, i + 4) for i in range(leaves - 4) if i & chip_mask == 0]
+    behind = [(i, i - 4) for i in range(4, leaves) if i & chip_mask != 0]
+    halo_far = lax.ppermute(halo_beside, "leaf", ahead + behind)
+    halo_across = xor_exchange(halo_beside, "leaf", core_mask)
+
+    for mask in gather_masks:
+        arrived = first_got if mask == gather_masks[0] else xor_exchange(gathered, "leaf", mask)
+        masks = masks + [m | mask for m in masks]
+        (gathered,) = call(
+            join_kernel, [((2 * gathered.shape[0], columns), BF16)], [gathered, arrived], moved=10**6
+        )
+    pieces = [(masks, gathered), ([m | last_mask for m in masks], xor_exchange(gathered, "leaf", last_mask))]
+    pieces += [([m | core_mask for m in part], xor_exchange(piece, "leaf", core_mask)) for part, piece in pieces]
+
+    for mask in add_masks[1:]:
+        cluster_sum, cluster_send = call(
+            add_kernel, sum_outs, [cluster_sum, got], after=[gathered], moved=10**6
+        )
+        got = xor_exchange(cluster_send, "leaf", mask)
+
+    (near,) = near_step(
+        functools.partial(near_kernel, 1, features),
+        ins=[flags, halo_beside, halo_across, targets, near],
+        after=[cluster_send],
+    )
+
+    sources = 2 * len(pieces[0][0]) * 2 * sk_half
+    field, field_send = call(
+        functools.partial(sibling_kernel, [p for p, _ in pieces], reduced, features, skeletons),
+        [((skeletons, columns), F32), ((skeletons, columns), BF16)],
+        [flags, partner] + [piece for _, piece in pieces],
+        scratch=[((sources, columns), BF16)] * 2
+        + [((2 * sources, columns), BF16)] * 2
+        + [((2 * skeletons, columns), BF16)],
+        after=[near],
+        flops=4 * skeletons * 2 * sources * (2 * features + columns),
+        moved=2 * 10**6,
+    )
+    field_got = xor_exchange(field_send, "leaf", reduced)
+
+    cluster_sum, cluster_send = call(add_kernel, sum_outs, [cluster_sum, got], after=[field], moved=10**6)
     own_group = [cluster_send]
+    mask = members
     while mask < leaves:
         own_group += [xor_exchange(pack, "leaf", mask) for pack in own_group]
         mask *= 2
@@ -335,46 +398,12 @@
         packs += [lax.ppermute(pack, "group", pairs) for pack in own_group]
     packs += [xor_exchange(pack, "leaf", core_mask) for pack in packs]
 
-    near_outs = ((leaf_points, columns), F32)
-    tile_scratch = [((leaf_points, columns), BF16)]
-    targets, near = call(
-        functools.partial(near_kernel, 0, features),
-        [((leaf_points, columns), BF16), near_outs],
-        [flags, halo, halo_core],
-        scratch=tile_scratch,
-        flops=2 * tile_flops,
-        moved=3 * 10**6,
-    )
-    near_step = functools.partial(
-        call, outs=[near_outs], scratch=tile_scratch, flops=3 * tile_flops // 2, moved=3 * 10**6
-    )
-    halo_across = xor_exchange(halo_beside, "leaf", core_mask)
-    (near,) = near_step(
-        functools.partial(near_kernel, 1, features),
-        ins=[flags, halo_beside, halo_across, targets, near],
-    )
-    ahead = [(i, i + 4) for i in range(leaves - 4) if i & chip_mask == 0]
-    behind = [(i, i - 4) for i in range(4, leaves) if i & chip_mask != 0]
-    halo_far = lax.ppermute(halo_beside, "leaf", ahead + behind)
     halo_far_across = xor_exchange(halo_far, "leaf", core_mask)
     (near,) = near_step(
         functools.partial(near_kernel, 2, features),
         ins=[flags, halo_far, halo_far_across, targets, near],
-    )
-
-    masks = sorted(pieces)
-    sources = len(masks) * sk_half
-    field, field_send = call(
-        functools.partial(sibling_kernel, masks, reduced, features),
-        [((skeletons, columns), F32), ((skeletons, columns), BF16)],
-        [flags, partner] + [pieces[m] for m in masks],
-        scratch=[((sources, columns), BF16)] * 2
-        + [((2 * sources, columns), BF16)] * 2
-        + [((2 * skeletons, columns), BF16)],
-        flops=4 * skeletons * 2 * sources * (2 * features + columns),
-        moved=2 * 10**6,
-    )
-    field_got = xor_exchange(field_send, "leaf", reduced)
+        after=[cluster_send],
+    )
 
     sources = len(packs) * (part // 2)
     (potential,) = call(

time: 62.8 us -> 64.6 us (1.029)
  the two profiles are of different devices: /device:TPU:5 before, /device:TPU:0 now
where the time goes in v2:
time: 64.6 us; the launch traced here: 64.4 us
  waiting for transfers between devices  22.4 us (35%)
  starting transfers between devices  21.7 us (34%)
  Pallas kernels  15.4 us (24%)
  local copies, waits for them, and re-layouts  4.64 us (7%)
    ppermute x14, waiting for transfers between devices, xor_exchange(): lax.ppermute(value, axis, [(i, i ^ mask) for i in range(lax.axis_size(axi...  19.2 us
    ppermute x14, starting transfers between devices, xor_exchange(): lax.ppermute(value, axis, [(i, i ^ mask) for i in range(lax.axis_size(axi...  16.6 us
    pallas_call x12, Pallas kernels, call(): pl.pallas_call(lambda *refs: body(*refs[waits:]), out_shape=[jax.ShapeDty...  15.4 us
    unnamed x22, local copies, waits for them, and re-layouts  4.64 us
    ppermute x1, starting transfers between devices, on_device(): halo_far = lax.ppermute(halo_beside, 'leaf', ahead + behind)  3.62 us
    ppermute x1, waiting for transfers between devices, on_device(): packs += [lax.ppermute(pack, 'group', pairs) for pack in own_group]  3.22 us
    ppermute x1, starting transfers between devices, on_device(): packs += [lax.ppermute(pack, 'group', pairs) for pack in own_group]  1.49 us
  transfers between devices with their start and end apart: 16, of which 7 were waited for; matrix products, arithmetic and copies ran while one was open for 0% of the time, Pallas kernels for 21%

profile of v2, /device:TPU:0, one launch (start us, length us, event | category | flops | bytes accessed | tf_op | source)
XLA Modules:
  0.0 64.4 jit_solution(2093884868211669936)
XLA Ops:
  0.0 1.0 %copy-done.1 = bf16[1024,128]{1,0:T(8,128)(2,1)S(1)} copy-done((bf16[1024,128]{1,0:T(8,128)(2,1)S(1)}, bf16[1024,128]{1,0:T(8,128)(2,1)}, u32[]{:S(2)}) %copy-start.1) | copy-done | bytes 262168
  1.0 0.9 %copy-done.2 = bf16[1024,64]{0,1:T(8,128)(2,1)S(1)} copy-done((bf16[1024,64]{0,1:T(8,128)(2,1)S(1)}, bf16[1024,64]{0,1:T(8,128)(2,1)}, u32[]{:S(2)}) %copy-start.2) | copy-done | bytes 131096
  1.9 0.3 shard_map.73.refs_0_.refs_2_
  2.2 0.5 collective-permute-start.2
  2.7 2.6 %collective-permute-start.5 = (bf16[1536,128]{1,0:T(8,128)(2,1)S(1)}, bf16[1536,128]{1,0:T(8,128)(2,1)S(1)}, u32[]{:S(2)}, u32[]{:S(2)}) collective-permute-start(bf16[1536,128]{1,0:T(8,128)(2,1)S(1)} %shard_map.73.refs_0_.refs_2_), channel_id=1, source_target_pairs={{0,2},{1,3},{2,0},{3,1},{4,6},{5,7},{6,4},{7,5},{8,10},{9,11},{10,... | collective-permute-start | bytes 1179656 | tf_op jit(solution)/shard_map/ppermute | solution.py:108
  5.3 0.7 %copy-done.8 = s32[1,512]{1,0:T(1,128)S(1)} copy-done((s32[1,512]{1,0:T(1,128)S(1)}, s32[1,512]{1,0:T(1,128)}, u32[]{:S(2)}) %copy-start.8) | copy-done | bytes 2072
  6.0 0.8 %shard_map.74 = (bf16[384,128]{1,0:T(8,128)(2,1)S(1)}, f32[384,128]{1,0:T(8,128)S(1)}, bf16[384,128]{1,0:T(8,128)(2,1)S(1)}) custom-call(bf16[1536,128]{1,0:T(8,128)(2,1)S(1)} %shard_map.73.refs_0_.refs_2_, bf16[64,1024]{1,0:T(8,128)(2,1)S(1)} %bitcast.2, bf16[1024,128]{1,0:T(8,128)(2,1)S(1)} %copy-done.1, bf16[1024,256]{1,0:T(8,128)(2,1)S(1)} %copy-done, ...), custom_call_target="tpu_custom_call" | custom-call | flops 134217728 | bytes 2000000 | tf_op jit(solution)/shard_map/pallas_call | solution.py:24
  6.8 0.2 collective-permute-start.1
  7.1 1.1 %collective-permute-done.1.refs_2_ = bf16[384,128]{1,0:T(8,128)(2,1)S(1)} collective-permute-done((bf16[384,128]{1,0:T(8,128)(2,1)S(1)}, bf16[384,128]{1,0:T(8,128)(2,1)S(1)}, u32[]{:S(2)}, u32[]{:S(2)}) %collective-permute-start.1) | collective-permute-done | bytes 98336 | tf_op jit(solution)/shard_map/ppermute | solution.py:108
  8.2 0.7 %copy-done.10 = s32[1,5]{1,0:T(1,128)S(1)} copy-done((s32[1,5]{1,0:T(1,128)S(1)}, s32[1,5]{1,0:T(1,128)}, u32[]{:S(2)}) %copy-start.10) | copy-done | bytes 44
  8.9 0.1 shard_map.76
  9.0 1.6 %collective-permute-start.3 = (bf16[528,128]{1,0:T(8,128)(2,1)S(1)}, bf16[528,128]{1,0:T(8,128)(2,1)S(1)}, u32[]{:S(2)}, u32[]{:S(2)}) collective-permute-start(bf16[528,128]{1,0:T(8,128)(2,1)S(1)} %get-tuple-element.22.refs_0_), channel_id=1, source_target_pairs={{0,4},{1,5},{2,6},{3,7},{4,0},{5,1},{6,2},{7,3},{8,12},{9,13},{10,... | collective-permute-start | bytes 405512 | tf_op jit(solution)/shard_map/ppermute | solution.py:108
  10.6 0.0 collective-permute-done.2.refs_3_
  10.6 3.6 %shard_map.77 = (bf16[1024,128]{1,0:T(8,128)(2,1)S(1)}, f32[1024,128]{1,0:T(8,128)S(1)}) custom-call(bf16[528,128]{1,0:T(8,128)(2,1)S(1)} %get-tuple-element.22.refs_0_, s32[1,5]{1,0:T(1,128)S(1)} %copy-done.10, bf16[1536,128]{1,0:T(8,128)(2,1)S(1)} %shard_map.73.refs_0_.refs_2_, bf16[1536,128]{1,0:T(8,128)(2,1)S(1)} %collective-permute-done.2.refs_3_), custom_call_target="tpu_custom_call" | custom-call | flops 1073741824 | bytes 3000000 | tf_op jit(solution)/shard_map/pallas_call | solution.py:24
  14.2 0.4 collective-permute-done.3.refs_2_
  14.7 0.0 copy-start.6
  14.7 0.6 copy-done.6
  15.3 0.0 collective-permute-done.5.refs_0_
  15.3 0.7 %copy-done.3 = bf16[1536,128]{1,0:T(8,128)(2,1)} copy-done((bf16[1536,128]{1,0:T(8,128)(2,1)}, bf16[1536,128]{1,0:T(8,128)(2,1)S(1)}, u32[]{:S(2)}) %copy-start.3) | copy-done | bytes 393240
  16.1 3.6 %collective-permute-start.11 = (bf16[1536,128]{1,0:T(8,128)(2,1)}, bf16[1536,128]{1,0:T(8,128)(2,1)S(1)}, u32[]{:S(2)}, u32[]{:S(2)}) collective-permute-start(bf16[1536,128]{1,0:T(8,128)(2,1)} %shard_map.80.refs_2_), channel_id=1, source_target_pairs={{0,4},{1,5},{4,8},{5,9},{8,12},{9,13},{6,2},{7,3},{10,6},{11,7},{1... | collective-permute-start | bytes 1179656 | tf_op jit(solution)/shard_map/ppermute | solution.py:351
  19.7 2.6 %collective-permute-start = (bf16[384,128]{1,0:T(8,128)(2,1)S(1)}, bf16[384,128]{1,0:T(8,128)(2,1)S(1)}, u32[]{:S(2)}, u32[]{:S(2)}) collective-permute-start(bf16[384,128]{1,0:T(8,128)(2,1)S(1)} %get-tuple-element.19.refs_0_.refs_3_.refs_2_), channel_id=1, source_target_pairs={{0,8},{1,9},{2,10},{3,11},{4,12},{5,13},{6,14},{7,15},{8,0},{9,1},... | collective-permute-start | bytes 294920 | tf_op jit(solution)/shard_map/ppermute | solution.py:108
  22.3 0.0 collective-permute-start.6
  22.3 7.8 %collective-permute-done.refs_1_ = bf16[384,128]{1,0:T(8,128)(2,1)S(1)} collective-permute-done((bf16[384,128]{1,0:T(8,128)(2,1)S(1)}, bf16[384,128]{1,0:T(8,128)(2,1)S(1)}, u32[]{:S(2)}, u32[]{:S(2)}) %collective-permute-start) | collective-permute-done | bytes 98336 | tf_op jit(solution)/shard_map/ppermute | solution.py:108
  30.2 5.6 %collective-permute-start.7 = (bf16[768,128]{1,0:T(8,128)(2,1)S(1)}, bf16[768,128]{1,0:T(8,128)(2,1)S(1)}, u32[]{:S(2)}, u32[]{:S(2)}) collective-permute-start(bf16[768,128]{1,0:T(8,128)(2,1)S(1)} %shard_map.75.refs_0_.refs_3_), channel_id=1, source_target_pairs={{0,2},{1,3},{2,0},{3,1},{4,6},{5,7},{6,4},{7,5},{8,10},{9,11},{10,... | collective-permute-start | bytes 589832 | tf_op jit(solution)/shard_map/ppermute | solution.py:108
  35.7 0.0 collective-permute-done.11.refs_2_
  35.7 0.0 collective-permute-start.12
  35.7 0.5 collective-permute-start.8
  36.2 3.1 %collective-permute-done.7.refs_4_ = bf16[768,128]{1,0:T(8,128)(2,1)S(1)} collective-permute-done((bf16[768,128]{1,0:T(8,128)(2,1)S(1)}, bf16[768,128]{1,0:T(8,128)(2,1)S(1)}, u32[]{:S(2)}, u32[]{:S(2)}) %collective-permute-start.7) | collective-permute-done | bytes 196640 | tf_op jit(solution)/shard_map/ppermute | solution.py:108
  39.4 0.0 collective-permute-start.9
  39.4 2.0 %collective-permute-start.4 = (bf16[384,128]{1,0:T(8,128)(2,1)S(1)}, bf16[384,128]{1,0:T(8,128)(2,1)S(1)}, u32[]{:S(2)}, u32[]{:S(2)}) collective-permute-start(bf16[384,128]{1,0:T(8,128)(2,1)S(1)} %copy-done.7), channel_id=1, source_target_pairs={{0,2},{1,3},{2,0},{3,1},{4,6},{5,7},{6,4},{7,5},{8,10},{9,11},{10,... | collective-permute-start | bytes 294920 | tf_op jit(solution)/shard_map/ppermute | solution.py:108
  41.4 3.5 %collective-permute-done.4.refs_2_ = bf16[384,128]{1,0:T(8,128)(2,1)S(1)} collective-permute-done((bf16[384,128]{1,0:T(8,128)(2,1)S(1)}, bf16[384,128]{1,0:T(8,128)(2,1)S(1)}, u32[]{:S(2)}, u32[]{:S(2)}) %collective-permute-start.4) | collective-permute-done | bytes 98336 | tf_op jit(solution)/shard_map/ppermute | solution.py:108
  44.9 0.1 collective-permute-start.10
  45.0 0.0 collective-permute-done.6.refs_3_
  45.0 2.1 %shard_map.81.refs_0_.refs_5_ = f32[1024,128]{1,0:T(8,128)S(1)} custom-call(bf16[384,128]{1,0:T(8,128)(2,1)S(1)} %get-tuple-element.27.refs_0_, s32[1,5]{1,0:T(1,128)S(1)} %copy-done.10, bf16[1536,128]{1,0:T(8,128)(2,1)S(1)} %copy-done.4, bf16[1536,128]{1,0:T(8,128)(2,1)S(1)} %collective-permute-done.6.refs_3_, ...), custom_call_target="tpu_custom_call" | custom-call | flops 805306368 | bytes 3000000 | tf_op jit(solution)/shard_map/pallas_call | solution.py:24
  47.1 0.0 collective-permute-done.8.refs_5_
  47.1 0.0 collective-permute-done.9.refs_6_
  47.1 2.2 %shard_map.82 = (f32[256,128]{1,0:T(8,128)S(1)}, bf16[256,128]{1,0:T(8,128)(2,1)S(1)}) custom-call(f32[1024,128]{1,0:T(8,128)S(1)} %shard_map.81.refs_0_.refs_5_, s32[1,5]{1,0:T(1,128)S(1)} %copy-done.10, bf16[528,128]{1,0:T(8,128)(2,1)S(1)} %collective-permute-done.3.refs_2_, bf16[768,128]{1,0:T(8,128)(2,1)S(1)} %shard_map.75.refs_0_.refs_3_, ...), custom_call_target="tpu_custom_call" | custom-call | flops 536870912 | bytes 2000000 | tf_op jit(solution)/shard_map/pallas_call | solution.py:24
  49.3 3.2 %collective-permute-done.10.refs_2_ = bf16[384,128]{1,0:T(8,128)(2,1)S(1)} collective-permute-done((bf16[384,128]{1,0:T(8,128)(2,1)S(1)}, bf16[384,128]{1,0:T(8,128)(2,1)S(1)}, u32[]{:S(2)}, u32[]{:S(2)}) %collective-permute-start.10) | collective-permute-done | bytes 98336 | tf_op jit(solution)/shard_map/ppermute | solution.py:108
  52.5 0.7 %shard_map.83 = (f32[384,128]{1,0:T(8,128)}, bf16[384,128]{1,0:T(8,128)(2,1)S(1)}) custom-call(f32[256,128]{1,0:T(8,128)S(1)} %get-tuple-element.29.refs_0_.refs_3_, f32[384,128]{1,0:T(8,128)S(1)} %get-tuple-element.30.refs_1_, bf16[384,128]{1,0:T(8,128)(2,1)S(1)} %collective-permute-done.10.refs_2_), custom_call_target="tpu_custom_call" | custom-call | bytes 1000000 | tf_op jit(solution)/shard_map/pallas_call | solution.py:24
  53.2 1.5 %collective-permute-start.14 = (bf16[384,128]{1,0:T(8,128)(2,1)S(1)}, bf16[384,128]{1,0:T(8,128)(2,1)S(1)}, u32[]{:S(2)}, u32[]{:S(2)}) collective-permute-start(bf16[384,128]{1,0:T(8,128)(2,1)S(1)} %get-tuple-element.31.refs_0_), channel_id=1, source_target_pairs={{0,16},{16,0},{1,17},{17,1},{2,18},{18,2},{3,19},{19,3},{4,20},{20... | collective-permute-start | bytes 294920 | tf_op jit(solution)/shard_map/ppermute | solution.py:398
  54.6 3.2 %collective-permute-done.14.refs_5_ = bf16[384,128]{1,0:T(8,128)(2,1)S(1)} collective-permute-done((bf16[384,128]{1,0:T(8,128)(2,1)S(1)}, bf16[384,128]{1,0:T(8,128)(2,1)S(1)}, u32[]{:S(2)}, u32[]{:S(2)}) %collective-permute-start.14) | collective-permute-done | bytes 98336 | tf_op jit(solution)/shard_map/ppermute | solution.py:398
  57.9 0.0 collective-permute-start.15
  57.9 0.9 %collective-permute-start.13 = (bf16[256,128]{1,0:T(8,128)(2,1)S(1)}, bf16[256,128]{1,0:T(8,128)(2,1)S(1)}, u32[]{:S(2)}, u32[]{:S(2)}) collective-permute-start(bf16[256,128]{1,0:T(8,128)(2,1)S(1)} %get-tuple-element.32), channel_id=1, source_target_pairs={{0,4},{1,5},{2,6},{3,7},{4,0},{5,1},{6,2},{7,3},{8,12},{9,13},{10,... | collective-permute-start | bytes 196616 | tf_op jit(solution)/shard_map/ppermute | solution.py:108
  58.8 0.0 collective-permute-done.12.refs_3_
  58.8 3.8 %shard_map.84.refs_0_ = f32[1024,128]{1,0:T(8,128)S(1)} custom-call(bf16[384,128]{1,0:T(8,128)(2,1)S(1)} %get-tuple-element.31.refs_0_, s32[1,5]{1,0:T(1,128)S(1)} %copy-done.10, bf16[1536,128]{1,0:T(8,128)(2,1)S(1)} %collective-permute-done.11.refs_2_, bf16[1536,128]{1,0:T(8,128)(2,1)S(1)} %collective-permute-done.12.refs_3_, ...), custom_call_target="tpu_custom_call" | custom-call | flops 805306368 | bytes 3000000 | tf_op jit(solution)/shard_map/pallas_call | solution.py:24
  62.6 0.0 collective-permute-done.13.refs_4_
  62.6 0.0 collective-permute-done.15.refs_6_
  62.6 1.8 %shard_map.85 = bf16[1024,128]{1,0:T(8,128)(2,1)} custom-call(f32[1024,128]{1,0:T(8,128)S(1)} %shard_map.84.refs_0_, bf16[1024,256]{1,0:T(8,128)(2,1)S(1)} %copy-done, bf16[384,128]{1,0:T(8,128)(2,1)S(1)} %get-tuple-element.19.refs_0_.refs_3_.refs_2_, f32[256,128]{1,0:T(8,128)S(1)} %get-tuple-element.29.refs_0_.refs_3_, ...), custom_call_target="tpu_custom_call" | custom-call | flops 67108864 | bytes 2000000 | tf_op jit(solution)/shard_map/pallas_call | solution.py:24
  (19 shorter events, 0.1 us)
Async XLA Ops:
  0.0 5.3 %copy-start = (bf16[1024,256]{1,0:T(8,128)(2,1)S(1)}, bf16[1024,256]{1,0:T(8,128)(2,1)}, u32[]{:S(2)}) copy-start(bf16[1024,256]{1,0:T(8,128)(2,1)} %refs_1_.11) | copy-start | bytes 1572868
  0.0 1.0 %copy-start.1 = (bf16[1024,128]{1,0:T(8,128)(2,1)S(1)}, bf16[1024,128]{1,0:T(8,128)(2,1)}, u32[]{:S(2)}) copy-start(bf16[1024,128]{1,0:T(8,128)(2,1)} %refs_2_.1) | copy-start | bytes 786436
  1.0 0.9 %copy-start.2 = (bf16[1024,64]{0,1:T(8,128)(2,1)S(1)}, bf16[1024,64]{0,1:T(8,128)(2,1)}, u32[]{:S(2)}) copy-start(bf16[1024,64]{0,1:T(8,128)(2,1)} %param.7) | copy-start | bytes 393220
  1.9 3.4 %copy-start.5 = (bf16[256,512]{1,0:T(8,128)(2,1)S(1)}, bf16[256,512]{1,0:T(8,128)(2,1)}, u32[]{:S(2)}) copy-start(bf16[256,512]{1,0:T(8,128)(2,1)} %refs_4_.1) | copy-start | bytes 786436
  1.9 3.4 %copy-start.9 = (s32[1,256]{1,0:T(1,128)S(1)}, s32[1,256]{1,0:T(1,128)}, u32[]{:S(2)}) copy-start(s32[1,256]{1,0:T(1,128)} %refs_5_.1) | copy-start | bytes 3076
  2.2 8.4 %collective-permute-start.2 = (bf16[1536,128]{1,0:T(8,128)(2,1)S(1)}, bf16[1536,128]{1,0:T(8,128)(2,1)S(1)}, u32[]{:S(2)}, u32[]{:S(2)}) collective-permute-start(bf16[1536,128]{1,0:T(8,128)(2,1)S(1)} %shard_map.73.refs_0_.refs_2_), channel_id=1, source_target_pairs={{0,1},{1,0},{2,3},{3,2},{4,5},{5,4},{6,7},{7,6},{8,9},{9,8},{10,11... | collective-permute-start | bytes 1179656 | tf_op jit(solution)/shard_map/ppermute | solution.py:108
  2.7 12.6 %collective-permute-start.5 = (bf16[1536,128]{1,0:T(8,128)(2,1)S(1)}, bf16[1536,128]{1,0:T(8,128)(2,1)S(1)}, u32[]{:S(2)}, u32[]{:S(2)}) collective-permute-start(bf16[1536,128]{1,0:T(8,128)(2,1)S(1)} %shard_map.73.refs_0_.refs_2_), channel_id=1, source_target_pairs={{0,2},{1,3},{2,0},{3,1},{4,6},{5,7},{6,4},{7,5},{8,10},{9,11},{10,... | collective-permute-start | bytes 1179656 | tf_op jit(solution)/shard_map/ppermute | solution.py:108
  5.3 0.7 %copy-start.8 = (s32[1,512]{1,0:T(1,128)S(1)}, s32[1,512]{1,0:T(1,128)}, u32[]{:S(2)}) copy-start(s32[1,512]{1,0:T(1,128)} %refs_6_.1) | copy-start | bytes 6148
  6.8 1.4 %collective-permute-start.1 = (bf16[384,128]{1,0:T(8,128)(2,1)S(1)}, bf16[384,128]{1,0:T(8,128)(2,1)S(1)}, u32[]{:S(2)}, u32[]{:S(2)}) collective-permute-start(bf16[384,128]{1,0:T(8,128)(2,1)S(1)} %get-tuple-element.21), channel_id=1, source_target_pairs={{0,1},{1,0},{2,3},{3,2},{4,5},{5,4},{6,7},{7,6},{8,9},{9,8},{10,11... | collective-permute-start | bytes 294920 | tf_op jit(solution)/shard_map/ppermute | solution.py:108
  8.2 0.7 %copy-start.10 = (s32[1,5]{1,0:T(1,128)S(1)}, s32[1,5]{1,0:T(1,128)}, u32[]{:S(2)}) copy-start(s32[1,5]{1,0:T(1,128)} %refs_1_.10) | copy-start | bytes 64
  9.0 5.7 %collective-permute-start.3 = (bf16[528,128]{1,0:T(8,128)(2,1)S(1)}, bf16[528,128]{1,0:T(8,128)(2,1)S(1)}, u32[]{:S(2)}, u32[]{:S(2)}) collective-permute-start(bf16[528,128]{1,0:T(8,128)(2,1)S(1)} %get-tuple-element.22.refs_0_), channel_id=1, source_target_pairs={{0,4},{1,5},{2,6},{3,7},{4,0},{5,1},{6,2},{7,3},{8,12},{9,13},{10,... | collective-permute-start | bytes 405512 | tf_op jit(solution)/shard_map/ppermute | solution.py:108
  14.7 0.6 copy-start.6
  15.3 0.7 %copy-start.3 = (bf16[1536,128]{1,0:T(8,128)(2,1)}, bf16[1536,128]{1,0:T(8,128)(2,1)S(1)}, u32[]{:S(2)}) copy-start(bf16[1536,128]{1,0:T(8,128)(2,1)S(1)} %collective-permute-done.5.refs_0_) | copy-start | bytes 1179652
  16.1 23.3 %copy-start.7 = (bf16[384,128]{1,0:T(8,128)(2,1)S(1)}, bf16[384,128]{1,0:T(8,128)(2,1)}, u32[]{:S(2)}) copy-start(bf16[384,128]{1,0:T(8,128)(2,1)} %copy-done.6) | copy-start | bytes 294916
  16.1 28.9 %copy-start.4 = (bf16[1536,128]{1,0:T(8,128)(2,1)S(1)}, bf16[1536,128]{1,0:T(8,128)(2,1)}, u32[]{:S(2)}) copy-start(bf16[1536,128]{1,0:T(8,128)(2,1)} %shard_map.80.refs_2_) | copy-start | bytes 1179652
  16.1 19.7 %collective-permute-start.11 = (bf16[1536,128]{1,0:T(8,128)(2,1)}, bf16[1536,128]{1,0:T(8,128)(2,1)S(1)}, u32[]{:S(2)}, u32[]{:S(2)}) collective-permute-start(bf16[1536,128]{1,0:T(8,128)(2,1)} %shard_map.80.refs_2_), channel_id=1, source_target_pairs={{0,4},{1,5},{4,8},{5,9},{8,12},{9,13},{6,2},{7,3},{10,6},{11,7},{1... | collective-permute-start | bytes 1179656 | tf_op jit(solution)/shard_map/ppermute | solution.py:351
  19.7 10.5 %collective-permute-start = (bf16[384,128]{1,0:T(8,128)(2,1)S(1)}, bf16[384,128]{1,0:T(8,128)(2,1)S(1)}, u32[]{:S(2)}, u32[]{:S(2)}) collective-permute-start(bf16[384,128]{1,0:T(8,128)(2,1)S(1)} %get-tuple-element.19.refs_0_.refs_3_.refs_2_), channel_id=1, source_target_pairs={{0,8},{1,9},{2,10},{3,11},{4,12},{5,13},{6,14},{7,15},{8,0},{9,1},... | collective-permute-start | bytes 294920 | tf_op jit(solution)/shard_map/ppermute | solution.py:108
  22.3 22.7 %collective-permute-start.6 = (bf16[1536,128]{1,0:T(8,128)(2,1)}, bf16[1536,128]{1,0:T(8,128)(2,1)S(1)}, u32[]{:S(2)}, u32[]{:S(2)}) collective-permute-start(bf16[1536,128]{1,0:T(8,128)(2,1)} %shard_map.80.refs_2_), channel_id=1, source_target_pairs={{0,1},{1,0},{2,3},{3,2},{4,5},{5,4},{6,7},{7,6},{8,9},{9,8},{10,11... | collective-permute-start | bytes 1179656 | tf_op jit(solution)/shard_map/ppermute | solution.py:108
  30.2 9.2 %collective-permute-start.7 = (bf16[768,128]{1,0:T(8,128)(2,1)S(1)}, bf16[768,128]{1,0:T(8,128)(2,1)S(1)}, u32[]{:S(2)}, u32[]{:S(2)}) collective-permute-start(bf16[768,128]{1,0:T(8,128)(2,1)S(1)} %shard_map.75.refs_0_.refs_3_), channel_id=1, source_target_pairs={{0,2},{1,3},{2,0},{3,1},{4,6},{5,7},{6,4},{7,5},{8,10},{9,11},{10,... | collective-permute-start | bytes 589832 | tf_op jit(solution)/shard_map/ppermute | solution.py:108
  35.7 23.0 %collective-permute-start.12 = (bf16[1536,128]{1,0:T(8,128)(2,1)S(1)}, bf16[1536,128]{1,0:T(8,128)(2,1)S(1)}, u32[]{:S(2)}, u32[]{:S(2)}) collective-permute-start(bf16[1536,128]{1,0:T(8,128)(2,1)S(1)} %collective-permute-done.11.refs_2_), channel_id=1, source_target_pairs={{0,1},{1,0},{2,3},{3,2},{4,5},{5,4},{6,7},{7,6},{8,9},{9,8},{10,11... | collective-permute-start | bytes 1179656 | tf_op jit(solution)/shard_map/ppermute | solution.py:108
  35.7 11.4 %collective-permute-start.8 = (bf16[768,128]{1,0:T(8,128)(2,1)S(1)}, bf16[768,128]{1,0:T(8,128)(2,1)S(1)}, u32[]{:S(2)}, u32[]{:S(2)}) collective-permute-start(bf16[768,128]{1,0:T(8,128)(2,1)S(1)} %shard_map.75.refs_0_.refs_3_), channel_id=1, source_target_pairs={{0,1},{1,0},{2,3},{3,2},{4,5},{5,4},{6,7},{7,6},{8,9},{9,8},{10,11... | collective-permute-start | bytes 589832 | tf_op jit(solution)/shard_map/ppermute | solution.py:108
  39.4 7.7 %collective-permute-start.9 = (bf16[768,128]{1,0:T(8,128)(2,1)S(1)}, bf16[768,128]{1,0:T(8,128)(2,1)S(1)}, u32[]{:S(2)}, u32[]{:S(2)}) collective-permute-start(bf16[768,128]{1,0:T(8,128)(2,1)S(1)} %collective-permute-done.7.refs_4_), channel_id=1, source_target_pairs={{0,1},{1,0},{2,3},{3,2},{4,5},{5,4},{6,7},{7,6},{8,9},{9,8},{10,11... | collective-permute-start | bytes 589832 | tf_op jit(solution)/shard_map/ppermute | solution.py:108
  39.4 5.5 %collective-permute-start.4 = (bf16[384,128]{1,0:T(8,128)(2,1)S(1)}, bf16[384,128]{1,0:T(8,128)(2,1)S(1)}, u32[]{:S(2)}, u32[]{:S(2)}) collective-permute-start(bf16[384,128]{1,0:T(8,128)(2,1)S(1)} %copy-done.7), channel_id=1, source_target_pairs={{0,2},{1,3},{2,0},{3,1},{4,6},{5,7},{6,4},{7,5},{8,10},{9,11},{10,... | collective-permute-start | bytes 294920 | tf_op jit(solution)/shard_map/ppermute | solution.py:108
  44.9 7.6 %collective-permute-start.10 = (bf16[384,128]{1,0:T(8,128)(2,1)S(1)}, bf16[384,128]{1,0:T(8,128)(2,1)S(1)}, u32[]{:S(2)}, u32[]{:S(2)}) collective-permute-start(bf16[384,128]{1,0:T(8,128)(2,1)S(1)} %get-tuple-element.27.refs_0_), channel_id=1, source_target_pairs={{0,8},{1,9},{2,10},{3,11},{4,12},{5,13},{6,14},{7,15},{8,0},{9,1},... | collective-permute-start | bytes 294920 | tf_op jit(solution)/shard_map/ppermute | solution.py:108
  53.2 4.7 %collective-permute-start.14 = (bf16[384,128]{1,0:T(8,128)(2,1)S(1)}, bf16[384,128]{1,0:T(8,128)(2,1)S(1)}, u32[]{:S(2)}, u32[]{:S(2)}) collective-permute-start(bf16[384,128]{1,0:T(8,128)(2,1)S(1)} %get-tuple-element.31.refs_0_), channel_id=1, source_target_pairs={{0,16},{16,0},{1,17},{17,1},{2,18},{18,2},{3,19},{19,3},{4,20},{20... | collective-permute-start | bytes 294920 | tf_op jit(solution)/shard_map/ppermute | solution.py:398
  57.9 4.7 %collective-permute-start.15 = (bf16[384,128]{1,0:T(8,128)(2,1)S(1)}, bf16[384,128]{1,0:T(8,128)(2,1)S(1)}, u32[]{:S(2)}, u32[]{:S(2)}) collective-permute-start(bf16[384,128]{1,0:T(8,128)(2,1)S(1)} %collective-permute-done.14.refs_5_), channel_id=1, source_target_pairs={{0,1},{1,0},{2,3},{3,2},{4,5},{5,4},{6,7},{7,6},{8,9},{9,8},{10,11... | collective-permute-start | bytes 294920 | tf_op jit(solution)/shard_map/ppermute | solution.py:108
  57.9 4.7 %collective-permute-start.13 = (bf16[256,128]{1,0:T(8,128)(2,1)S(1)}, bf16[256,128]{1,0:T(8,128)(2,1)S(1)}, u32[]{:S(2)}, u32[]{:S(2)}) collective-permute-start(bf16[256,128]{1,0:T(8,128)(2,1)S(1)} %get-tuple-element.32), channel_id=1, source_target_pairs={{0,4},{1,5},{2,6},{3,7},{4,0},{5,1},{6,2},{7,3},{8,12},{9,13},{10,... | collective-permute-start | bytes 196616 | tf_op jit(solution)/shard_map/ppermute | solution.py:108

commit v3 on v0

v3 whole, which is shorter than its diff:
```python
import functools
import math

import jax
import jax.numpy as jnp
from jax import lax
from jax.experimental import pallas as pl
from jax.experimental.pallas import tpu as pltpu
from jax.sharding import PartitionSpec as P

BF16 = jnp.bfloat16
F32 = jnp.float32
VMEM_BYTES = 24 * 1024 * 1024
LANES = 128
TARGET_ROWS = 512
SOURCE_ROWS = 512
WORK = {
    "prepare": 10**6,
    "first_add": 10**6,
    "near_self": 2 * 10**9,
    "near_core": 2 * 10**9,
    "add_a": 10**6,
    "near_beside": 2 * 10**9,
    "add_b": 10**6,
    "near_across": 2 * 10**9,
    "add_c": 10**6,
    "sibling": 2 * 10**9,
    "near_far": 2 * 10**9,
    "near_last": 2 * 10**9,
    "final": 2 * 10**9,
}


def vmem():
    return pl.BlockSpec(memory_space=pltpu.VMEM)


def call(body, outs, ins, scratch=(), after=(), in_place=False, work=10**6):
    waits = len(after)
    return pl.pallas_call(
        lambda *refs: body(*refs[waits:]),
        out_shape=[jax.ShapeDtypeStruct(shape, dtype) for shape, dtype in outs],
        in_specs=[pl.BlockSpec(memory_space=pl.ANY) for _ in after] + [vmem() for _ in ins],
        out_specs=[vmem() for _ in outs],
        scratch_shapes=[pltpu.VMEM(shape, dtype) for shape, dtype in scratch],
        input_output_aliases={waits: 0} if in_place else {},
        compiler_params=pltpu.CompilerParams(vmem_limit_bytes=VMEM_BYTES),
        cost_estimate=pl.CostEstimate(flops=work, bytes_accessed=0, transcendentals=0),
    )(*after, *ins)


def hand_on(value, *after):
    return pl.pallas_call(
        lambda *refs: None,
        out_shape=jax.ShapeDtypeStruct(value.shape, value.dtype),
        in_specs=[vmem()] + [pl.BlockSpec(memory_space=pl.ANY) for _ in after],
        out_specs=vmem(),
        input_output_aliases={0: 0},
        compiler_params=pltpu.CompilerParams(vmem_limit_bytes=VMEM_BYTES),
        cost_estimate=pl.CostEstimate(flops=0, bytes_accessed=0, transcendentals=0),
    )(value, *after)


def dot_nt(a, b):
    return lax.dot_general(a, b, (((1,), (1,)), ((), ())), preferred_element_type=F32)


def dot_nn(a, b):
    return jnp.dot(a, b, preferred_element_type=F32)


def xor_exchange(value, axis, mask):
    return lax.ppermute(value, axis, [(i, i ^ mask) for i in range(lax.axis_size(axis))])


def up16(rows):
    return -(-rows // 16) * 16


def norm_rows(points):
    return up16(3 * points // LANES)


def scale_of(features):
    return 4.0 / features * math.log2(math.e)


def three_parts(values):
    high = values.astype(BF16).astype(F32)
    rest = values - high
    middle = rest.astype(BF16).astype(F32)
    return high, middle, rest - middle


def norm_block(norms):
    count = norms.shape[1] // LANES
    parts = [
        part[:, i * LANES : (i + 1) * LANES] for part in three_parts(norms) for i in range(count)
    ]
    rest = norm_rows(norms.shape[1]) - len(parts)
    return jnp.concatenate(parts + [jnp.zeros((rest, LANES), F32)], axis=0)


def source_norms(block, points):
    count = points // LANES
    block = block.astype(F32)
    rows = block[:count] + block[count : 2 * count] + block[2 * count : 3 * count]
    return tuple(
        jnp.concatenate([rows[i : i + 1] for i in range(h * count // 2, (h + 1) * count // 2)], axis=1)
        for h in range(2)
    )


def target_forms(packed, features):
    wide = packed.astype(F32)
    turned = pltpu.roll(wide, features, 1)
    lane = lax.broadcasted_iota(jnp.int32, wide.shape, 1)
    low, high, norms = [], [], []
    for first, second in ((wide, turned), (turned, wide)):
        kept = jnp.where(lane < features, first, 0.0)
        low.append(kept)
        high.append(jnp.where(lane >= features, second, 0.0))
        parts = three_parts(-0.5 * jnp.sum(kept * kept, axis=1, keepdims=True))
        norms.append(
            jnp.where(lane == 0, parts[0], jnp.where(lane == 1, parts[1], jnp.where(lane == 2, parts[2], 0.0)))
        )
    return tuple(jnp.concatenate(form, axis=0).astype(BF16) for form in (low, high, norms))


def ones_beside(packed):
    lane = lax.broadcasted_iota(jnp.int32, packed.shape, 1)
    return jnp.concatenate([packed, jnp.where(lane < 3, 1.0, 0.0).astype(BF16)], axis=1)


def kernel_values(targets, parts, sources, norms, features):
    exponent = dot_nt(jnp.concatenate([targets, parts], axis=1), sources) * scale_of(features) + norms
    return jnp.exp2(exponent).astype(BF16)


def flag_of(flags_ref, distance):
    columns = flags_ref.shape[1]
    lane = lax.broadcasted_iota(jnp.int32, (1, columns), 1)
    here = lane == distance + (columns - 1) // 2
    return jnp.sum(jnp.where(here, flags_ref[...], 0).astype(F32), axis=1, keepdims=True)


def prepare_kernel(
    points_hbm, weights_hbm, interp_hbm, ci_hbm, rows_hbm, flags_hbm, ids_hbm,
    halo_ref, sv_ref, sum_ref, send_ref, flags_ref,
    points_ref, interp_ref, ci_ref, rows_ref, ids_ref, all_ref, arrived,
):
    features, points = points_ref.shape
    half, skeletons = points // 2, interp_ref.shape[1]
    pairs = (
        (rows_hbm, rows_ref),
        (points_hbm, points_ref),
        (weights_hbm, halo_ref.at[pl.ds(half, points)]),
        (interp_hbm, interp_ref),
        (ids_hbm, ids_ref),
        (ci_hbm, ci_ref),
        (flags_hbm, flags_ref),
    )
    copies = [pltpu.make_async_copy(source, place, arrived.at[i]) for i, (source, place) in enumerate(pairs)]
    for copy in copies:
        copy.start()
    leaf = lax.axis_index("leaf")
    core = leaf % 2
    cluster_count, picked = ids_ref.shape
    members = lax.axis_size("leaf") // cluster_count
    source_scale = -0.5 * scale_of(features)

    def packed(turned):
        n = turned.shape[1]
        return jnp.concatenate([turned[:, : n // 2], turned[:, n // 2 :]], axis=0).T

    def norms(turned):
        return source_scale * jnp.sum(turned * turned, axis=0, keepdims=True)

    copies[0].wait()
    one = (
        lax.broadcasted_iota(jnp.int32, (points, skeletons), 0) == rows_ref[...]
    ).astype(F32).astype(BF16)
    copies[1].wait()
    skeleton = dot_nn(points_ref[...], one)
    copies[2].wait()
    weights_turned = halo_ref[half : half + points, :].astype(F32).T.astype(BF16)
    copies[3].wait()
    charges_turned = dot_nn(weights_turned, interp_ref[...]).astype(BF16)
    copies[4].wait()
    ids = ids_ref[pl.ds(leaf // members, 1), :] - (leaf % members) * skeletons
    chosen = (
        lax.broadcasted_iota(jnp.int32, (skeletons, picked), 0) == ids
    ).astype(F32).astype(BF16)
    cluster = dot_nn(skeleton.astype(BF16), chosen)
    copies[5].wait()
    sums = dot_nn(charges_turned, ci_ref[...]).T
    part = picked // 2
    rows = sum_ref.shape[0]
    for h in range(2):
        columns = slice(h * part, (h + 1) * part)
        place = slice(h * rows, h * rows + part)
        all_ref[place, :] = sums[columns]
        place = slice(h * rows + part, h * rows + part + part // 2)
        all_ref[place, :] = packed(cluster[:, columns])
        place = slice(h * rows + part + part // 2, (h + 1) * rows)
        all_ref[place, :] = norm_block(norms(cluster[:, columns]))
    sum_ref[...] = all_ref[pl.ds(core * rows, rows), :]
    send_ref[...] = all_ref[pl.ds((1 - core) * rows, rows), :].astype(BF16)
    sk_half, sk_norms = skeletons // 2, norm_rows(skeletons)
    sv_ref[:sk_half, :] = packed(skeleton).astype(BF16)
    sv_ref[sk_half : sk_half + sk_norms, :] = norm_block(norms(skeleton)).astype(BF16)
    sv_ref[sk_half + sk_norms :, :] = charges_turned.astype(F32).T.astype(BF16)
    wide = points_ref[...].astype(F32)
    halo_ref[:half, :] = packed(wide).astype(BF16)
    halo_ref[half + points :, :] = norm_block(norms(wide)).astype(BF16)
    copies[6].wait()


def add_kernel(with_skeleton, last, sum_ref, got_ref, *refs):
    rows = sum_ref.shape[0]
    total = sum_ref[...] + got_ref[:rows, :].astype(F32)
    if with_skeleton:
        flags_ref, sv_ref, *refs = refs
        send_ref = refs[0]
        points = send_ref.shape[0] - 16 - rows
        send_ref[rows : rows + points, :] = sv_ref[:points, :]
        columns = flags_ref.shape[1]
        row = lax.broadcasted_iota(jnp.int32, (columns, LANES), 0)
        lane = lax.broadcasted_iota(jnp.int32, (columns, LANES), 1)
        spread = dot_nn(flags_ref[...].astype(F32), (row == lane).astype(F32))
        send_ref[rows + points :, :] = jnp.broadcast_to(spread, (16, LANES)).astype(BF16)
    refs[0][:rows, :] = total.astype(BF16)
    if not last:
        refs[1][...] = total


def near_kernel(stage, across, features, *refs):
    leaf = lax.axis_index("leaf")
    core, chip = leaf % 2, (leaf // 2) % 2
    side, beside = 1 - 2 * core, 1 - 2 * chip
    first = stage == 0 and not across
    if first:
        flags_ref, halo_ref, low_ref, high_ref, parts_ref, near_ref = refs
        half = near_ref.shape[0] // 2
        forms = target_forms(halo_ref[:half, :], features)
        for ref, form in zip((low_ref, high_ref, parts_ref), forms):
            ref[...] = form
        distance = 0
    else:
        before_ref, flags_ref, halo_ref, low_ref, high_ref, parts_ref, near_ref = refs
        half = near_ref.shape[0] // 2
        if across:
            distance = side if stage == 0 else -side
        else:
            distance = 2 * beside if stage == 1 else -2 * beside

    def tile():
        flag = flag_of(flags_ref, distance)
        norms = source_norms(halo_ref[3 * half :, :], 2 * half)
        step = min(SOURCE_ROWS, half)
        for start in range(0, 2 * half, TARGET_ROWS):
            rows = slice(start, min(start + TARGET_ROWS, 2 * half))
            total = None
            for place in range(0, half, step):
                sources = ones_beside(halo_ref[place : place + step, :])
                for h, ref in enumerate((low_ref, high_ref)):
                    terms = norms[h][:, place : place + step]
                    values = kernel_values(ref[rows, :], parts_ref[rows, :], sources, terms, features)
                    mass = halo_ref[(h + 1) * half + place : (h + 1) * half + place + step, :]
                    term = dot_nn(values, mass)
                    total = term if total is None else total + term
            near_ref[rows, :] = flag * total if first else before_ref[rows, :] + flag * total

    if across and stage > 0:
        pl.when(core != chip if stage == 1 else core == chip)(tile)
    else:
        tile()


def grouped(count, rows):
    step = max(1, SOURCE_ROWS // rows)
    return [range(i, min(i + step, count)) for i in range(0, count, step)]


def sibling_kernel(masks, reduced, features, skeletons, flags_ref, got_ref, *refs):
    pieces, (own_ref, send_ref) = refs[: len(masks)], refs[len(masks) :]
    leaf = lax.axis_index("leaf")
    reach = (flags_ref.shape[1] - 1) // 2
    half, points = skeletons // 2, skeletons // 2 + norm_rows(skeletons)
    start = got_ref.shape[0] - 16 - points
    other_flags = got_ref[start + points :, :].astype(F32)[:1, :]
    lane = lax.broadcasted_iota(jnp.int32, other_flags.shape, 1)
    forms = zip(
        target_forms(pieces[0][:half, :], features),
        target_forms(got_ref[start : start + half, :], features),
    )
    low, high, parts = [jnp.concatenate(form, axis=0) for form in forms]
    kept = []
    for mask in masks:
        source = leaf ^ mask
        flagged = jnp.where(lane == source - (leaf ^ reduced) + reach, other_flags, 0.0)
        other = 1.0 - jnp.sum(flagged, axis=1, keepdims=True)
        kept.append((1.0 - flag_of(flags_ref, source - leaf), other))
    own = send = None
    for group in grouped(len(masks), half):
        sources = ones_beside(jnp.concatenate([pieces[i][:half, :] for i in group], axis=0))
        norms = [source_norms(pieces[i][half:points, :], skeletons) for i in group]
        for h, targets in enumerate((low, high)):
            terms = jnp.concatenate([n[h] for n in norms], axis=1)
            values = kernel_values(targets, parts, sources, terms, features)
            mass = [pieces[i][points + h * half : points + (h + 1) * half, :].astype(F32) for i in group]
            masses = [
                jnp.concatenate([m * kept[i][k] for m, i in zip(mass, group)], axis=0).astype(BF16)
                for k in range(2)
            ]
            to_own = dot_nn(values[:skeletons], masses[0])
            to_other = dot_nn(values[skeletons:], masses[1])
            own = to_own if own is None else own + to_own
            send = to_other if send is None else send + to_other
    own_ref[...] = own
    send_ref[...] = send.astype(send_ref.dtype)


def final_kernel(count, features, near_ref, interp_ref, sv_ref, own_ref, got_ref, *refs):
    packs, out_ref = refs[:count], refs[count]
    skeletons = interp_ref.shape[1]
    low, high, parts = target_forms(sv_ref[: skeletons // 2, :], features)
    half = max(r for r in range(1, packs[0].shape[0]) if 3 * r + norm_rows(2 * r) <= packs[0].shape[0])
    field = own_ref[...] + got_ref[...].astype(F32)
    for group in grouped(count, half):
        sources = ones_beside(jnp.concatenate([packs[i][2 * half : 3 * half, :] for i in group], axis=0))
        norms = [source_norms(packs[i][3 * half :, :], 2 * half) for i in group]
        for h, targets in enumerate((low, high)):
            terms = jnp.concatenate([n[h] for n in norms], axis=1)
            values = kernel_values(targets, parts, sources, terms, features)
            mass = jnp.concatenate([packs[i][h * half : (h + 1) * half, :] for i in group], axis=0)
            field += dot_nn(values, mass)
    coarse = field.astype(BF16)
    out_ref[...] = (near_ref[...] + dot_nn(interp_ref[...], coarse)).astype(out_ref.dtype)


def on_device(points, weights, interp, cluster_interp, skeleton_rows, near_flags, cluster_rows):
    leaves, groups = lax.axis_size("leaf"), lax.axis_size("group")
    leaf_points, features = points.shape
    columns = weights.shape[1]
    skeletons = interp.shape[1]
    cluster_count, picked = cluster_rows.shape
    members = leaves // cluster_count
    core_mask, chip_mask, reduced = 1, 2, 4
    half, part = leaf_points // 2, picked // 2
    sum_rows = part + part // 2 + norm_rows(part)
    sv_points = skeletons // 2 + norm_rows(skeletons)

    arguments = [points.T, weights, interp, cluster_interp, skeleton_rows, near_flags, cluster_rows]
    outs = [
        ((half + leaf_points + norm_rows(leaf_points), columns), BF16),
        ((sv_points + skeletons, columns), BF16),
        ((sum_rows, columns), F32),
        ((sum_rows, columns), BF16),
        (near_flags.shape, near_flags.dtype),
    ]
    scratch = [(x.shape, x.dtype) for x in (arguments[0], interp, cluster_interp, skeleton_rows, cluster_rows)]
    scratch += [((2 * sum_rows, columns), F32)]
    halo, skeleton, cluster_sum, cluster_send, flags = pl.pallas_call(
        prepare_kernel,
        out_shape=[jax.ShapeDtypeStruct(shape, dtype) for shape, dtype in outs],
        in_specs=[pl.BlockSpec(memory_space=pltpu.HBM) for _ in arguments],
        out_specs=[vmem() for _ in outs],
        scratch_shapes=[pltpu.VMEM(shape, dtype) for shape, dtype in scratch]
        + [pltpu.SemaphoreType.DMA((len(arguments),))],
        compiler_params=pltpu.CompilerParams(vmem_limit_bytes=VMEM_BYTES),
        cost_estimate=pl.CostEstimate(flops=WORK["prepare"], bytes_accessed=0, transcendentals=0),
    )(*[pltpu.with_memory_space_constraint(x, pltpu.HBM) for x in arguments])

    def add(name, total, got, mask, after=(), last=False):
        with_skeleton = mask == reduced
        rows = sum_rows + (sv_points + 16 if with_skeleton else 0)
        outs = [((rows, columns), BF16)] + ([] if last else [((sum_rows, columns), F32)])
        ins = [total, got] + ([flags, skeleton] if with_skeleton else [])
        body = functools.partial(add_kernel, with_skeleton, last)
        send, *total = call(body, outs, ins, after=after, work=WORK[name])
        return send, total[0] if total else None

    got = xor_exchange(cluster_send, "leaf", core_mask)
    pieces = {0: skeleton}
    pieces[chip_mask] = xor_exchange(skeleton, "leaf", chip_mask)
    pieces[core_mask] = xor_exchange(skeleton, "leaf", core_mask)
    halo_core = xor_exchange(halo, "leaf", core_mask)
    halo_beside = xor_exchange(halo, "leaf", chip_mask)
    add_masks = [1 << i for i in reversed(range(1, members.bit_length() - 1))]
    names = ["first_add", "add_a", "add_b", "add_c"]
    cluster_send, cluster_sum = add(names[0], cluster_sum, got, add_masks[0])
    got = xor_exchange(cluster_send, "leaf", add_masks[0])

    gather_masks = [1 << i for i in reversed(range(2, leaves.bit_length() - 1)) if 1 << i != reduced]
    known = [0]
    for mask in gather_masks:
        for m in list(known):
            pieces[m | mask] = xor_exchange(pieces[m], "leaf", mask)
            known.append(m | mask)
    for m in known[1:]:
        pieces[m | chip_mask] = xor_exchange(pieces[m], "leaf", chip_mask)
    for m in known:
        for n in (m, m | chip_mask):
            if n:
                pieces[n | core_mask] = xor_exchange(pieces[n], "leaf", core_mask)

    tile = ((leaf_points, columns), BF16)
    *targets, near = call(
        functools.partial(near_kernel, 0, False, features),
        [tile, tile, tile, ((leaf_points, columns), F32)],
        [flags, halo],
        after=[cluster_send],
        work=WORK["near_self"],
    )

    def near_step(name, near, stage, across, other, *after):
        return call(
            functools.partial(near_kernel, stage, across, features),
            [((leaf_points, columns), F32)],
            [near, flags, other, *targets],
            after=after,
            in_place=True,
            work=WORK[name],
        )[0]

    near = near_step("near_core", near, 0, True, halo_core)

    cluster_send, cluster_sum = add(names[1], cluster_sum, got, add_masks[1], [near])
    partner = got = xor_exchange(cluster_send, "leaf", add_masks[1])

    halo_beside = hand_on(halo_beside, cluster_send)
    ahead = [(i, i + 4) for i in range(leaves - 4) if i & chip_mask == 0]
    behind = [(i, i - 4) for i in range(4, leaves) if i & chip_mask != 0]
    halo_far = lax.ppermute(halo_beside, "leaf", ahead + behind)
    halo_across = xor_exchange(halo_beside, "leaf", core_mask)
    near = near_step("near_beside", near, 1, False, halo_beside)

    cluster_send, cluster_sum = add(names[2], cluster_sum, got, add_masks[2], [near])
    got = xor_exchange(cluster_send, "leaf", add_masks[2])
    near = near_step("near_across", near, 1, True, halo_across, cluster_send)

    cluster_send, _ = add(names[3], cluster_sum, got, 0, [near], True)
    own_group = [cluster_send]
    mask = members
    while mask < leaves:
        own_group += [xor_exchange(pack, "leaf", mask) for pack in own_group]
        mask *= 2
    packs = []
    for shift in range(1, groups):
        order = [(i, (i + shift) % groups) for i in range(groups)]
        packs += [lax.ppermute(pack, "group", order) for pack in own_group]

    masks = sorted(pieces)
    field, field_send = call(
        functools.partial(sibling_kernel, masks, reduced, features, skeletons),
        [((skeletons, columns), F32), ((skeletons, columns), BF16)],
        [flags, partner] + [pieces[m] for m in masks],
        after=[cluster_send],
        work=WORK["sibling"],
    )
    field_got = xor_exchange(field_send, "leaf", reduced)

    halo_far = hand_on(halo_far, field)
    halo_far_across = xor_exchange(halo_far, "leaf", core_mask)
    near = near_step("near_far", near, 2, False, halo_far)
    packs += [xor_exchange(pack, "leaf", core_mask) for pack in packs]
    near = near_step("near_last", near, 2, True, halo_far_across)

    (potential,) = call(
        functools.partial(final_kernel, len(packs), features),
        [((leaf_points, columns), BF16)],
        [near, interp, skeleton, field, field_got] + packs,
        work=WORK["final"],
    )
    return potential


def solution(mesh):
    placed = (P(("group", "leaf"), None),) * 6 + (P("group", None),)
    return jax.shard_map(
        on_device, mesh=mesh, in_specs=placed, out_specs=P(("group", "leaf"), None), check_vma=False
    )
```

time: 151 us -> 51.4 us (0.34)
  blocking collectives: 82.8 us -> 0 us
  matrix products: 20.8 us -> 0 us
  between operations: 16.8 us -> 0.19 us
  waiting for transfers between devices: 0.08 us -> 14.7 us
  Pallas kernels: 0 us -> 14.3 us
  local copies, waits for them, and re-layouts: 7.73 us -> 0.01 us
  starting transfers between devices: 16.8 us -> 21.5 us
  other arithmetic: 3.86 us -> 0 us
    all_gather x5 -> x0, blocking collectives: 82.8 us -> none  [the longest x1 30.7 us: on_device(): lax.all_gather(skeleton, 'leaf', axis=0, tiled=True)]
    dot_general x12 -> x0, matrix products: 20.8 us -> none  [the longest x8 19.2 us: tile_product(): jnp.dot(kernel_tile(targets, sources), source_weights, preferred_element_...]
    ppermute x8 -> x19, waiting for transfers between devices: 0.02 us -> 14.7 us  [the longest x17 11.8 us: xor_exchange(): lax.ppermute(value, axis, [(i, i ^ mask) for i in range(lax.axis_size(axi...]
    pallas_call x0 -> x15, Pallas kernels: none -> 14.3 us  [the longest x12 12.1 us: call(): pl.pallas_call(lambda *refs: body(*refs[waits:]), out_shape=[jax.ShapeDty...]
    ppermute x8 -> x19, starting transfers between devices: 16.8 us -> 21.5 us  [the longest x17 17.1 us: xor_exchange(): lax.ppermute(value, axis, [(i, i ^ mask) for i in range(lax.axis_size(axi...]
    unnamed x22 -> x2, local copies, waits for them, and re-layouts: 3.27 us -> 0.01 us
    slice x5 -> x0, local copies, waits for them, and re-layouts: 2.44 us -> none  [the longest x2 0.94 us: on_device(): cluster_mass = received[:, feature_count:].astype(jnp.bfloat16)]
    reduce_sum x13 -> x0, other arithmetic: 1.63 us -> none  [the longest x7 1.07 us: kernel_tile(): source_norm = jnp.sum(jnp.square(sources.astype(jnp.float32)), axis=1)]
  transfers between devices with their start and end apart: 10 -> 19, of which waited for: 0 -> 8; matrix products, arithmetic and copies ran while one was open for 14% -> 0% of each run, Pallas kernels for 0% -> 21%
where the time goes in v3:
time: 51.4 us; the launch traced here: 50.7 us
  starting transfers between devices  21.5 us (42%)
  waiting for transfers between devices  14.7 us (29%)
  Pallas kernels  14.3 us (28%)
    ppermute x17, starting transfers between devices, xor_exchange(): lax.ppermute(value, axis, [(i, i ^ mask) for i in range(lax.axis_size(axi...  17.1 us
    pallas_call x12, Pallas kernels, call(): pl.pallas_call(lambda *refs: body(*refs[waits:]), out_shape=[jax.ShapeDty...  12.1 us
    ppermute x17, waiting for transfers between devices, xor_exchange(): lax.ppermute(value, axis, [(i, i ^ mask) for i in range(lax.axis_size(axi...  11.8 us
    ppermute x1, waiting for transfers between devices, on_device(): halo_far = lax.ppermute(halo_beside, 'leaf', ahead + behind)  2.97 us
    ppermute x1, starting transfers between devices, on_device(): halo_far = lax.ppermute(halo_beside, 'leaf', ahead + behind)  2.9 us
    pallas_call x1, Pallas kernels, on_device(): pl.pallas_call(prepare_kernel, out_shape=[jax.ShapeDtypeStruct(shape, dty...  2.22 us
    ppermute x1, starting transfers between devices, on_device(): packs += [lax.ppermute(pack, 'group', order) for pack in own_group]  1.5 us
  transfers between devices with their start and end apart: 19, of which 8 were waited for; matrix products, arithmetic and copies ran while one was open for 0% of the time, Pallas kernels for 21%

profile of v3, /device:TPU:0, one launch (start us, length us, event | category | flops | bytes accessed | tf_op | source)
XLA Modules:
  0.0 50.7 jit_solution(5657071238358379841)
XLA Ops:
  0.0 2.2 %shard_map.73 = (bf16[1568,128]{1,0:T(8,128)(2,1)S(1)}, bf16[400,128]{1,0:T(8,128)(2,1)S(1)}, f32[400,128]{1,0:T(8,128)S(1)}, bf16[400,128]{1,0:T(8,128)(2,1)S(1)}, s32[1,5]{1,0:T(1,128)S(1)}) custom-call(bf16[64,1024]{1,0:T(8,128)(2,1)} %bitcast.1, bf16[1024,128]{1,0:T(8,128)(2,1)} %weights_hbm.1, bf16[1024,256]{1,0:T(8,128)(2,1)} %refs_1_.1, ...), custom_call_target="tpu_custom_call" | custom-call | flops 1000000 | tf_op jit(solution)/shard_map/pallas_call | solution.py:364
  2.2 0.5 %collective-permute-start.1 = (bf16[1568,128]{1,0:T(8,128)(2,1)S(1)}, bf16[1568,128]{1,0:T(8,128)(2,1)S(1)}, u32[]{:S(2)}, u32[]{:S(2)}) collective-permute-start(bf16[1568,128]{1,0:T(8,128)(2,1)S(1)} %get-tuple-element.26.refs_2_), channel_id=1, source_target_pairs={{0,1},{1,0},{2,3},{3,2},{4,5},{5,4},{6,7},{7,6},{8,9},{9,8},{10,11... | collective-permute-start | bytes 1204232 | tf_op jit(solution)/shard_map/ppermute | solution.py:73
  2.7 0.1 collective-permute-start
  2.8 2.9 %collective-permute-start.2 = (bf16[1568,128]{1,0:T(8,128)(2,1)S(1)}, bf16[1568,128]{1,0:T(8,128)(2,1)S(1)}, u32[]{:S(2)}, u32[]{:S(2)}) collective-permute-start(bf16[1568,128]{1,0:T(8,128)(2,1)S(1)} %get-tuple-element.26.refs_2_), channel_id=1, source_target_pairs={{0,2},{1,3},{2,0},{3,1},{4,6},{5,7},{6,4},{7,5},{8,10},{9,11},{10,... | collective-permute-start | bytes 1204232 | tf_op jit(solution)/shard_map/ppermute | solution.py:73
  5.8 0.0 collective-permute-done.refs_1_
  5.8 2.7 %collective-permute-start.3 = (bf16[400,128]{1,0:T(8,128)(2,1)S(1)}, bf16[400,128]{1,0:T(8,128)(2,1)S(1)}, u32[]{:S(2)}, u32[]{:S(2)}) collective-permute-start(bf16[400,128]{1,0:T(8,128)(2,1)S(1)} %get-tuple-element.24.refs_0_), channel_id=1, source_target_pairs={{0,8},{1,9},{2,10},{3,11},{4,12},{5,13},{6,14},{7,15},{8,0},{9,1},... | collective-permute-start | bytes 307208 | tf_op jit(solution)/shard_map/ppermute | solution.py:73
  8.5 1.7 %shard_map.75 = (bf16[1024,128]{1,0:T(8,128)(2,1)S(1)}, bf16[1024,128]{1,0:T(8,128)(2,1)S(1)}, bf16[1024,128]{1,0:T(8,128)(2,1)S(1)}, f32[1024,128]{1,0:T(8,128)S(1)}) custom-call(bf16[400,128]{1,0:T(8,128)(2,1)S(1)} %get-tuple-element.24.refs_0_, s32[1,5]{1,0:T(1,128)S(1)} %get-tuple-element.25.refs_1_.refs_3_.refs_2_, ...), custom_call_target="tpu_custom_call" | custom-call | flops 2000000000 | tf_op jit(solution)/shard_map/pallas_call | solution.py:40
  10.2 0.0 collective-permute-done.1.refs_2_
  10.2 1.7 %shard_map.76.refs_0_ = f32[1024,128]{1,0:T(8,128)S(1)} custom-call(f32[1024,128]{1,0:T(8,128)S(1)} %get-tuple-element.27.refs_0_, s32[1,5]{1,0:T(1,128)S(1)} %get-tuple-element.25.refs_1_.refs_3_.refs_2_, bf16[1568,128]{1,0:T(8,128)(2,1)S(1)} %collective-permute-done.1.refs_2_, ...), custom_call_target="tpu_custom_call", output_to_operand_aliasing={{}: (0, {})} | custom-call | flops 2000000000 | tf_op jit(solution)/shard_map/pallas_call | solution.py:40
  11.9 1.8 %collective-permute-done.3.refs_2_ = bf16[400,128]{1,0:T(8,128)(2,1)S(1)} collective-permute-done((bf16[400,128]{1,0:T(8,128)(2,1)S(1)}, bf16[400,128]{1,0:T(8,128)(2,1)S(1)}, u32[]{:S(2)}, u32[]{:S(2)}) %collective-permute-start.3) | collective-permute-done | bytes 102432 | tf_op jit(solution)/shard_map/ppermute | solution.py:73
  13.7 0.1 shard_map.77
  13.8 1.5 %collective-permute-done.2.refs_0_ = bf16[1568,128]{1,0:T(8,128)(2,1)S(1)} collective-permute-done((bf16[1568,128]{1,0:T(8,128)(2,1)S(1)}, bf16[1568,128]{1,0:T(8,128)(2,1)S(1)}, u32[]{:S(2)}, u32[]{:S(2)}) %collective-permute-start.2) | collective-permute-done | bytes 401440 | tf_op jit(solution)/shard_map/ppermute | solution.py:73
  15.3 0.0 collective-permute-start.5
  15.3 2.8 %collective-permute-start.11 = (bf16[400,128]{1,0:T(8,128)(2,1)S(1)}, bf16[400,128]{1,0:T(8,128)(2,1)S(1)}, u32[]{:S(2)}, u32[]{:S(2)}) collective-permute-start(bf16[400,128]{1,0:T(8,128)(2,1)S(1)} %get-tuple-element.32.refs_4_.refs_3_.refs_2_), channel_id=1, source_target_pairs={{0,8},{1,9},{2,10},{3,11},{4,12},{5,13},{6,14},{7,15},{8,0},{9,1},... | collective-permute-start | bytes 307208 | tf_op jit(solution)/shard_map/ppermute | solution.py:73
  18.1 1.5 %collective-permute-start.9 = (bf16[400,128]{1,0:T(8,128)(2,1)S(1)}, bf16[400,128]{1,0:T(8,128)(2,1)S(1)}, u32[]{:S(2)}, u32[]{:S(2)}) collective-permute-start(bf16[400,128]{1,0:T(8,128)(2,1)S(1)} %get-tuple-element.32.refs_4_.refs_3_.refs_2_), channel_id=1, source_target_pairs={{0,2},{1,3},{2,0},{3,1},{4,6},{5,7},{6,4},{7,5},{8,10},{9,11},{10,... | collective-permute-start | bytes 307208 | tf_op jit(solution)/shard_map/ppermute | solution.py:73
  19.6 4.2 %collective-permute-done.11.refs_7_ = bf16[400,128]{1,0:T(8,128)(2,1)S(1)} collective-permute-done((bf16[400,128]{1,0:T(8,128)(2,1)S(1)}, bf16[400,128]{1,0:T(8,128)(2,1)S(1)}, u32[]{:S(2)}, u32[]{:S(2)}) %collective-permute-start.11) | collective-permute-done | bytes 102432 | tf_op jit(solution)/shard_map/ppermute | solution.py:73
  23.9 1.6 %collective-permute-start.13 = (bf16[400,128]{1,0:T(8,128)(2,1)S(1)}, bf16[400,128]{1,0:T(8,128)(2,1)S(1)}, u32[]{:S(2)}, u32[]{:S(2)}) collective-permute-start(bf16[400,128]{1,0:T(8,128)(2,1)S(1)} %collective-permute-done.11.refs_7_), channel_id=1, source_target_pairs={{0,2},{1,3},{2,0},{3,1},{4,6},{5,7},{6,4},{7,5},{8,10},{9,11},{10,... | collective-permute-start | bytes 307208 | tf_op jit(solution)/shard_map/ppermute | solution.py:73
  25.4 0.7 %collective-permute-start.4 = (bf16[560,128]{1,0:T(8,128)(2,1)S(1)}, bf16[560,128]{1,0:T(8,128)(2,1)S(1)}, u32[]{:S(2)}, u32[]{:S(2)}) collective-permute-start(bf16[560,128]{1,0:T(8,128)(2,1)S(1)} %get-tuple-element.33.refs_1_), channel_id=1, source_target_pairs={{0,4},{1,5},{2,6},{3,7},{4,0},{5,1},{6,2},{7,3},{8,12},{9,13},{10,... | collective-permute-start | bytes 430088 | tf_op jit(solution)/shard_map/ppermute | solution.py:73
  26.1 1.7 %shard_map.79.refs_0_.refs_1_ = f32[1024,128]{1,0:T(8,128)S(1)} custom-call(f32[1024,128]{1,0:T(8,128)S(1)} %shard_map.76.refs_0_, s32[1,5]{1,0:T(1,128)S(1)} %get-tuple-element.25.refs_1_.refs_3_.refs_2_, bf16[1568,128]{1,0:T(8,128)(2,1)S(1)} %shard_map.78.refs_2_, ...), custom_call_target="tpu_custom_call", output_to_operand_aliasing={{}: (0, {})} | custom-call | flops 2000000000 | tf_op jit(solution)/shard_map/pallas_call | solution.py:40
  27.8 2.7 %collective-permute-done.4.refs_2_ = bf16[560,128]{1,0:T(8,128)(2,1)S(1)} collective-permute-done((bf16[560,128]{1,0:T(8,128)(2,1)S(1)}, bf16[560,128]{1,0:T(8,128)(2,1)S(1)}, u32[]{:S(2)}, u32[]{:S(2)}) %collective-permute-start.4) | collective-permute-done | bytes 143392 | tf_op jit(solution)/shard_map/ppermute | solution.py:73
  30.6 0.6 %collective-permute-start.7 = (bf16[400,128]{1,0:T(8,128)(2,1)S(1)}, bf16[400,128]{1,0:T(8,128)(2,1)S(1)}, u32[]{:S(2)}, u32[]{:S(2)}) collective-permute-start(bf16[400,128]{1,0:T(8,128)(2,1)S(1)} %get-tuple-element.35.refs_0_), channel_id=1, source_target_pairs={{0,2},{1,3},{2,0},{3,1},{4,6},{5,7},{6,4},{7,5},{8,10},{9,11},{10,... | collective-permute-start | bytes 307208 | tf_op jit(solution)/shard_map/ppermute | solution.py:73
  31.2 2.9 %collective-permute-start.6 = (bf16[1568,128]{1,0:T(8,128)(2,1)S(1)}, bf16[1568,128]{1,0:T(8,128)(2,1)S(1)}, u32[]{:S(2)}, u32[]{:S(2)}) collective-permute-start(bf16[1568,128]{1,0:T(8,128)(2,1)S(1)} %shard_map.78.refs_2_), channel_id=1, source_target_pairs={{0,4},{1,5},{4,8},{5,9},{8,12},{9,13},{6,2},{7,3},{10,6},{11,7},{1... | collective-permute-start | bytes 1204232 | tf_op jit(solution)/shard_map/ppermute | solution.py:435
  34.1 0.0 collective-permute-done.9.refs_5_
  34.1 0.1 collective-permute-start.8
  34.2 0.0 collective-permute-done.13.refs_9_
  34.2 0.5 collective-permute-start.12
  34.7 0.6 %collective-permute-done.7.refs_2_ = bf16[400,128]{1,0:T(8,128)(2,1)S(1)} collective-permute-done((bf16[400,128]{1,0:T(8,128)(2,1)S(1)}, bf16[400,128]{1,0:T(8,128)(2,1)S(1)}, u32[]{:S(2)}, u32[]{:S(2)}) %collective-permute-start.7) | collective-permute-done | bytes 102432 | tf_op jit(solution)/shard_map/ppermute | solution.py:73
  35.3 0.0 collective-permute-start.10
  35.3 0.0 collective-permute-done.5.refs_3_
  35.3 0.5 %collective-permute-start.14 = (bf16[400,128]{1,0:T(8,128)(2,1)S(1)}, bf16[400,128]{1,0:T(8,128)(2,1)S(1)}, u32[]{:S(2)}, u32[]{:S(2)}) collective-permute-start(bf16[400,128]{1,0:T(8,128)(2,1)S(1)} %collective-permute-done.13.refs_9_), channel_id=1, source_target_pairs={{0,1},{1,0},{2,3},{3,2},{4,5},{5,4},{6,7},{7,6},{8,9},{9,8},{10,11... | collective-permute-start | bytes 307208 | tf_op jit(solution)/shard_map/ppermute | solution.py:73
  35.8 0.0 collective-permute-done.8.refs_4_
  35.9 0.0 collective-permute-done.12.refs_8_
  35.9 0.7 %collective-permute-done.10.refs_6_ = bf16[400,128]{1,0:T(8,128)(2,1)S(1)} collective-permute-done((bf16[400,128]{1,0:T(8,128)(2,1)S(1)}, bf16[400,128]{1,0:T(8,128)(2,1)S(1)}, u32[]{:S(2)}, u32[]{:S(2)}) %collective-permute-start.10) | collective-permute-done | bytes 102432 | tf_op jit(solution)/shard_map/ppermute | solution.py:73
  36.6 0.2 collective-permute-done.14.refs_10_
  36.8 1.6 %shard_map.83 = (f32[256,128]{1,0:T(8,128)S(1)}, bf16[256,128]{1,0:T(8,128)(2,1)S(1)}) custom-call(bf16[400,128]{1,0:T(8,128)(2,1)S(1)} %shard_map.82.refs_0_, s32[1,5]{1,0:T(1,128)S(1)} %get-tuple-element.25.refs_1_.refs_3_.refs_2_, bf16[560,128]{1,0:T(8,128)(2,1)S(1)} %collective-permute-done.4.refs_2_, ...), custom_call_target="tpu_custom_call" | custom-call | flops 2000000000 | tf_op jit(solution)/shard_map/pallas_call | solution.py:40
  38.4 3.0 %collective-permute-done.6.refs_0_ = bf16[1568,128]{1,0:T(8,128)(2,1)S(1)} collective-permute-done((bf16[1568,128]{1,0:T(8,128)(2,1)S(1)}, bf16[1568,128]{1,0:T(8,128)(2,1)S(1)}, u32[]{:S(2)}, u32[]{:S(2)}) %collective-permute-start.6) | collective-permute-done | bytes 401440 | tf_op jit(solution)/shard_map/ppermute | solution.py:435
  41.4 0.0 collective-permute-start.15
  41.4 1.5 %collective-permute-start.17 = (bf16[400,128]{1,0:T(8,128)(2,1)S(1)}, bf16[400,128]{1,0:T(8,128)(2,1)S(1)}, u32[]{:S(2)}, u32[]{:S(2)}) collective-permute-start(bf16[400,128]{1,0:T(8,128)(2,1)S(1)} %shard_map.82.refs_0_), channel_id=1, source_target_pairs={{0,16},{16,0},{1,17},{17,1},{2,18},{18,2},{3,19},{19,3},{4,20},{20... | collective-permute-start | bytes 307208 | tf_op jit(solution)/shard_map/ppermute | solution.py:452
  42.9 2.6 %collective-permute-start.16 = (bf16[256,128]{1,0:T(8,128)(2,1)S(1)}, bf16[256,128]{1,0:T(8,128)(2,1)S(1)}, u32[]{:S(2)}, u32[]{:S(2)}) collective-permute-start(bf16[256,128]{1,0:T(8,128)(2,1)S(1)} %get-tuple-element.38), channel_id=1, source_target_pairs={{0,4},{1,5},{2,6},{3,7},{4,0},{5,1},{6,2},{7,3},{8,12},{9,13},{10,... | collective-permute-start | bytes 196616 | tf_op jit(solution)/shard_map/ppermute | solution.py:73
  45.4 1.7 %shard_map.85.refs_0_ = f32[1024,128]{1,0:T(8,128)S(1)} custom-call(f32[1024,128]{1,0:T(8,128)S(1)} %shard_map.81.refs_0_, s32[1,5]{1,0:T(1,128)S(1)} %get-tuple-element.25.refs_1_.refs_3_.refs_2_, bf16[1568,128]{1,0:T(8,128)(2,1)S(1)} %shard_map.84.refs_2_, bf16[1024,128]{1,0:T(8,128)(2,1)S(1)} %get-tuple-element.28.refs_3_.refs_4_, ...), custom_call_target="tpu_custom_call", output_to_operand_aliasing={{}: (0, {})} | custom-call | flops 2000000000 | tf_op jit(solution)/shard_map/pallas_call | solution.py:40
  47.1 0.0 copy-start
  47.1 0.0 collective-permute-done.17.refs_5_
  47.2 0.1 collective-permute-start.18
  47.2 0.0 collective-permute-done.15.refs_2_
  47.2 1.7 %shard_map.86.refs_0_ = f32[1024,128]{1,0:T(8,128)S(1)} custom-call(f32[1024,128]{1,0:T(8,128)S(1)} %shard_map.85.refs_0_, s32[1,5]{1,0:T(1,128)S(1)} %get-tuple-element.25.refs_1_.refs_3_.refs_2_, bf16[1568,128]{1,0:T(8,128)(2,1)S(1)} %collective-permute-done.15.refs_2_, ...), custom_call_target="tpu_custom_call", output_to_operand_aliasing={{}: (0, {})} | custom-call | flops 2000000000 | tf_op jit(solution)/shard_map/pallas_call | solution.py:40
  49.0 0.0 collective-permute-done.16.refs_4_
  49.0 0.0 collective-permute-done.18.refs_6_
  49.0 1.7 %shard_map.87 = bf16[1024,128]{1,0:T(8,128)(2,1)} custom-call(f32[1024,128]{1,0:T(8,128)S(1)} %shard_map.86.refs_0_, bf16[1024,256]{1,0:T(8,128)(2,1)S(1)} %copy-done, bf16[400,128]{1,0:T(8,128)(2,1)S(1)} %get-tuple-element.32.refs_4_.refs_3_.refs_2_, f32[256,128]{1,0:T(8,128)S(1)} %get-tuple-element.37.refs_1_.refs_3_, ...), custom_call_target="tpu_custom_call" | custom-call | flops 2000000000 | tf_op jit(solution)/shard_map/pallas_call | solution.py:40
  (7 shorter events, 0.1 us)
Async XLA Ops:
  2.2 7.9 %collective-permute-start.1 = (bf16[1568,128]{1,0:T(8,128)(2,1)S(1)}, bf16[1568,128]{1,0:T(8,128)(2,1)S(1)}, u32[]{:S(2)}, u32[]{:S(2)}) collective-permute-start(bf16[1568,128]{1,0:T(8,128)(2,1)S(1)} %get-tuple-element.26.refs_2_), channel_id=1, source_target_pairs={{0,1},{1,0},{2,3},{3,2},{4,5},{5,4},{6,7},{7,6},{8,9},{9,8},{10,11... | collective-permute-start | bytes 1204232 | tf_op jit(solution)/shard_map/ppermute | solution.py:73
  2.7 3.0 %collective-permute-start = (bf16[400,128]{1,0:T(8,128)(2,1)S(1)}, bf16[400,128]{1,0:T(8,128)(2,1)S(1)}, u32[]{:S(2)}, u32[]{:S(2)}) collective-permute-start(bf16[400,128]{1,0:T(8,128)(2,1)S(1)} %get-tuple-element.23), channel_id=1, source_target_pairs={{0,1},{1,0},{2,3},{3,2},{4,5},{5,4},{6,7},{7,6},{8,9},{9,8},{10,11... | collective-permute-start | bytes 307208 | tf_op jit(solution)/shard_map/ppermute | solution.py:73
  2.8 12.5 %collective-permute-start.2 = (bf16[1568,128]{1,0:T(8,128)(2,1)S(1)}, bf16[1568,128]{1,0:T(8,128)(2,1)S(1)}, u32[]{:S(2)}, u32[]{:S(2)}) collective-permute-start(bf16[1568,128]{1,0:T(8,128)(2,1)S(1)} %get-tuple-element.26.refs_2_), channel_id=1, source_target_pairs={{0,2},{1,3},{2,0},{3,1},{4,6},{5,7},{6,4},{7,5},{8,10},{9,11},{10,... | collective-permute-start | bytes 1204232 | tf_op jit(solution)/shard_map/ppermute | solution.py:73
  5.8 7.9 %collective-permute-start.3 = (bf16[400,128]{1,0:T(8,128)(2,1)S(1)}, bf16[400,128]{1,0:T(8,128)(2,1)S(1)}, u32[]{:S(2)}, u32[]{:S(2)}) collective-permute-start(bf16[400,128]{1,0:T(8,128)(2,1)S(1)} %get-tuple-element.24.refs_0_), channel_id=1, source_target_pairs={{0,8},{1,9},{2,10},{3,11},{4,12},{5,13},{6,14},{7,15},{8,0},{9,1},... | collective-permute-start | bytes 307208 | tf_op jit(solution)/shard_map/ppermute | solution.py:73
  15.3 20.0 %collective-permute-start.5 = (bf16[1568,128]{1,0:T(8,128)(2,1)S(1)}, bf16[1568,128]{1,0:T(8,128)(2,1)S(1)}, u32[]{:S(2)}, u32[]{:S(2)}) collective-permute-start(bf16[1568,128]{1,0:T(8,128)(2,1)S(1)} %shard_map.78.refs_2_), channel_id=1, source_target_pairs={{0,1},{1,0},{2,3},{3,2},{4,5},{5,4},{6,7},{7,6},{8,9},{9,8},{10,11... | collective-permute-start | bytes 1204232 | tf_op jit(solution)/shard_map/ppermute | solution.py:73
  15.3 8.6 %collective-permute-start.11 = (bf16[400,128]{1,0:T(8,128)(2,1)S(1)}, bf16[400,128]{1,0:T(8,128)(2,1)S(1)}, u32[]{:S(2)}, u32[]{:S(2)}) collective-permute-start(bf16[400,128]{1,0:T(8,128)(2,1)S(1)} %get-tuple-element.32.refs_4_.refs_3_.refs_2_), channel_id=1, source_target_pairs={{0,8},{1,9},{2,10},{3,11},{4,12},{5,13},{6,14},{7,15},{8,0},{9,1},... | collective-permute-start | bytes 307208 | tf_op jit(solution)/shard_map/ppermute | solution.py:73
  18.1 16.0 %collective-permute-start.9 = (bf16[400,128]{1,0:T(8,128)(2,1)S(1)}, bf16[400,128]{1,0:T(8,128)(2,1)S(1)}, u32[]{:S(2)}, u32[]{:S(2)}) collective-permute-start(bf16[400,128]{1,0:T(8,128)(2,1)S(1)} %get-tuple-element.32.refs_4_.refs_3_.refs_2_), channel_id=1, source_target_pairs={{0,2},{1,3},{2,0},{3,1},{4,6},{5,7},{6,4},{7,5},{8,10},{9,11},{10,... | collective-permute-start | bytes 307208 | tf_op jit(solution)/shard_map/ppermute | solution.py:73
  23.9 10.3 %collective-permute-start.13 = (bf16[400,128]{1,0:T(8,128)(2,1)S(1)}, bf16[400,128]{1,0:T(8,128)(2,1)S(1)}, u32[]{:S(2)}, u32[]{:S(2)}) collective-permute-start(bf16[400,128]{1,0:T(8,128)(2,1)S(1)} %collective-permute-done.11.refs_7_), channel_id=1, source_target_pairs={{0,2},{1,3},{2,0},{3,1},{4,6},{5,7},{6,4},{7,5},{8,10},{9,11},{10,... | collective-permute-start | bytes 307208 | tf_op jit(solution)/shard_map/ppermute | solution.py:73
  25.4 5.1 %collective-permute-start.4 = (bf16[560,128]{1,0:T(8,128)(2,1)S(1)}, bf16[560,128]{1,0:T(8,128)(2,1)S(1)}, u32[]{:S(2)}, u32[]{:S(2)}) collective-permute-start(bf16[560,128]{1,0:T(8,128)(2,1)S(1)} %get-tuple-element.33.refs_1_), channel_id=1, source_target_pairs={{0,4},{1,5},{2,6},{3,7},{4,0},{5,1},{6,2},{7,3},{8,12},{9,13},{10,... | collective-permute-start | bytes 430088 | tf_op jit(solution)/shard_map/ppermute | solution.py:73
  30.6 4.7 %collective-permute-start.7 = (bf16[400,128]{1,0:T(8,128)(2,1)S(1)}, bf16[400,128]{1,0:T(8,128)(2,1)S(1)}, u32[]{:S(2)}, u32[]{:S(2)}) collective-permute-start(bf16[400,128]{1,0:T(8,128)(2,1)S(1)} %get-tuple-element.35.refs_0_), channel_id=1, source_target_pairs={{0,2},{1,3},{2,0},{3,1},{4,6},{5,7},{6,4},{7,5},{8,10},{9,11},{10,... | collective-permute-start | bytes 307208 | tf_op jit(solution)/shard_map/ppermute | solution.py:73
  31.2 10.2 %collective-permute-start.6 = (bf16[1568,128]{1,0:T(8,128)(2,1)S(1)}, bf16[1568,128]{1,0:T(8,128)(2,1)S(1)}, u32[]{:S(2)}, u32[]{:S(2)}) collective-permute-start(bf16[1568,128]{1,0:T(8,128)(2,1)S(1)} %shard_map.78.refs_2_), channel_id=1, source_target_pairs={{0,4},{1,5},{4,8},{5,9},{8,12},{9,13},{6,2},{7,3},{10,6},{11,7},{1... | collective-permute-start | bytes 1204232 | tf_op jit(solution)/shard_map/ppermute | solution.py:435
  34.1 1.7 %collective-permute-start.8 = (bf16[400,128]{1,0:T(8,128)(2,1)S(1)}, bf16[400,128]{1,0:T(8,128)(2,1)S(1)}, u32[]{:S(2)}, u32[]{:S(2)}) collective-permute-start(bf16[400,128]{1,0:T(8,128)(2,1)S(1)} %get-tuple-element.32.refs_4_.refs_3_.refs_2_), channel_id=1, source_target_pairs={{0,1},{1,0},{2,3},{3,2},{4,5},{5,4},{6,7},{7,6},{8,9},{9,8},{10,11... | collective-permute-start | bytes 307208 | tf_op jit(solution)/shard_map/ppermute | solution.py:73
  34.2 1.7 %collective-permute-start.12 = (bf16[400,128]{1,0:T(8,128)(2,1)S(1)}, bf16[400,128]{1,0:T(8,128)(2,1)S(1)}, u32[]{:S(2)}, u32[]{:S(2)}) collective-permute-start(bf16[400,128]{1,0:T(8,128)(2,1)S(1)} %collective-permute-done.11.refs_7_), channel_id=1, source_target_pairs={{0,1},{1,0},{2,3},{3,2},{4,5},{5,4},{6,7},{7,6},{8,9},{9,8},{10,11... | collective-permute-start | bytes 307208 | tf_op jit(solution)/shard_map/ppermute | solution.py:73
  35.3 1.3 %collective-permute-start.10 = (bf16[400,128]{1,0:T(8,128)(2,1)S(1)}, bf16[400,128]{1,0:T(8,128)(2,1)S(1)}, u32[]{:S(2)}, u32[]{:S(2)}) collective-permute-start(bf16[400,128]{1,0:T(8,128)(2,1)S(1)} %collective-permute-done.9.refs_5_), channel_id=1, source_target_pairs={{0,1},{1,0},{2,3},{3,2},{4,5},{5,4},{6,7},{7,6},{8,9},{9,8},{10,11... | collective-permute-start | bytes 307208 | tf_op jit(solution)/shard_map/ppermute | solution.py:73
  35.3 1.5 %collective-permute-start.14 = (bf16[400,128]{1,0:T(8,128)(2,1)S(1)}, bf16[400,128]{1,0:T(8,128)(2,1)S(1)}, u32[]{:S(2)}, u32[]{:S(2)}) collective-permute-start(bf16[400,128]{1,0:T(8,128)(2,1)S(1)} %collective-permute-done.13.refs_9_), channel_id=1, source_target_pairs={{0,1},{1,0},{2,3},{3,2},{4,5},{5,4},{6,7},{7,6},{8,9},{9,8},{10,11... | collective-permute-start | bytes 307208 | tf_op jit(solution)/shard_map/ppermute | solution.py:73
  41.4 5.9 %collective-permute-start.15 = (bf16[1568,128]{1,0:T(8,128)(2,1)S(1)}, bf16[1568,128]{1,0:T(8,128)(2,1)S(1)}, u32[]{:S(2)}, u32[]{:S(2)}) collective-permute-start(bf16[1568,128]{1,0:T(8,128)(2,1)S(1)} %shard_map.84.refs_2_), channel_id=1, source_target_pairs={{0,1},{1,0},{2,3},{3,2},{4,5},{5,4},{6,7},{7,6},{8,9},{9,8},{10,11... | collective-permute-start | bytes 1204232 | tf_op jit(solution)/shard_map/ppermute | solution.py:73
  41.4 5.8 %collective-permute-start.17 = (bf16[400,128]{1,0:T(8,128)(2,1)S(1)}, bf16[400,128]{1,0:T(8,128)(2,1)S(1)}, u32[]{:S(2)}, u32[]{:S(2)}) collective-permute-start(bf16[400,128]{1,0:T(8,128)(2,1)S(1)} %shard_map.82.refs_0_), channel_id=1, source_target_pairs={{0,16},{16,0},{1,17},{17,1},{2,18},{18,2},{3,19},{19,3},{4,20},{20... | collective-permute-start | bytes 307208 | tf_op jit(solution)/shard_map/ppermute | solution.py:452
  42.9 6.1 %collective-permute-start.16 = (bf16[256,128]{1,0:T(8,128)(2,1)S(1)}, bf16[256,128]{1,0:T(8,128)(2,1)S(1)}, u32[]{:S(2)}, u32[]{:S(2)}) collective-permute-start(bf16[256,128]{1,0:T(8,128)(2,1)S(1)} %get-tuple-element.38), channel_id=1, source_target_pairs={{0,4},{1,5},{2,6},{3,7},{4,0},{5,1},{6,2},{7,3},{8,12},{9,13},{10,... | collective-permute-start | bytes 196616 | tf_op jit(solution)/shard_map/ppermute | solution.py:73
  47.1 1.9 %copy-start = (bf16[1024,256]{1,0:T(8,128)(2,1)S(1)}, bf16[1024,256]{1,0:T(8,128)(2,1)}, u32[]{:S(2)}) copy-start(bf16[1024,256]{1,0:T(8,128)(2,1)} %refs_1_.1) | copy-start | bytes 1572868
  47.2 1.9 %collective-permute-start.18 = (bf16[400,128]{1,0:T(8,128)(2,1)S(1)}, bf16[400,128]{1,0:T(8,128)(2,1)S(1)}, u32[]{:S(2)}, u32[]{:S(2)}) collective-permute-start(bf16[400,128]{1,0:T(8,128)(2,1)S(1)} %collective-permute-done.17.refs_5_), channel_id=1, source_target_pairs={{0,1},{1,0},{2,3},{3,2},{4,5},{5,4},{6,7},{7,6},{8,9},{9,8},{10,11... | collective-permute-start | bytes 307208 | tf_op jit(solution)/shard_map/ppermute | solution.py:73

commit v4 on v3

--- a/solution.py
+++ b/solution.py
@@ -14,21 +14,28 @@
 LANES = 128
 TARGET_ROWS = 512
 SOURCE_ROWS = 512
-WORK = {
-    "prepare": 10**6,
-    "first_add": 10**6,
-    "near_self": 2 * 10**9,
-    "near_core": 2 * 10**9,
-    "add_a": 10**6,
-    "near_beside": 2 * 10**9,
-    "add_b": 10**6,
-    "near_across": 2 * 10**9,
-    "add_c": 10**6,
-    "sibling": 2 * 10**9,
-    "near_far": 2 * 10**9,
-    "near_last": 2 * 10**9,
-    "final": 2 * 10**9,
+ORDER = {
+    "first_add": 1000000,
+    "near_self": 2000000000,
+    "near_core": 2000000000,
+    "near_beside": 2000000000,
+    "add_a": 1000000,
+    "add_b": 1000000,
+    "sibling": 2000000000,
+    "near_across": 2000000000,
+    "add_c": 1000000,
+    "field": 1000000,
+    "near_far": 2000000000,
+    "near_last": 2000000000,
+    "final": 2000000000,
 }
+DEADLINES = {
+    "add_a": ["sv_8"],
+    "sibling": ["sv_10"],
+    "near_far": ["packs"],
+    "near_last": ["packs_core"],
+}
+RELEASES = {"sv_0": "first_add", "halo_next": "add_a", "halo_far": "add_c"}
 
 
 def vmem():
@@ -142,6 +149,15 @@
     lane = lax.broadcasted_iota(jnp.int32, (1, columns), 1)
     here = lane == distance + (columns - 1) // 2
     return jnp.sum(jnp.where(here, flags_ref[...], 0).astype(F32), axis=1, keepdims=True)
+
+
+def flag_row(flags_ref):
+    columns = flags_ref.shape[1]
+    lane = lax.broadcasted_iota(jnp.int32, (1, LANES), 1)
+    row = jnp.zeros((1, LANES), F32)
+    for column in range(columns):
+        row = jnp.where(lane == column, flag_of(flags_ref, column - (columns - 1) // 2), row)
+    return row
 
 
 def prepare_kernel(
@@ -208,27 +224,26 @@
     send_ref[...] = all_ref[pl.ds((1 - core) * rows, rows), :].astype(BF16)
     sk_half, sk_norms = skeletons // 2, norm_rows(skeletons)
     sv_ref[:sk_half, :] = packed(skeleton).astype(BF16)
-    sv_ref[sk_half : sk_half + sk_norms, :] = norm_block(norms(skeleton)).astype(BF16)
+    copies[6].wait()
+    block = norm_block(norms(skeleton))
+    row = lax.broadcasted_iota(jnp.int32, block.shape, 0)
+    block = jnp.where(row == sk_norms - 1, flag_row(flags_ref), block)
+    sv_ref[sk_half : sk_half + sk_norms, :] = block.astype(BF16)
     sv_ref[sk_half + sk_norms :, :] = charges_turned.astype(F32).T.astype(BF16)
     wide = points_ref[...].astype(F32)
     halo_ref[:half, :] = packed(wide).astype(BF16)
     halo_ref[half + points :, :] = norm_block(norms(wide)).astype(BF16)
-    copies[6].wait()
 
 
 def add_kernel(with_skeleton, last, sum_ref, got_ref, *refs):
     rows = sum_ref.shape[0]
     total = sum_ref[...] + got_ref[:rows, :].astype(F32)
     if with_skeleton:
-        flags_ref, sv_ref, *refs = refs
+        own_ref, other_ref, *refs = refs
         send_ref = refs[0]
-        points = send_ref.shape[0] - 16 - rows
-        send_ref[rows : rows + points, :] = sv_ref[:points, :]
-        columns = flags_ref.shape[1]
-        row = lax.broadcasted_iota(jnp.int32, (columns, LANES), 0)
-        lane = lax.broadcasted_iota(jnp.int32, (columns, LANES), 1)
-        spread = dot_nn(flags_ref[...].astype(F32), (row == lane).astype(F32))
-        send_ref[rows + points :, :] = jnp.broadcast_to(spread, (16, LANES)).astype(BF16)
+        points = (send_ref.shape[0] - rows) // 2
+        send_ref[rows : rows + points, :] = own_ref[:points, :]
+        send_ref[rows + points :, :] = other_ref[:points, :]
     refs[0][:rows, :] = total.astype(BF16)
     if not last:
         refs[1][...] = total
@@ -240,14 +255,14 @@
     side, beside = 1 - 2 * core, 1 - 2 * chip
     first = stage == 0 and not across
     if first:
-        flags_ref, halo_ref, low_ref, high_ref, parts_ref, near_ref = refs
+        flags_ref, halo_ref, low_ref, high_ref, parts_ref, near_ref, mass_ref = refs
         half = near_ref.shape[0] // 2
         forms = target_forms(halo_ref[:half, :], features)
         for ref, form in zip((low_ref, high_ref, parts_ref), forms):
             ref[...] = form
         distance = 0
     else:
-        before_ref, flags_ref, halo_ref, low_ref, high_ref, parts_ref, near_ref = refs
+        before_ref, flags_ref, halo_ref, low_ref, high_ref, parts_ref, near_ref, mass_ref = refs
         half = near_ref.shape[0] // 2
         if across:
             distance = side if stage == 0 else -side
@@ -257,6 +272,7 @@
     def tile():
         flag = flag_of(flags_ref, distance)
         norms = source_norms(halo_ref[3 * half :, :], 2 * half)
+        mass_ref[...] = (halo_ref[half : 3 * half, :].astype(F32) * flag).astype(BF16)
         step = min(SOURCE_ROWS, half)
         for start in range(0, 2 * half, TARGET_ROWS):
             rows = slice(start, min(start + TARGET_ROWS, 2 * half))
@@ -266,10 +282,9 @@
                 for h, ref in enumerate((low_ref, high_ref)):
                     terms = norms[h][:, place : place + step]
                     values = kernel_values(ref[rows, :], parts_ref[rows, :], sources, terms, features)
-                    mass = halo_ref[(h + 1) * half + place : (h + 1) * half + place + step, :]
-                    term = dot_nn(values, mass)
+                    term = dot_nn(values, mass_ref[h * half + place : h * half + place + step, :])
                     total = term if total is None else total + term
-            near_ref[rows, :] = flag * total if first else before_ref[rows, :] + flag * total
+            near_ref[rows, :] = total if first else before_ref[rows, :] + total
 
     if across and stage > 0:
         pl.when(core != chip if stage == 1 else core == chip)(tile)
@@ -282,43 +297,50 @@
     return [range(i, min(i + step, count)) for i in range(0, count, step)]
 
 
-def sibling_kernel(masks, reduced, features, skeletons, flags_ref, got_ref, *refs):
-    pieces, (own_ref, send_ref) = refs[: len(masks)], refs[len(masks) :]
+def sibling_kernel(masks, reduced, features, skeletons, reach, partner_ref, core_ref, *refs):
+    pieces, (own_ref, other_ref, send_ref) = refs[: len(masks)], refs[len(masks) :]
     leaf = lax.axis_index("leaf")
-    reach = (flags_ref.shape[1] - 1) // 2
     half, points = skeletons // 2, skeletons // 2 + norm_rows(skeletons)
-    start = got_ref.shape[0] - 16 - points
-    other_flags = got_ref[start + points :, :].astype(F32)[:1, :]
-    lane = lax.broadcasted_iota(jnp.int32, other_flags.shape, 1)
-    forms = zip(
-        target_forms(pieces[0][:half, :], features),
-        target_forms(got_ref[start : start + half, :], features),
-    )
+    start = partner_ref.shape[0] - 2 * points
+    blocks = [
+        (0, pieces[0][:points, :]),
+        (reduced, partner_ref[start : start + points, :]),
+        (1, core_ref[:points, :]),
+        (reduced | 1, partner_ref[start + points :, :]),
+    ]
+    forms = zip(*[target_forms(block[:half], features) for _, block in blocks])
     low, high, parts = [jnp.concatenate(form, axis=0) for form in forms]
-    kept = []
-    for mask in masks:
-        source = leaf ^ mask
-        flagged = jnp.where(lane == source - (leaf ^ reduced) + reach, other_flags, 0.0)
-        other = 1.0 - jnp.sum(flagged, axis=1, keepdims=True)
-        kept.append((1.0 - flag_of(flags_ref, source - leaf), other))
-    own = send = None
+    lane = lax.broadcasted_iota(jnp.int32, (1, LANES), 1)
+    fields = [None] * len(blocks)
     for group in grouped(len(masks), half):
         sources = ones_beside(jnp.concatenate([pieces[i][:half, :] for i in group], axis=0))
         norms = [source_norms(pieces[i][half:points, :], skeletons) for i in group]
+        mass = [pieces[i][points:, :].astype(F32) for i in group]
+        masses = []
+        for target, block in blocks:
+            flags = block[points - 16 :].astype(F32)[15:16]
+            kept = []
+            for i in group:
+                distance = (leaf ^ masks[i]) - (leaf ^ target)
+                kept.append(1.0 - jnp.sum(jnp.where(lane == distance + reach, flags, 0.0), axis=1, keepdims=True))
+            masses.append([(m * k).astype(BF16) for m, k in zip(mass, kept)])
         for h, targets in enumerate((low, high)):
             terms = jnp.concatenate([n[h] for n in norms], axis=1)
             values = kernel_values(targets, parts, sources, terms, features)
-            mass = [pieces[i][points + h * half : points + (h + 1) * half, :].astype(F32) for i in group]
-            masses = [
-                jnp.concatenate([m * kept[i][k] for m, i in zip(mass, group)], axis=0).astype(BF16)
-                for k in range(2)
-            ]
-            to_own = dot_nn(values[:skeletons], masses[0])
-            to_other = dot_nn(values[skeletons:], masses[1])
-            own = to_own if own is None else own + to_own
-            send = to_other if send is None else send + to_other
-    own_ref[...] = own
-    send_ref[...] = send.astype(send_ref.dtype)
+            for k in range(len(blocks)):
+                both = jnp.concatenate([m[h * half : (h + 1) * half] for m in masses[k]], axis=0)
+                term = dot_nn(values[k * skeletons : (k + 1) * skeletons], both)
+                fields[k] = term if fields[k] is None else fields[k] + term
+    own_ref[...] = fields[0]
+    other_ref[...] = fields[1]
+    send_ref[:skeletons, :] = fields[2].astype(BF16)
+    send_ref[skeletons:, :] = fields[3].astype(BF16)
+
+
+def field_kernel(own_ref, other_ref, got_ref, field_ref, send_ref):
+    rows = own_ref.shape[0]
+    field_ref[...] = own_ref[...] + got_ref[:rows, :].astype(F32)
+    send_ref[...] = (other_ref[...] + got_ref[rows:, :].astype(F32)).astype(BF16)
 
 
 def final_kernel(count, features, near_ref, interp_ref, sv_ref, own_ref, got_ref, *refs):
@@ -369,111 +391,146 @@
         scratch_shapes=[pltpu.VMEM(shape, dtype) for shape, dtype in scratch]
         + [pltpu.SemaphoreType.DMA((len(arguments),))],
         compiler_params=pltpu.CompilerParams(vmem_limit_bytes=VMEM_BYTES),
-        cost_estimate=pl.CostEstimate(flops=WORK["prepare"], bytes_accessed=0, transcendentals=0),
+        cost_estimate=pl.CostEstimate(flops=10**6, bytes_accessed=0, transcendentals=0),
     )(*[pltpu.with_memory_space_constraint(x, pltpu.HBM) for x in arguments])
 
-    def add(name, total, got, mask, after=(), last=False):
-        with_skeleton = mask == reduced
-        rows = sum_rows + (sv_points + 16 if with_skeleton else 0)
-        outs = [((rows, columns), BF16)] + ([] if last else [((sum_rows, columns), F32)])
-        ins = [total, got] + ([flags, skeleton] if with_skeleton else [])
-        body = functools.partial(add_kernel, with_skeleton, last)
-        send, *total = call(body, outs, ins, after=after, work=WORK[name])
-        return send, total[0] if total else None
-
-    got = xor_exchange(cluster_send, "leaf", core_mask)
-    pieces = {0: skeleton}
-    pieces[chip_mask] = xor_exchange(skeleton, "leaf", chip_mask)
-    pieces[core_mask] = xor_exchange(skeleton, "leaf", core_mask)
-    halo_core = xor_exchange(halo, "leaf", core_mask)
-    halo_beside = xor_exchange(halo, "leaf", chip_mask)
+    have, done = {}, {}
     add_masks = [1 << i for i in reversed(range(1, members.bit_length() - 1))]
-    names = ["first_add", "add_a", "add_b", "add_c"]
-    cluster_send, cluster_sum = add(names[0], cluster_sum, got, add_masks[0])
-    got = xor_exchange(cluster_send, "leaf", add_masks[0])
-
+    adds = dict(zip(("first_add", "add_a", "add_b", "add_c"), add_masks + [0]))
     gather_masks = [1 << i for i in reversed(range(2, leaves.bit_length() - 1)) if 1 << i != reduced]
-    known = [0]
-    for mask in gather_masks:
-        for m in list(known):
-            pieces[m | mask] = xor_exchange(pieces[m], "leaf", mask)
-            known.append(m | mask)
-    for m in known[1:]:
-        pieces[m | chip_mask] = xor_exchange(pieces[m], "leaf", chip_mask)
-    for m in known:
-        for n in (m, m | chip_mask):
-            if n:
-                pieces[n | core_mask] = xor_exchange(pieces[n], "leaf", core_mask)
-
-    tile = ((leaf_points, columns), BF16)
-    *targets, near = call(
-        functools.partial(near_kernel, 0, False, features),
-        [tile, tile, tile, ((leaf_points, columns), F32)],
-        [flags, halo],
-        after=[cluster_send],
-        work=WORK["near_self"],
-    )
-
-    def near_step(name, near, stage, across, other, *after):
-        return call(
-            functools.partial(near_kernel, stage, across, features),
-            [((leaf_points, columns), F32)],
-            [near, flags, other, *targets],
-            after=after,
-            in_place=True,
-            work=WORK[name],
-        )[0]
-
-    near = near_step("near_core", near, 0, True, halo_core)
-
-    cluster_send, cluster_sum = add(names[1], cluster_sum, got, add_masks[1], [near])
-    partner = got = xor_exchange(cluster_send, "leaf", add_masks[1])
-
-    halo_beside = hand_on(halo_beside, cluster_send)
+    piece_masks = [m for m in range(leaves) if not m & (reduced | core_mask)]
+    reach = (near_flags.shape[1] - 1) // 2
     ahead = [(i, i + 4) for i in range(leaves - 4) if i & chip_mask == 0]
     behind = [(i, i - 4) for i in range(4, leaves) if i & chip_mask != 0]
-    halo_far = lax.ppermute(halo_beside, "leaf", ahead + behind)
-    halo_across = xor_exchange(halo_beside, "leaf", core_mask)
-    near = near_step("near_beside", near, 1, False, halo_beside)
-
-    cluster_send, cluster_sum = add(names[2], cluster_sum, got, add_masks[2], [near])
-    got = xor_exchange(cluster_send, "leaf", add_masks[2])
-    near = near_step("near_across", near, 1, True, halo_across, cluster_send)
-
-    cluster_send, _ = add(names[3], cluster_sum, got, 0, [near], True)
-    own_group = [cluster_send]
-    mask = members
-    while mask < leaves:
-        own_group += [xor_exchange(pack, "leaf", mask) for pack in own_group]
-        mask *= 2
-    packs = []
-    for shift in range(1, groups):
-        order = [(i, (i + shift) % groups) for i in range(groups)]
-        packs += [lax.ppermute(pack, "group", order) for pack in own_group]
-
-    masks = sorted(pieces)
-    field, field_send = call(
-        functools.partial(sibling_kernel, masks, reduced, features, skeletons),
-        [((skeletons, columns), F32), ((skeletons, columns), BF16)],
-        [flags, partner] + [pieces[m] for m in masks],
-        after=[cluster_send],
-        work=WORK["sibling"],
-    )
-    field_got = xor_exchange(field_send, "leaf", reduced)
-
-    halo_far = hand_on(halo_far, field)
-    halo_far_across = xor_exchange(halo_far, "leaf", core_mask)
-    near = near_step("near_far", near, 2, False, halo_far)
-    packs += [xor_exchange(pack, "leaf", core_mask) for pack in packs]
-    near = near_step("near_last", near, 2, True, halo_far_across)
-
-    (potential,) = call(
-        functools.partial(final_kernel, len(packs), features),
-        [((leaf_points, columns), BF16)],
-        [near, interp, skeleton, field, field_got] + packs,
-        work=WORK["final"],
-    )
-    return potential
+    tile = ((leaf_points, columns), BF16)
+    near_ins = {
+        "near_core": (0, True, "halo_core"),
+        "near_beside": (1, False, "halo_beside"),
+        "near_across": (1, True, "halo_across"),
+        "near_far": (2, False, "halo_far"),
+        "near_last": (2, True, "halo_last"),
+    }
+
+    def get(name):
+        if name not in have:
+            value = arrive(name)
+            if name in RELEASES:
+                value = hand_on(value, done[RELEASES[name]])
+            have[name] = value
+        return have[name]
+
+    def arrive(name):
+        if name == "sv_1":
+            return xor_exchange(skeleton, "leaf", core_mask)
+        if name.startswith("sv_"):
+            mask = int(name[3:])
+            if mask == 0:
+                return skeleton
+            step = core_mask if mask & core_mask else chip_mask if mask & chip_mask else mask & -mask
+            return xor_exchange(get(f"sv_{mask ^ step}"), "leaf", step)
+        if name == "halo_core":
+            return xor_exchange(halo, "leaf", core_mask)
+        if name == "halo_beside":
+            return xor_exchange(halo, "leaf", chip_mask)
+        if name == "halo_next":
+            return get("halo_beside")
+        if name == "halo_across":
+            return xor_exchange(get("halo_next"), "leaf", core_mask)
+        if name == "halo_far":
+            return lax.ppermute(get("halo_next"), "leaf", ahead + behind)
+        if name == "halo_last":
+            return xor_exchange(get("halo_far"), "leaf", core_mask)
+        if name == "field":
+            return xor_exchange(have["field_send"], "leaf", reduced)
+        if name.startswith("sum_"):
+            return xor_exchange(have["sum_send"], "leaf", int(name[4:]))
+        if name == "packs":
+            own_group = [have["sum_send"]]
+            mask = members
+            while mask < leaves:
+                own_group += [xor_exchange(pack, "leaf", mask) for pack in own_group]
+                mask *= 2
+            packs = []
+            for shift in range(1, groups):
+                order = [(i, (i + shift) % groups) for i in range(groups)]
+                packs += [lax.ppermute(pack, "group", order) for pack in own_group]
+            return jnp.concatenate(packs, axis=0) if len(packs) > 1 else packs[0]
+        if name == "packs_core":
+            return xor_exchange(get("packs"), "leaf", core_mask)
+        raise KeyError(name)
+
+    have["sum"], have["sum_send"] = cluster_sum, cluster_send
+    have["sum_1"] = xor_exchange(cluster_send, "leaf", core_mask)
+    received, token = "sum_1", None
+    for name, work in ORDER.items():
+        after = ([token] if token is not None else []) + [get(x) for x in DEADLINES.get(name, ())]
+        if name in adds:
+            mask, last = adds[name], adds[name] == 0
+            with_skeleton = mask == reduced
+            rows = sum_rows + (2 * sv_points if with_skeleton else 0)
+            outs = [((rows, columns), BF16)] + ([] if last else [((sum_rows, columns), F32)])
+            ins = [have["sum"], have[received]] + ([get("sv_0"), get("sv_1")] if with_skeleton else [])
+            body = functools.partial(add_kernel, with_skeleton, last)
+            have["sum_send"], *total = call(body, outs, ins, after=after, work=work)
+            token = have["sum_send"]
+            if not last:
+                have["sum"], received = total[0], f"sum_{mask}"
+                have[received] = arrive(received)
+            else:
+                get("packs")
+        elif name == "near_self":
+            *targets, near = call(
+                functools.partial(near_kernel, 0, False, features),
+                [tile, tile, tile, ((leaf_points, columns), F32)],
+                [flags, halo],
+                scratch=[((leaf_points, columns), BF16)],
+                after=after,
+                work=work,
+            )
+            token = near
+        elif name in near_ins:
+            stage, across, source = near_ins[name]
+            (near,) = call(
+                functools.partial(near_kernel, stage, across, features),
+                [((leaf_points, columns), F32)],
+                [near, flags, get(source), *targets],
+                scratch=[((leaf_points, columns), BF16)],
+                after=after if token is not near else after[1:],
+                in_place=True,
+                work=work,
+            )
+            token = near
+        elif name == "sibling":
+            *fields, have["field_send"] = call(
+                functools.partial(sibling_kernel, piece_masks, reduced, features, skeletons, reach),
+                [((skeletons, columns), F32)] * 2 + [((2 * skeletons, columns), BF16)],
+                [have[f"sum_{reduced}"], get("sv_1")] + [get(f"sv_{m}") for m in piece_masks],
+                after=after,
+                work=work,
+            )
+            token = fields[0]
+            have["field_core"] = xor_exchange(have["field_send"], "leaf", core_mask)
+        elif name == "field":
+            field, have["field_send"] = call(
+                field_kernel,
+                [((skeletons, columns), F32), ((skeletons, columns), BF16)],
+                fields + [have["field_core"]],
+                after=after,
+                work=work,
+            )
+            token = field
+            get("field")
+        elif name == "final":
+            packs = [get("packs"), get("packs_core")]
+            packs = [p[i : i + sum_rows] for p in packs for i in range(0, p.shape[0], sum_rows)]
+            (token,) = call(
+                functools.partial(final_kernel, len(packs), features),
+                [((leaf_points, columns), BF16)],
+                [near, interp, get("sv_0"), field, get("field")] + packs,
+                work=work,
+            )
+        done[name] = token
+    return token
 
 
 def solution(mesh):

time: 51.4 us -> 43.8 us (0.85)
  the two profiles are of different devices: /device:TPU:0 before, /device:TPU:23 now
where the time goes in v4:
time: 43.8 us; the launch traced here: 43.7 us
  waiting for transfers between devices  16 us (37%)
  starting transfers between devices  14.3 us (33%)
  Pallas kernels  13.2 us (30%)
    ppermute x15, starting transfers between devices, xor_exchange(): lax.ppermute(value, axis, [(i, i ^ mask) for i in range(lax.axis_size(axi...  12.1 us
    pallas_call x13, Pallas kernels, call(): pl.pallas_call(lambda *refs: body(*refs[waits:]), out_shape=[jax.ShapeDty...  10.8 us
    ppermute x15, waiting for transfers between devices, xor_exchange(): lax.ppermute(value, axis, [(i, i ^ mask) for i in range(lax.axis_size(axi...  9.14 us
    ppermute x1, waiting for transfers between devices, arrive(): return lax.ppermute(get('halo_next'), 'leaf', ahead + behind)  4.57 us
    pallas_call x1, Pallas kernels, on_device(): pl.pallas_call(prepare_kernel, out_shape=[jax.ShapeDtypeStruct(shape, dty...  2.4 us
    ppermute x1, waiting for transfers between devices, arrive(): packs += [lax.ppermute(pack, 'group', order) for pack in own_group]  2.28 us
    ppermute x1, starting transfers between devices, arrive(): return lax.ppermute(get('halo_next'), 'leaf', ahead + behind)  1.91 us
  transfers between devices with their start and end apart: 17, of which 8 were waited for; matrix products, arithmetic and copies ran while one was open for 0% of the time, Pallas kernels for 21%

profile of v4, /device:TPU:23, one launch (start us, length us, event | category | flops | bytes accessed | tf_op | source)
XLA Modules:
  0.0 43.7 jit_solution(2934503988893603045)
XLA Ops:
  0.0 2.4 %shard_map.73 = (bf16[1568,128]{1,0:T(8,128)(2,1)S(1)}, bf16[400,128]{1,0:T(8,128)(2,1)S(1)}, f32[400,128]{1,0:T(8,128)S(1)}, bf16[400,128]{1,0:T(8,128)(2,1)S(1)}, s32[1,5]{1,0:T(1,128)S(1)}) custom-call(bf16[64,1024]{1,0:T(8,128)(2,1)} %bitcast.1, bf16[1024,128]{1,0:T(8,128)(2,1)} %weights_hbm.1, bf16[1024,256]{1,0:T(8,128)(2,1)} %refs_1_.1, ...), custom_call_target="tpu_custom_call" | custom-call | flops 1000000 | tf_op jit(solution)/shard_map/pallas_call | solution.py:386
  2.4 0.7 %collective-permute-start.1 = (bf16[1568,128]{1,0:T(8,128)(2,1)S(1)}, bf16[1568,128]{1,0:T(8,128)(2,1)S(1)}, u32[]{:S(2)}, u32[]{:S(2)}) collective-permute-start(bf16[1568,128]{1,0:T(8,128)(2,1)S(1)} %get-tuple-element.29.refs_2_), channel_id=1, source_target_pairs={{0,1},{1,0},{2,3},{3,2},{4,5},{5,4},{6,7},{7,6},{8,9},{9,8},{10,11... | collective-permute-start | bytes 1204232 | tf_op jit(solution)/shard_map/ppermute | solution.py:80
  3.2 0.1 collective-permute-start
  3.2 0.4 collective-permute-start.5
  3.7 0.2 collective-permute-start.2
  3.9 0.8 %collective-permute-done.refs_1_ = bf16[400,128]{1,0:T(8,128)(2,1)S(1)} collective-permute-done((bf16[400,128]{1,0:T(8,128)(2,1)S(1)}, bf16[400,128]{1,0:T(8,128)(2,1)S(1)}, u32[]{:S(2)}, u32[]{:S(2)}) %collective-permute-start) | collective-permute-done | bytes 102432 | tf_op jit(solution)/shard_map/ppermute | solution.py:80
  4.7 0.1 collective-permute-start.4
  4.8 0.0 collective-permute-done.5.refs_5_.refs_3_
  4.8 2.3 %collective-permute-start.3 = (bf16[400,128]{1,0:T(8,128)(2,1)S(1)}, bf16[400,128]{1,0:T(8,128)(2,1)S(1)}, u32[]{:S(2)}, u32[]{:S(2)}) collective-permute-start(bf16[400,128]{1,0:T(8,128)(2,1)S(1)} %shard_map.78.refs_4_.refs_2_), channel_id=1, source_target_pairs={{0,8},{1,9},{2,10},{3,11},{4,12},{5,13},{6,14},{7,15},{8,0},{9,1},... | collective-permute-start | bytes 307208 | tf_op jit(solution)/shard_map/ppermute | solution.py:80
  7.1 1.7 %shard_map.75 = (bf16[1024,128]{1,0:T(8,128)(2,1)S(1)}, bf16[1024,128]{1,0:T(8,128)(2,1)S(1)}, bf16[1024,128]{1,0:T(8,128)(2,1)S(1)}, f32[1024,128]{1,0:T(8,128)S(1)}) custom-call(bf16[400,128]{1,0:T(8,128)(2,1)S(1)} %get-tuple-element.27.refs_0_.refs_1_, s32[1,5]{1,0:T(1,128)S(1)} %get-tuple-element.28.refs_1_.refs_2_.refs_3_, ...), custom_call_target="tpu_custom_call" | custom-call | flops 2000000000 | tf_op jit(solution)/shard_map/pallas_call | solution.py:47
  8.9 0.0 collective-permute-done.1.refs_2_
  8.9 1.3 %shard_map.76.refs_0_ = f32[1024,128]{1,0:T(8,128)S(1)} custom-call(f32[1024,128]{1,0:T(8,128)S(1)} %get-tuple-element.30.refs_0_, s32[1,5]{1,0:T(1,128)S(1)} %get-tuple-element.28.refs_1_.refs_2_.refs_3_, bf16[1568,128]{1,0:T(8,128)(2,1)S(1)} %collective-permute-done.1.refs_2_, ...), custom_call_target="tpu_custom_call", output_to_operand_aliasing={{}: (0, {})} | custom-call | flops 2000000000 | tf_op jit(solution)/shard_map/pallas_call | solution.py:47
  10.2 4.3 %collective-permute-done.2.refs_2_.refs_0_ = bf16[1568,128]{1,0:T(8,128)(2,1)S(1)} collective-permute-done((bf16[1568,128]{1,0:T(8,128)(2,1)S(1)}, bf16[1568,128]{1,0:T(8,128)(2,1)S(1)}, u32[]{:S(2)}, u32[]{:S(2)}) %collective-permute-start.2) | collective-permute-done | bytes 401440 | tf_op jit(solution)/shard_map/ppermute | solution.py:80
  14.5 1.3 %shard_map.77.refs_0_.refs_1_ = f32[1024,128]{1,0:T(8,128)S(1)} custom-call(f32[1024,128]{1,0:T(8,128)S(1)} %shard_map.76.refs_0_, s32[1,5]{1,0:T(1,128)S(1)} %get-tuple-element.28.refs_1_.refs_2_.refs_3_, bf16[1568,128]{1,0:T(8,128)(2,1)S(1)} %collective-permute-done.2.refs_2_.refs_0_, ...), custom_call_target="tpu_custom_call", output_to_operand_aliasing={{}: (0, {})} | custom-call | flops 2000000000 | tf_op jit(solution)/shard_map/pallas_call | solution.py:47
  15.9 0.0 collective-permute-done.3.refs_1_.refs_6_
  15.9 0.0 collective-permute-done.4.refs_3_
  15.9 0.9 %collective-permute-start.9 = (bf16[1568,128]{1,0:T(8,128)(2,1)S(1)}, bf16[1568,128]{1,0:T(8,128)(2,1)S(1)}, u32[]{:S(2)}, u32[]{:S(2)}) collective-permute-start(bf16[1568,128]{1,0:T(8,128)(2,1)S(1)} %shard_map.82), channel_id=1, source_target_pairs={{0,1},{1,0},{2,3},{3,2},{4,5},{5,4},{6,7},{7,6},{8,9},{9,8},{10,11... | collective-permute-start | bytes 1204232 | tf_op jit(solution)/shard_map/ppermute | solution.py:80
  16.9 2.0 %collective-permute-start.6 = (bf16[688,128]{1,0:T(8,128)(2,1)S(1)}, bf16[688,128]{1,0:T(8,128)(2,1)S(1)}, u32[]{:S(2)}, u32[]{:S(2)}) collective-permute-start(bf16[688,128]{1,0:T(8,128)(2,1)S(1)} %get-tuple-element.36.refs_0_.refs_1_), channel_id=1, source_target_pairs={{0,4},{1,5},{2,6},{3,7},{4,0},{5,1},{6,2},{7,3},{8,12},{9,13},{10,... | collective-permute-start | bytes 528392 | tf_op jit(solution)/shard_map/ppermute | solution.py:80
  18.9 0.5 %collective-permute-start.8 = (bf16[400,128]{1,0:T(8,128)(2,1)S(1)}, bf16[400,128]{1,0:T(8,128)(2,1)S(1)}, u32[]{:S(2)}, u32[]{:S(2)}) collective-permute-start(bf16[400,128]{1,0:T(8,128)(2,1)S(1)} %shard_map.78.refs_4_.refs_2_), channel_id=1, source_target_pairs={{0,2},{1,3},{2,0},{3,1},{4,6},{5,7},{6,4},{7,5},{8,10},{9,11},{10,... | collective-permute-start | bytes 307208 | tf_op jit(solution)/shard_map/ppermute | solution.py:80
  19.3 1.0 %collective-permute-start.7 = (bf16[400,128]{1,0:T(8,128)(2,1)S(1)}, bf16[400,128]{1,0:T(8,128)(2,1)S(1)}, u32[]{:S(2)}, u32[]{:S(2)}) collective-permute-start(bf16[400,128]{1,0:T(8,128)(2,1)S(1)} %collective-permute-done.3.refs_1_.refs_6_), channel_id=1, source_target_pairs={{0,2},{1,3},{2,0},{3,1},{4,6},{5,7},{6,4},{7,5},{8,10},{9,11},{10,... | collective-permute-start | bytes 307208 | tf_op jit(solution)/shard_map/ppermute | solution.py:80
  20.3 1.9 %collective-permute-start.14 = (bf16[1568,128]{1,0:T(8,128)(2,1)S(1)}, bf16[1568,128]{1,0:T(8,128)(2,1)S(1)}, u32[]{:S(2)}, u32[]{:S(2)}) collective-permute-start(bf16[1568,128]{1,0:T(8,128)(2,1)S(1)} %shard_map.82), channel_id=1, source_target_pairs={{0,4},{1,5},{4,8},{5,9},{8,12},{9,13},{6,2},{7,3},{10,6},{11,7},{1... | collective-permute-start | bytes 1204232 | tf_op jit(solution)/shard_map/ppermute | solution.py:440
  22.2 1.4 %collective-permute-done.6.refs_2_ = bf16[688,128]{1,0:T(8,128)(2,1)S(1)} collective-permute-done((bf16[688,128]{1,0:T(8,128)(2,1)S(1)}, bf16[688,128]{1,0:T(8,128)(2,1)S(1)}, u32[]{:S(2)}, u32[]{:S(2)}) %collective-permute-start.6) | collective-permute-done | bytes 176160 | tf_op jit(solution)/shard_map/ppermute | solution.py:80
  23.6 0.6 %collective-permute-start.10 = (bf16[400,128]{1,0:T(8,128)(2,1)S(1)}, bf16[400,128]{1,0:T(8,128)(2,1)S(1)}, u32[]{:S(2)}, u32[]{:S(2)}) collective-permute-start(bf16[400,128]{1,0:T(8,128)(2,1)S(1)} %get-tuple-element.38.refs_0_), channel_id=1, source_target_pairs={{0,2},{1,3},{2,0},{3,1},{4,6},{5,7},{6,4},{7,5},{8,10},{9,11},{10,... | collective-permute-start | bytes 307208 | tf_op jit(solution)/shard_map/ppermute | solution.py:80
  24.2 0.0 collective-permute-done.8.refs_5_
  24.2 1.0 %collective-permute-done.7.refs_1_.refs_7_ = bf16[400,128]{1,0:T(8,128)(2,1)S(1)} collective-permute-done((bf16[400,128]{1,0:T(8,128)(2,1)S(1)}, bf16[400,128]{1,0:T(8,128)(2,1)S(1)}, u32[]{:S(2)}, u32[]{:S(2)}) %collective-permute-start.7) | collective-permute-done | bytes 102432 | tf_op jit(solution)/shard_map/ppermute | solution.py:80
  25.2 1.9 %shard_map.81 = (f32[256,128]{1,0:T(8,128)S(1)}, f32[256,128]{1,0:T(8,128)S(1)}, bf16[512,128]{1,0:T(8,128)(2,1)S(1)}) custom-call(bf16[400,128]{1,0:T(8,128)(2,1)S(1)} %get-tuple-element.38.refs_0_, bf16[400,128]{1,0:T(8,128)(2,1)S(1)} %collective-permute-done.7.refs_1_.refs_7_, bf16[688,128]{1,0:T(8,128)(2,1)S(1)} %collective-permute-done.6.refs_2_, ...), custom_call_target="tpu_custom_call" | custom-call | flops 2000000000 | tf_op jit(solution)/shard_map/pallas_call | solution.py:47
  27.1 0.0 collective-permute-done.9.refs_3_
  27.1 0.4 collective-permute-done.10.refs_2_
  27.5 4.6 %collective-permute-done.14.refs_0_ = bf16[1568,128]{1,0:T(8,128)(2,1)S(1)} collective-permute-done((bf16[1568,128]{1,0:T(8,128)(2,1)S(1)}, bf16[1568,128]{1,0:T(8,128)(2,1)S(1)}, u32[]{:S(2)}, u32[]{:S(2)}) %collective-permute-start.14) | collective-permute-done | bytes 401440 | tf_op jit(solution)/shard_map/ppermute | solution.py:440
  32.1 1.8 %collective-permute-start.15 = (bf16[1568,128]{1,0:T(8,128)(2,1)S(1)}, bf16[1568,128]{1,0:T(8,128)(2,1)S(1)}, u32[]{:S(2)}, u32[]{:S(2)}) collective-permute-start(bf16[1568,128]{1,0:T(8,128)(2,1)S(1)} %shard_map.86.refs_4_), channel_id=1, source_target_pairs={{0,1},{1,0},{2,3},{3,2},{4,5},{5,4},{6,7},{7,6},{8,9},{9,8},{10,11... | collective-permute-start | bytes 1204232 | tf_op jit(solution)/shard_map/ppermute | solution.py:80
  33.9 0.0 collective-permute-start.13
  33.9 0.3 collective-permute-start.11
  34.2 1.3 %collective-permute-done.13.refs_3_ = bf16[512,128]{1,0:T(8,128)(2,1)S(1)} collective-permute-done((bf16[512,128]{1,0:T(8,128)(2,1)S(1)}, bf16[512,128]{1,0:T(8,128)(2,1)S(1)}, u32[]{:S(2)}, u32[]{:S(2)}) %collective-permute-start.13) | collective-permute-done | bytes 131104 | tf_op jit(solution)/shard_map/ppermute | solution.py:80
  35.5 0.1 collective-permute-start.16
  35.6 2.3 %collective-permute-done.11.refs_1_.refs_5_ = bf16[400,128]{1,0:T(8,128)(2,1)S(1)} collective-permute-done((bf16[400,128]{1,0:T(8,128)(2,1)S(1)}, bf16[400,128]{1,0:T(8,128)(2,1)S(1)}, u32[]{:S(2)}, u32[]{:S(2)}) %collective-permute-start.11) | collective-permute-done | bytes 102432 | tf_op jit(solution)/shard_map/ppermute | solution.py:456
  37.9 1.4 %collective-permute-start.12 = (bf16[400,128]{1,0:T(8,128)(2,1)S(1)}, bf16[400,128]{1,0:T(8,128)(2,1)S(1)}, u32[]{:S(2)}, u32[]{:S(2)}) collective-permute-start(bf16[400,128]{1,0:T(8,128)(2,1)S(1)} %collective-permute-done.11.refs_1_.refs_5_), channel_id=1, source_target_pairs={{0,1},{1,0},{2,3},{3,2},{4,5},{5,4},{6,7},{7,6},{8,9},{9,8},{10,11... | collective-permute-start | bytes 307208 | tf_op jit(solution)/shard_map/ppermute | solution.py:80
  39.2 1.3 %shard_map.87.refs_1_ = f32[1024,128]{1,0:T(8,128)S(1)} custom-call(f32[256,128]{1,0:T(8,128)S(1)} %get-tuple-element.43.refs_0_.refs_3_, bf16[400,128]{1,0:T(8,128)(2,1)S(1)} %collective-permute-done.11.refs_1_.refs_5_, f32[1024,128]{1,0:T(8,128)S(1)} %shard_map.83.refs_0_.refs_2_, ...), custom_call_target="tpu_custom_call", output_to_operand_aliasing={{}: (2, {})} | custom-call | flops 2000000000 | tf_op jit(solution)/shard_map/pallas_call | solution.py:47
  40.5 0.0 copy-start
  40.6 0.0 collective-permute-done.12.refs_0_.refs_6_
  40.6 0.0 collective-permute-done.15.refs_3_
  40.6 1.4 %shard_map.88.refs_0_ = f32[1024,128]{1,0:T(8,128)S(1)} custom-call(bf16[400,128]{1,0:T(8,128)(2,1)S(1)} %collective-permute-done.12.refs_0_.refs_6_, f32[1024,128]{1,0:T(8,128)S(1)} %shard_map.87.refs_1_, s32[1,5]{1,0:T(1,128)S(1)} %get-tuple-element.28.refs_1_.refs_2_.refs_3_, ...), custom_call_target="tpu_custom_call", output_to_operand_aliasing={{}: (1, {})} | custom-call | flops 2000000000 | tf_op jit(solution)/shard_map/pallas_call | solution.py:47
  41.9 0.0 collective-permute-done.16.refs_4_
  42.0 0.0 copy-done
  42.0 1.7 %shard_map.89 = bf16[1024,128]{1,0:T(8,128)(2,1)} custom-call(f32[1024,128]{1,0:T(8,128)S(1)} %shard_map.88.refs_0_, bf16[1024,256]{1,0:T(8,128)(2,1)S(1)} %copy-done, bf16[400,128]{1,0:T(8,128)(2,1)S(1)} %shard_map.78.refs_4_.refs_2_, f32[256,128]{1,0:T(8,128)S(1)} %get-tuple-element.43.refs_0_.refs_3_, ...), custom_call_target="tpu_custom_call" | custom-call | flops 2000000000 | tf_op jit(solution)/shard_map/pallas_call | solution.py:47
  (9 shorter events, 0.2 us)
Async XLA Ops:
  2.4 6.5 %collective-permute-start.1 = (bf16[1568,128]{1,0:T(8,128)(2,1)S(1)}, bf16[1568,128]{1,0:T(8,128)(2,1)S(1)}, u32[]{:S(2)}, u32[]{:S(2)}) collective-permute-start(bf16[1568,128]{1,0:T(8,128)(2,1)S(1)} %get-tuple-element.29.refs_2_), channel_id=1, source_target_pairs={{0,1},{1,0},{2,3},{3,2},{4,5},{5,4},{6,7},{7,6},{8,9},{9,8},{10,11... | collective-permute-start | bytes 1204232 | tf_op jit(solution)/shard_map/ppermute | solution.py:80
  3.2 1.5 %collective-permute-start = (bf16[400,128]{1,0:T(8,128)(2,1)S(1)}, bf16[400,128]{1,0:T(8,128)(2,1)S(1)}, u32[]{:S(2)}, u32[]{:S(2)}) collective-permute-start(bf16[400,128]{1,0:T(8,128)(2,1)S(1)} %get-tuple-element.26), channel_id=1, source_target_pairs={{0,1},{1,0},{2,3},{3,2},{4,5},{5,4},{6,7},{7,6},{8,9},{9,8},{10,11... | collective-permute-start | bytes 307208 | tf_op jit(solution)/shard_map/ppermute | solution.py:80
  3.2 1.6 %collective-permute-start.5 = (bf16[400,128]{1,0:T(8,128)(2,1)S(1)}, bf16[400,128]{1,0:T(8,128)(2,1)S(1)}, u32[]{:S(2)}, u32[]{:S(2)}) collective-permute-start(bf16[400,128]{1,0:T(8,128)(2,1)S(1)} %get-tuple-element.34.refs_0_), channel_id=1, source_target_pairs={{0,1},{1,0},{2,3},{3,2},{4,5},{5,4},{6,7},{7,6},{8,9},{9,8},{10,11... | collective-permute-start | bytes 307208 | tf_op jit(solution)/shard_map/ppermute | solution.py:80
  3.7 10.9 %collective-permute-start.2 = (bf16[1568,128]{1,0:T(8,128)(2,1)S(1)}, bf16[1568,128]{1,0:T(8,128)(2,1)S(1)}, u32[]{:S(2)}, u32[]{:S(2)}) collective-permute-start(bf16[1568,128]{1,0:T(8,128)(2,1)S(1)} %get-tuple-element.29.refs_2_), channel_id=1, source_target_pairs={{0,2},{1,3},{2,0},{3,1},{4,6},{5,7},{6,4},{7,5},{8,10},{9,11},{10,... | collective-permute-start | bytes 1204232 | tf_op jit(solution)/shard_map/ppermute | solution.py:80
  4.7 11.2 %collective-permute-start.4 = (bf16[400,128]{1,0:T(8,128)(2,1)S(1)}, bf16[400,128]{1,0:T(8,128)(2,1)S(1)}, u32[]{:S(2)}, u32[]{:S(2)}) collective-permute-start(bf16[400,128]{1,0:T(8,128)(2,1)S(1)} %get-tuple-element.27.refs_0_.refs_1_), channel_id=1, source_target_pairs={{0,8},{1,9},{2,10},{3,11},{4,12},{5,13},{6,14},{7,15},{8,0},{9,1},... | collective-permute-start | bytes 307208 | tf_op jit(solution)/shard_map/ppermute | solution.py:80
  4.8 11.0 %collective-permute-start.3 = (bf16[400,128]{1,0:T(8,128)(2,1)S(1)}, bf16[400,128]{1,0:T(8,128)(2,1)S(1)}, u32[]{:S(2)}, u32[]{:S(2)}) collective-permute-start(bf16[400,128]{1,0:T(8,128)(2,1)S(1)} %shard_map.78.refs_4_.refs_2_), channel_id=1, source_target_pairs={{0,8},{1,9},{2,10},{3,11},{4,12},{5,13},{6,14},{7,15},{8,0},{9,1},... | collective-permute-start | bytes 307208 | tf_op jit(solution)/shard_map/ppermute | solution.py:80
  15.9 11.1 %collective-permute-start.9 = (bf16[1568,128]{1,0:T(8,128)(2,1)S(1)}, bf16[1568,128]{1,0:T(8,128)(2,1)S(1)}, u32[]{:S(2)}, u32[]{:S(2)}) collective-permute-start(bf16[1568,128]{1,0:T(8,128)(2,1)S(1)} %shard_map.82), channel_id=1, source_target_pairs={{0,1},{1,0},{2,3},{3,2},{4,5},{5,4},{6,7},{7,6},{8,9},{9,8},{10,11... | collective-permute-start | bytes 1204232 | tf_op jit(solution)/shard_map/ppermute | solution.py:80
  16.9 6.7 %collective-permute-start.6 = (bf16[688,128]{1,0:T(8,128)(2,1)S(1)}, bf16[688,128]{1,0:T(8,128)(2,1)S(1)}, u32[]{:S(2)}, u32[]{:S(2)}) collective-permute-start(bf16[688,128]{1,0:T(8,128)(2,1)S(1)} %get-tuple-element.36.refs_0_.refs_1_), channel_id=1, source_target_pairs={{0,4},{1,5},{2,6},{3,7},{4,0},{5,1},{6,2},{7,3},{8,12},{9,13},{10,... | collective-permute-start | bytes 528392 | tf_op jit(solution)/shard_map/ppermute | solution.py:80
  18.9 5.3 %collective-permute-start.8 = (bf16[400,128]{1,0:T(8,128)(2,1)S(1)}, bf16[400,128]{1,0:T(8,128)(2,1)S(1)}, u32[]{:S(2)}, u32[]{:S(2)}) collective-permute-start(bf16[400,128]{1,0:T(8,128)(2,1)S(1)} %shard_map.78.refs_4_.refs_2_), channel_id=1, source_target_pairs={{0,2},{1,3},{2,0},{3,1},{4,6},{5,7},{6,4},{7,5},{8,10},{9,11},{10,... | collective-permute-start | bytes 307208 | tf_op jit(solution)/shard_map/ppermute | solution.py:80
  19.3 5.8 %collective-permute-start.7 = (bf16[400,128]{1,0:T(8,128)(2,1)S(1)}, bf16[400,128]{1,0:T(8,128)(2,1)S(1)}, u32[]{:S(2)}, u32[]{:S(2)}) collective-permute-start(bf16[400,128]{1,0:T(8,128)(2,1)S(1)} %collective-permute-done.3.refs_1_.refs_6_), channel_id=1, source_target_pairs={{0,2},{1,3},{2,0},{3,1},{4,6},{5,7},{6,4},{7,5},{8,10},{9,11},{10,... | collective-permute-start | bytes 307208 | tf_op jit(solution)/shard_map/ppermute | solution.py:80
  20.3 11.8 %collective-permute-start.14 = (bf16[1568,128]{1,0:T(8,128)(2,1)S(1)}, bf16[1568,128]{1,0:T(8,128)(2,1)S(1)}, u32[]{:S(2)}, u32[]{:S(2)}) collective-permute-start(bf16[1568,128]{1,0:T(8,128)(2,1)S(1)} %shard_map.82), channel_id=1, source_target_pairs={{0,4},{1,5},{4,8},{5,9},{8,12},{9,13},{6,2},{7,3},{10,6},{11,7},{1... | collective-permute-start | bytes 1204232 | tf_op jit(solution)/shard_map/ppermute | solution.py:440
  23.6 3.9 %collective-permute-start.10 = (bf16[400,128]{1,0:T(8,128)(2,1)S(1)}, bf16[400,128]{1,0:T(8,128)(2,1)S(1)}, u32[]{:S(2)}, u32[]{:S(2)}) collective-permute-start(bf16[400,128]{1,0:T(8,128)(2,1)S(1)} %get-tuple-element.38.refs_0_), channel_id=1, source_target_pairs={{0,2},{1,3},{2,0},{3,1},{4,6},{5,7},{6,4},{7,5},{8,10},{9,11},{10,... | collective-permute-start | bytes 307208 | tf_op jit(solution)/shard_map/ppermute | solution.py:80
  32.1 8.5 %collective-permute-start.15 = (bf16[1568,128]{1,0:T(8,128)(2,1)S(1)}, bf16[1568,128]{1,0:T(8,128)(2,1)S(1)}, u32[]{:S(2)}, u32[]{:S(2)}) collective-permute-start(bf16[1568,128]{1,0:T(8,128)(2,1)S(1)} %shard_map.86.refs_4_), channel_id=1, source_target_pairs={{0,1},{1,0},{2,3},{3,2},{4,5},{5,4},{6,7},{7,6},{8,9},{9,8},{10,11... | collective-permute-start | bytes 1204232 | tf_op jit(solution)/shard_map/ppermute | solution.py:80
  33.9 1.5 %collective-permute-start.13 = (bf16[512,128]{1,0:T(8,128)(2,1)S(1)}, bf16[512,128]{1,0:T(8,128)(2,1)S(1)}, u32[]{:S(2)}, u32[]{:S(2)}) collective-permute-start(bf16[512,128]{1,0:T(8,128)(2,1)S(1)} %get-tuple-element.42), channel_id=1, source_target_pairs={{0,1},{1,0},{2,3},{3,2},{4,5},{5,4},{6,7},{7,6},{8,9},{9,8},{10,11... | collective-permute-start | bytes 393224 | tf_op jit(solution)/shard_map/ppermute | solution.py:80
  33.9 3.9 %collective-permute-start.11 = (bf16[400,128]{1,0:T(8,128)(2,1)S(1)}, bf16[400,128]{1,0:T(8,128)(2,1)S(1)}, u32[]{:S(2)}, u32[]{:S(2)}) collective-permute-start(bf16[400,128]{1,0:T(8,128)(2,1)S(1)} %shard_map.84.refs_0_.refs_1_), channel_id=1, source_target_pairs={{0,16},{16,0},{1,17},{17,1},{2,18},{18,2},{3,19},{19,3},{4,20},{20... | collective-permute-start | bytes 307208 | tf_op jit(solution)/shard_map/ppermute | solution.py:456
  35.5 6.5 %collective-permute-start.16 = (bf16[256,128]{1,0:T(8,128)(2,1)S(1)}, bf16[256,128]{1,0:T(8,128)(2,1)S(1)}, u32[]{:S(2)}, u32[]{:S(2)}) collective-permute-start(bf16[256,128]{1,0:T(8,128)(2,1)S(1)} %get-tuple-element.44), channel_id=1, source_target_pairs={{0,4},{1,5},{2,6},{3,7},{4,0},{5,1},{6,2},{7,3},{8,12},{9,13},{10,... | collective-permute-start | bytes 196616 | tf_op jit(solution)/shard_map/ppermute | solution.py:80
  37.9 2.7 %collective-permute-start.12 = (bf16[400,128]{1,0:T(8,128)(2,1)S(1)}, bf16[400,128]{1,0:T(8,128)(2,1)S(1)}, u32[]{:S(2)}, u32[]{:S(2)}) collective-permute-start(bf16[400,128]{1,0:T(8,128)(2,1)S(1)} %collective-permute-done.11.refs_1_.refs_5_), channel_id=1, source_target_pairs={{0,1},{1,0},{2,3},{3,2},{4,5},{5,4},{6,7},{7,6},{8,9},{9,8},{10,11... | collective-permute-start | bytes 307208 | tf_op jit(solution)/shard_map/ppermute | solution.py:80
  40.5 1.4 %copy-start = (bf16[1024,256]{1,0:T(8,128)(2,1)S(1)}, bf16[1024,256]{1,0:T(8,128)(2,1)}, u32[]{:S(2)}) copy-start(bf16[1024,256]{1,0:T(8,128)(2,1)} %refs_1_.1) | copy-start | bytes 1572868

commit v5 on v4

--- a/solution.py
+++ b/solution.py
@@ -32,10 +32,9 @@
 DEADLINES = {
     "add_a": ["sv_8"],
     "sibling": ["sv_10"],
-    "near_far": ["packs"],
-    "near_last": ["packs_core"],
+    "field": ["packs"],
 }
-RELEASES = {"sv_0": "first_add", "halo_next": "add_a", "halo_far": "add_c"}
+RELEASES = {"sv_0": "first_add", "halo_next": "near_core", "halo_far": "field"}
 
 
 def vmem():
@@ -405,7 +404,7 @@
     tile = ((leaf_points, columns), BF16)
     near_ins = {
         "near_core": (0, True, "halo_core"),
-        "near_beside": (1, False, "halo_beside"),
+        "near_beside": (1, False, "halo_next"),
         "near_across": (1, True, "halo_across"),
         "near_far": (2, False, "halo_far"),
         "near_last": (2, True, "halo_last"),

time: 43.8 us -> 41.7 us (0.952)
  the two profiles are of different devices: /device:TPU:23 before, /device:TPU:0 now
where the time goes in v5:
time: 41.7 us; the launch traced here: 41.6 us
  starting transfers between devices  17.7 us (42%)
  Pallas kernels  13.2 us (32%)
  waiting for transfers between devices  10.4 us (25%)
    ppermute x15, starting transfers between devices, xor_exchange(): lax.ppermute(value, axis, [(i, i ^ mask) for i in range(lax.axis_size(axi...  12.9 us
    pallas_call x13, Pallas kernels, call(): pl.pallas_call(lambda *refs: body(*refs[waits:]), out_shape=[jax.ShapeDty...  10.8 us
    ppermute x15, waiting for transfers between devices, xor_exchange(): lax.ppermute(value, axis, [(i, i ^ mask) for i in range(lax.axis_size(axi...  6.43 us
    ppermute x1, waiting for transfers between devices, arrive(): packs += [lax.ppermute(pack, 'group', order) for pack in own_group]  4 us
    ppermute x1, starting transfers between devices, arrive(): return lax.ppermute(get('halo_next'), 'leaf', ahead + behind)  3.26 us
    pallas_call x1, Pallas kernels, on_device(): pl.pallas_call(prepare_kernel, out_shape=[jax.ShapeDtypeStruct(shape, dty...  2.41 us
    ppermute x1, starting transfers between devices, arrive(): packs += [lax.ppermute(pack, 'group', order) for pack in own_group]  1.56 us
  transfers between devices with their start and end apart: 17, of which 5 were waited for; matrix products, arithmetic and copies ran while one was open for 0% of the time, Pallas kernels for 22%

profile of v5, /device:TPU:0, one launch (start us, length us, event | category | flops | bytes accessed | tf_op | source)
XLA Modules:
  0.0 41.6 jit_solution(10499753369633689665)
XLA Ops:
  0.0 2.4 %shard_map.73 = (bf16[1568,128]{1,0:T(8,128)(2,1)S(1)}, bf16[400,128]{1,0:T(8,128)(2,1)S(1)}, f32[400,128]{1,0:T(8,128)S(1)}, bf16[400,128]{1,0:T(8,128)(2,1)S(1)}, s32[1,5]{1,0:T(1,128)S(1)}) custom-call(bf16[64,1024]{1,0:T(8,128)(2,1)} %bitcast.1, bf16[1024,128]{1,0:T(8,128)(2,1)} %weights_hbm.1, bf16[1024,256]{1,0:T(8,128)(2,1)} %refs_1_.1, ...), custom_call_target="tpu_custom_call" | custom-call | flops 1000000 | tf_op jit(solution)/shard_map/pallas_call | solution.py:385
  2.4 0.5 %collective-permute-start.1 = (bf16[1568,128]{1,0:T(8,128)(2,1)S(1)}, bf16[1568,128]{1,0:T(8,128)(2,1)S(1)}, u32[]{:S(2)}, u32[]{:S(2)}) collective-permute-start(bf16[1568,128]{1,0:T(8,128)(2,1)S(1)} %get-tuple-element.29.refs_2_), channel_id=1, source_target_pairs={{0,1},{1,0},{2,3},{3,2},{4,5},{5,4},{6,7},{7,6},{8,9},{9,8},{10,11... | collective-permute-start | bytes 1204232 | tf_op jit(solution)/shard_map/ppermute | solution.py:79
  2.9 0.1 collective-permute-start
  3.0 0.4 %collective-permute-start.5 = (bf16[400,128]{1,0:T(8,128)(2,1)S(1)}, bf16[400,128]{1,0:T(8,128)(2,1)S(1)}, u32[]{:S(2)}, u32[]{:S(2)}) collective-permute-start(bf16[400,128]{1,0:T(8,128)(2,1)S(1)} %get-tuple-element.34.refs_0_), channel_id=1, source_target_pairs={{0,1},{1,0},{2,3},{3,2},{4,5},{5,4},{6,7},{7,6},{8,9},{9,8},{10,11... | collective-permute-start | bytes 307208 | tf_op jit(solution)/shard_map/ppermute | solution.py:79
  3.4 2.6 %collective-permute-start.2 = (bf16[1568,128]{1,0:T(8,128)(2,1)S(1)}, bf16[1568,128]{1,0:T(8,128)(2,1)S(1)}, u32[]{:S(2)}, u32[]{:S(2)}) collective-permute-start(bf16[1568,128]{1,0:T(8,128)(2,1)S(1)} %get-tuple-element.29.refs_2_), channel_id=1, source_target_pairs={{0,2},{1,3},{2,0},{3,1},{4,6},{5,7},{6,4},{7,5},{8,10},{9,11},{10,... | collective-permute-start | bytes 1204232 | tf_op jit(solution)/shard_map/ppermute | solution.py:79
  6.0 0.0 collective-permute-done.refs_1_
  6.1 2.7 %collective-permute-start.4 = (bf16[400,128]{1,0:T(8,128)(2,1)S(1)}, bf16[400,128]{1,0:T(8,128)(2,1)S(1)}, u32[]{:S(2)}, u32[]{:S(2)}) collective-permute-start(bf16[400,128]{1,0:T(8,128)(2,1)S(1)} %get-tuple-element.27.refs_0_.refs_1_), channel_id=1, source_target_pairs={{0,8},{1,9},{2,10},{3,11},{4,12},{5,13},{6,14},{7,15},{8,0},{9,1},... | collective-permute-start | bytes 307208 | tf_op jit(solution)/shard_map/ppermute | solution.py:79
  8.7 0.0 collective-permute-done.5.refs_5_.refs_3_
  8.7 0.3 collective-permute-start.3
  9.1 1.7 %shard_map.75 = (bf16[1024,128]{1,0:T(8,128)(2,1)S(1)}, bf16[1024,128]{1,0:T(8,128)(2,1)S(1)}, bf16[1024,128]{1,0:T(8,128)(2,1)S(1)}, f32[1024,128]{1,0:T(8,128)S(1)}) custom-call(bf16[400,128]{1,0:T(8,128)(2,1)S(1)} %get-tuple-element.27.refs_0_.refs_1_, s32[1,5]{1,0:T(1,128)S(1)} %get-tuple-element.28.refs_1_.refs_2_, ...), custom_call_target="tpu_custom_call" | custom-call | flops 2000000000 | tf_op jit(solution)/shard_map/pallas_call | solution.py:46
  10.8 0.0 collective-permute-done.1.refs_2_
  10.8 1.3 %shard_map.76.refs_1_.refs_0_ = f32[1024,128]{1,0:T(8,128)S(1)} custom-call(f32[1024,128]{1,0:T(8,128)S(1)} %get-tuple-element.30.refs_0_, s32[1,5]{1,0:T(1,128)S(1)} %get-tuple-element.28.refs_1_.refs_2_, bf16[1568,128]{1,0:T(8,128)(2,1)S(1)} %collective-permute-done.1.refs_2_, ...), custom_call_target="tpu_custom_call", output_to_operand_aliasing={{}: (0, {})} | custom-call | flops 2000000000 | tf_op jit(solution)/shard_map/pallas_call | solution.py:46
  12.1 3.8 %collective-permute-done.2.refs_0_ = bf16[1568,128]{1,0:T(8,128)(2,1)S(1)} collective-permute-done((bf16[1568,128]{1,0:T(8,128)(2,1)S(1)}, bf16[1568,128]{1,0:T(8,128)(2,1)S(1)}, u32[]{:S(2)}, u32[]{:S(2)}) %collective-permute-start.2) | collective-permute-done | bytes 401440 | tf_op jit(solution)/shard_map/ppermute | solution.py:79
  15.9 0.0 collective-permute-start.9
  15.9 1.3 %shard_map.78.refs_0_.refs_1_ = f32[1024,128]{1,0:T(8,128)S(1)} custom-call(f32[1024,128]{1,0:T(8,128)S(1)} %shard_map.76.refs_1_.refs_0_, s32[1,5]{1,0:T(1,128)S(1)} %get-tuple-element.28.refs_1_.refs_2_, bf16[1568,128]{1,0:T(8,128)(2,1)S(1)} %shard_map.77.refs_2_, ...), custom_call_target="tpu_custom_call", output_to_operand_aliasing={{}: (0, {})} | custom-call | flops 2000000000 | tf_op jit(solution)/shard_map/pallas_call | solution.py:46
  17.3 1.3 %collective-permute-done.3.refs_1_.refs_6_ = bf16[400,128]{1,0:T(8,128)(2,1)S(1)} collective-permute-done((bf16[400,128]{1,0:T(8,128)(2,1)S(1)}, bf16[400,128]{1,0:T(8,128)(2,1)S(1)}, u32[]{:S(2)}, u32[]{:S(2)}) %collective-permute-start.3) | collective-permute-done | bytes 102432 | tf_op jit(solution)/shard_map/ppermute | solution.py:79
  18.6 0.0 collective-permute-done.4.refs_3_
  18.6 0.8 %collective-permute-start.6 = (bf16[688,128]{1,0:T(8,128)(2,1)S(1)}, bf16[688,128]{1,0:T(8,128)(2,1)S(1)}, u32[]{:S(2)}, u32[]{:S(2)}) collective-permute-start(bf16[688,128]{1,0:T(8,128)(2,1)S(1)} %get-tuple-element.36.refs_0_), channel_id=1, source_target_pairs={{0,4},{1,5},{2,6},{3,7},{4,0},{5,1},{6,2},{7,3},{8,12},{9,13},{10,... | collective-permute-start | bytes 528392 | tf_op jit(solution)/shard_map/ppermute | solution.py:79
  19.4 1.3 %collective-permute-start.8 = (bf16[400,128]{1,0:T(8,128)(2,1)S(1)}, bf16[400,128]{1,0:T(8,128)(2,1)S(1)}, u32[]{:S(2)}, u32[]{:S(2)}) collective-permute-start(bf16[400,128]{1,0:T(8,128)(2,1)S(1)} %shard_map.79.refs_4_.refs_2_), channel_id=1, source_target_pairs={{0,2},{1,3},{2,0},{3,1},{4,6},{5,7},{6,4},{7,5},{8,10},{9,11},{10,... | collective-permute-start | bytes 307208 | tf_op jit(solution)/shard_map/ppermute | solution.py:79
  20.7 0.7 %collective-permute-start.7 = (bf16[400,128]{1,0:T(8,128)(2,1)S(1)}, bf16[400,128]{1,0:T(8,128)(2,1)S(1)}, u32[]{:S(2)}, u32[]{:S(2)}) collective-permute-start(bf16[400,128]{1,0:T(8,128)(2,1)S(1)} %collective-permute-done.3.refs_1_.refs_6_), channel_id=1, source_target_pairs={{0,2},{1,3},{2,0},{3,1},{4,6},{5,7},{6,4},{7,5},{8,10},{9,11},{10,... | collective-permute-start | bytes 307208 | tf_op jit(solution)/shard_map/ppermute | solution.py:79
  21.4 3.3 %collective-permute-start.13 = (bf16[1568,128]{1,0:T(8,128)(2,1)S(1)}, bf16[1568,128]{1,0:T(8,128)(2,1)S(1)}, u32[]{:S(2)}, u32[]{:S(2)}) collective-permute-start(bf16[1568,128]{1,0:T(8,128)(2,1)S(1)} %shard_map.77.refs_2_), channel_id=1, source_target_pairs={{0,4},{1,5},{4,8},{5,9},{8,12},{9,13},{6,2},{7,3},{10,6},{11,7},{1... | collective-permute-start | bytes 1204232 | tf_op jit(solution)/shard_map/ppermute | solution.py:439
  24.7 0.0 collective-permute-done.6.refs_2_
  24.7 1.4 %collective-permute-start.10 = (bf16[400,128]{1,0:T(8,128)(2,1)S(1)}, bf16[400,128]{1,0:T(8,128)(2,1)S(1)}, u32[]{:S(2)}, u32[]{:S(2)}) collective-permute-start(bf16[400,128]{1,0:T(8,128)(2,1)S(1)} %get-tuple-element.38.refs_0_), channel_id=1, source_target_pairs={{0,2},{1,3},{2,0},{3,1},{4,6},{5,7},{6,4},{7,5},{8,10},{9,11},{10,... | collective-permute-start | bytes 307208 | tf_op jit(solution)/shard_map/ppermute | solution.py:79
  26.1 0.0 collective-permute-done.8.refs_5_
  26.1 0.8 %collective-permute-done.7.refs_1_.refs_7_ = bf16[400,128]{1,0:T(8,128)(2,1)S(1)} collective-permute-done((bf16[400,128]{1,0:T(8,128)(2,1)S(1)}, bf16[400,128]{1,0:T(8,128)(2,1)S(1)}, u32[]{:S(2)}, u32[]{:S(2)}) %collective-permute-start.7) | collective-permute-done | bytes 102432 | tf_op jit(solution)/shard_map/ppermute | solution.py:79
  26.9 1.9 %shard_map.82 = (f32[256,128]{1,0:T(8,128)S(1)}, f32[256,128]{1,0:T(8,128)S(1)}, bf16[512,128]{1,0:T(8,128)(2,1)S(1)}) custom-call(bf16[400,128]{1,0:T(8,128)(2,1)S(1)} %get-tuple-element.38.refs_0_, bf16[400,128]{1,0:T(8,128)(2,1)S(1)} %collective-permute-done.7.refs_1_.refs_7_, bf16[688,128]{1,0:T(8,128)(2,1)S(1)} %collective-permute-done.6.refs_2_, ...), custom_call_target="tpu_custom_call" | custom-call | flops 2000000000 | tf_op jit(solution)/shard_map/pallas_call | solution.py:46
  28.8 0.1 collective-permute-start.12
  28.9 0.0 collective-permute-done.9.refs_3_
  28.9 0.5 %collective-permute-done.10.refs_2_ = bf16[400,128]{1,0:T(8,128)(2,1)S(1)} collective-permute-done((bf16[400,128]{1,0:T(8,128)(2,1)S(1)}, bf16[400,128]{1,0:T(8,128)(2,1)S(1)}, u32[]{:S(2)}, u32[]{:S(2)}) %collective-permute-start.10) | collective-permute-done | bytes 102432 | tf_op jit(solution)/shard_map/ppermute | solution.py:79
  29.5 1.6 %collective-permute-start.11 = (bf16[400,128]{1,0:T(8,128)(2,1)S(1)}, bf16[400,128]{1,0:T(8,128)(2,1)S(1)}, u32[]{:S(2)}, u32[]{:S(2)}) collective-permute-start(bf16[400,128]{1,0:T(8,128)(2,1)S(1)} %shard_map.84.refs_0_), channel_id=1, source_target_pairs={{0,16},{16,0},{1,17},{17,1},{2,18},{18,2},{3,19},{19,3},{4,20},{20... | collective-permute-start | bytes 307208 | tf_op jit(solution)/shard_map/ppermute | solution.py:455
  31.0 0.0 collective-permute-done.12.refs_4_
  31.0 4.0 %collective-permute-done.11.refs_1_.refs_5_ = bf16[400,128]{1,0:T(8,128)(2,1)S(1)} collective-permute-done((bf16[400,128]{1,0:T(8,128)(2,1)S(1)}, bf16[400,128]{1,0:T(8,128)(2,1)S(1)}, u32[]{:S(2)}, u32[]{:S(2)}) %collective-permute-start.11) | collective-permute-done | bytes 102432 | tf_op jit(solution)/shard_map/ppermute | solution.py:455
  35.1 0.0 collective-permute-done.13.refs_0_
  35.1 0.2 collective-permute-start.14
  35.3 1.7 %collective-permute-start.15 = (bf16[256,128]{1,0:T(8,128)(2,1)S(1)}, bf16[256,128]{1,0:T(8,128)(2,1)S(1)}, u32[]{:S(2)}, u32[]{:S(2)}) collective-permute-start(bf16[256,128]{1,0:T(8,128)(2,1)S(1)} %get-tuple-element.44), channel_id=1, source_target_pairs={{0,4},{1,5},{2,6},{3,7},{4,0},{5,1},{6,2},{7,3},{8,12},{9,13},{10,... | collective-permute-start | bytes 196616 | tf_op jit(solution)/shard_map/ppermute | solution.py:79
  37.0 0.2 collective-permute-start.16
  37.1 1.3 %shard_map.87.refs_0_ = f32[1024,128]{1,0:T(8,128)S(1)} custom-call(f32[256,128]{1,0:T(8,128)S(1)} %get-tuple-element.43.refs_1_.refs_0_.refs_3_, f32[1024,128]{1,0:T(8,128)S(1)} %shard_map.83.refs_0_.refs_1_, s32[1,5]{1,0:T(1,128)S(1)} %get-tuple-element.28.refs_1_.refs_2_, ...), custom_call_target="tpu_custom_call", output_to_operand_aliasing={{}: (1, {})} | custom-call | flops 2000000000 | tf_op jit(solution)/shard_map/pallas_call | solution.py:46
  38.5 0.0 copy-start
  38.5 0.0 collective-permute-done.14.refs_2_
  38.5 1.3 %shard_map.88.refs_0_ = f32[1024,128]{1,0:T(8,128)S(1)} custom-call(f32[1024,128]{1,0:T(8,128)S(1)} %shard_map.87.refs_0_, s32[1,5]{1,0:T(1,128)S(1)} %get-tuple-element.28.refs_1_.refs_2_, bf16[1568,128]{1,0:T(8,128)(2,1)S(1)} %collective-permute-done.14.refs_2_, ...), custom_call_target="tpu_custom_call", output_to_operand_aliasing={{}: (0, {})} | custom-call | flops 2000000000 | tf_op jit(solution)/shard_map/pallas_call | solution.py:46
  39.8 0.0 collective-permute-done.15.refs_4_
  39.8 0.0 collective-permute-done.16.refs_6_
  39.8 0.0 copy-done
  39.9 1.7 %shard_map.89 = bf16[1024,128]{1,0:T(8,128)(2,1)} custom-call(f32[1024,128]{1,0:T(8,128)S(1)} %shard_map.88.refs_0_, bf16[1024,256]{1,0:T(8,128)(2,1)S(1)} %copy-done, bf16[400,128]{1,0:T(8,128)(2,1)S(1)} %shard_map.79.refs_4_.refs_2_, f32[256,128]{1,0:T(8,128)S(1)} %get-tuple-element.43.refs_1_.refs_0_.refs_3_, ...), custom_call_target="tpu_custom_call" | custom-call | flops 2000000000 | tf_op jit(solution)/shard_map/pallas_call | solution.py:46
  (9 shorter events, 0.2 us)
Async XLA Ops:
  2.4 8.4 %collective-permute-start.1 = (bf16[1568,128]{1,0:T(8,128)(2,1)S(1)}, bf16[1568,128]{1,0:T(8,128)(2,1)S(1)}, u32[]{:S(2)}, u32[]{:S(2)}) collective-permute-start(bf16[1568,128]{1,0:T(8,128)(2,1)S(1)} %get-tuple-element.29.refs_2_), channel_id=1, source_target_pairs={{0,1},{1,0},{2,3},{3,2},{4,5},{5,4},{6,7},{7,6},{8,9},{9,8},{10,11... | collective-permute-start | bytes 1204232 | tf_op jit(solution)/shard_map/ppermute | solution.py:79
  2.9 3.1 %collective-permute-start = (bf16[400,128]{1,0:T(8,128)(2,1)S(1)}, bf16[400,128]{1,0:T(8,128)(2,1)S(1)}, u32[]{:S(2)}, u32[]{:S(2)}) collective-permute-start(bf16[400,128]{1,0:T(8,128)(2,1)S(1)} %get-tuple-element.26), channel_id=1, source_target_pairs={{0,1},{1,0},{2,3},{3,2},{4,5},{5,4},{6,7},{7,6},{8,9},{9,8},{10,11... | collective-permute-start | bytes 307208 | tf_op jit(solution)/shard_map/ppermute | solution.py:79
  3.0 5.7 %collective-permute-start.5 = (bf16[400,128]{1,0:T(8,128)(2,1)S(1)}, bf16[400,128]{1,0:T(8,128)(2,1)S(1)}, u32[]{:S(2)}, u32[]{:S(2)}) collective-permute-start(bf16[400,128]{1,0:T(8,128)(2,1)S(1)} %get-tuple-element.34.refs_0_), channel_id=1, source_target_pairs={{0,1},{1,0},{2,3},{3,2},{4,5},{5,4},{6,7},{7,6},{8,9},{9,8},{10,11... | collective-permute-start | bytes 307208 | tf_op jit(solution)/shard_map/ppermute | solution.py:79
  3.4 12.5 %collective-permute-start.2 = (bf16[1568,128]{1,0:T(8,128)(2,1)S(1)}, bf16[1568,128]{1,0:T(8,128)(2,1)S(1)}, u32[]{:S(2)}, u32[]{:S(2)}) collective-permute-start(bf16[1568,128]{1,0:T(8,128)(2,1)S(1)} %get-tuple-element.29.refs_2_), channel_id=1, source_target_pairs={{0,2},{1,3},{2,0},{3,1},{4,6},{5,7},{6,4},{7,5},{8,10},{9,11},{10,... | collective-permute-start | bytes 1204232 | tf_op jit(solution)/shard_map/ppermute | solution.py:79
  6.1 12.5 %collective-permute-start.4 = (bf16[400,128]{1,0:T(8,128)(2,1)S(1)}, bf16[400,128]{1,0:T(8,128)(2,1)S(1)}, u32[]{:S(2)}, u32[]{:S(2)}) collective-permute-start(bf16[400,128]{1,0:T(8,128)(2,1)S(1)} %get-tuple-element.27.refs_0_.refs_1_), channel_id=1, source_target_pairs={{0,8},{1,9},{2,10},{3,11},{4,12},{5,13},{6,14},{7,15},{8,0},{9,1},... | collective-permute-start | bytes 307208 | tf_op jit(solution)/shard_map/ppermute | solution.py:79
  8.7 9.8 %collective-permute-start.3 = (bf16[400,128]{1,0:T(8,128)(2,1)S(1)}, bf16[400,128]{1,0:T(8,128)(2,1)S(1)}, u32[]{:S(2)}, u32[]{:S(2)}) collective-permute-start(bf16[400,128]{1,0:T(8,128)(2,1)S(1)} %shard_map.79.refs_4_.refs_2_), channel_id=1, source_target_pairs={{0,8},{1,9},{2,10},{3,11},{4,12},{5,13},{6,14},{7,15},{8,0},{9,1},... | collective-permute-start | bytes 307208 | tf_op jit(solution)/shard_map/ppermute | solution.py:79
  15.9 13.0 %collective-permute-start.9 = (bf16[1568,128]{1,0:T(8,128)(2,1)S(1)}, bf16[1568,128]{1,0:T(8,128)(2,1)S(1)}, u32[]{:S(2)}, u32[]{:S(2)}) collective-permute-start(bf16[1568,128]{1,0:T(8,128)(2,1)S(1)} %shard_map.77.refs_2_), channel_id=1, source_target_pairs={{0,1},{1,0},{2,3},{3,2},{4,5},{5,4},{6,7},{7,6},{8,9},{9,8},{10,11... | collective-permute-start | bytes 1204232 | tf_op jit(solution)/shard_map/ppermute | solution.py:79
  18.6 6.0 %collective-permute-start.6 = (bf16[688,128]{1,0:T(8,128)(2,1)S(1)}, bf16[688,128]{1,0:T(8,128)(2,1)S(1)}, u32[]{:S(2)}, u32[]{:S(2)}) collective-permute-start(bf16[688,128]{1,0:T(8,128)(2,1)S(1)} %get-tuple-element.36.refs_0_), channel_id=1, source_target_pairs={{0,4},{1,5},{2,6},{3,7},{4,0},{5,1},{6,2},{7,3},{8,12},{9,13},{10,... | collective-permute-start | bytes 528392 | tf_op jit(solution)/shard_map/ppermute | solution.py:79
  19.4 6.8 %collective-permute-start.8 = (bf16[400,128]{1,0:T(8,128)(2,1)S(1)}, bf16[400,128]{1,0:T(8,128)(2,1)S(1)}, u32[]{:S(2)}, u32[]{:S(2)}) collective-permute-start(bf16[400,128]{1,0:T(8,128)(2,1)S(1)} %shard_map.79.refs_4_.refs_2_), channel_id=1, source_target_pairs={{0,2},{1,3},{2,0},{3,1},{4,6},{5,7},{6,4},{7,5},{8,10},{9,11},{10,... | collective-permute-start | bytes 307208 | tf_op jit(solution)/shard_map/ppermute | solution.py:79
  20.7 6.2 %collective-permute-start.7 = (bf16[400,128]{1,0:T(8,128)(2,1)S(1)}, bf16[400,128]{1,0:T(8,128)(2,1)S(1)}, u32[]{:S(2)}, u32[]{:S(2)}) collective-permute-start(bf16[400,128]{1,0:T(8,128)(2,1)S(1)} %collective-permute-done.3.refs_1_.refs_6_), channel_id=1, source_target_pairs={{0,2},{1,3},{2,0},{3,1},{4,6},{5,7},{6,4},{7,5},{8,10},{9,11},{10,... | collective-permute-start | bytes 307208 | tf_op jit(solution)/shard_map/ppermute | solution.py:79
  21.4 13.7 %collective-permute-start.13 = (bf16[1568,128]{1,0:T(8,128)(2,1)S(1)}, bf16[1568,128]{1,0:T(8,128)(2,1)S(1)}, u32[]{:S(2)}, u32[]{:S(2)}) collective-permute-start(bf16[1568,128]{1,0:T(8,128)(2,1)S(1)} %shard_map.77.refs_2_), channel_id=1, source_target_pairs={{0,4},{1,5},{4,8},{5,9},{8,12},{9,13},{6,2},{7,3},{10,6},{11,7},{1... | collective-permute-start | bytes 1204232 | tf_op jit(solution)/shard_map/ppermute | solution.py:439
  24.7 4.7 %collective-permute-start.10 = (bf16[400,128]{1,0:T(8,128)(2,1)S(1)}, bf16[400,128]{1,0:T(8,128)(2,1)S(1)}, u32[]{:S(2)}, u32[]{:S(2)}) collective-permute-start(bf16[400,128]{1,0:T(8,128)(2,1)S(1)} %get-tuple-element.38.refs_0_), channel_id=1, source_target_pairs={{0,2},{1,3},{2,0},{3,1},{4,6},{5,7},{6,4},{7,5},{8,10},{9,11},{10,... | collective-permute-start | bytes 307208 | tf_op jit(solution)/shard_map/ppermute | solution.py:79
  28.8 2.2 %collective-permute-start.12 = (bf16[512,128]{1,0:T(8,128)(2,1)S(1)}, bf16[512,128]{1,0:T(8,128)(2,1)S(1)}, u32[]{:S(2)}, u32[]{:S(2)}) collective-permute-start(bf16[512,128]{1,0:T(8,128)(2,1)S(1)} %get-tuple-element.42), channel_id=1, source_target_pairs={{0,1},{1,0},{2,3},{3,2},{4,5},{5,4},{6,7},{7,6},{8,9},{9,8},{10,11... | collective-permute-start | bytes 393224 | tf_op jit(solution)/shard_map/ppermute | solution.py:79
  29.5 5.6 %collective-permute-start.11 = (bf16[400,128]{1,0:T(8,128)(2,1)S(1)}, bf16[400,128]{1,0:T(8,128)(2,1)S(1)}, u32[]{:S(2)}, u32[]{:S(2)}) collective-permute-start(bf16[400,128]{1,0:T(8,128)(2,1)S(1)} %shard_map.84.refs_0_), channel_id=1, source_target_pairs={{0,16},{16,0},{1,17},{17,1},{2,18},{18,2},{3,19},{19,3},{4,20},{20... | collective-permute-start | bytes 307208 | tf_op jit(solution)/shard_map/ppermute | solution.py:455
  35.1 3.4 %collective-permute-start.14 = (bf16[1568,128]{1,0:T(8,128)(2,1)S(1)}, bf16[1568,128]{1,0:T(8,128)(2,1)S(1)}, u32[]{:S(2)}, u32[]{:S(2)}) collective-permute-start(bf16[1568,128]{1,0:T(8,128)(2,1)S(1)} %shard_map.86.refs_3_), channel_id=1, source_target_pairs={{0,1},{1,0},{2,3},{3,2},{4,5},{5,4},{6,7},{7,6},{8,9},{9,8},{10,11... | collective-permute-start | bytes 1204232 | tf_op jit(solution)/shard_map/ppermute | solution.py:79
  35.3 4.6 %collective-permute-start.15 = (bf16[256,128]{1,0:T(8,128)(2,1)S(1)}, bf16[256,128]{1,0:T(8,128)(2,1)S(1)}, u32[]{:S(2)}, u32[]{:S(2)}) collective-permute-start(bf16[256,128]{1,0:T(8,128)(2,1)S(1)} %get-tuple-element.44), channel_id=1, source_target_pairs={{0,4},{1,5},{2,6},{3,7},{4,0},{5,1},{6,2},{7,3},{8,12},{9,13},{10,... | collective-permute-start | bytes 196616 | tf_op jit(solution)/shard_map/ppermute | solution.py:79
  37.0 2.9 %collective-permute-start.16 = (bf16[400,128]{1,0:T(8,128)(2,1)S(1)}, bf16[400,128]{1,0:T(8,128)(2,1)S(1)}, u32[]{:S(2)}, u32[]{:S(2)}) collective-permute-start(bf16[400,128]{1,0:T(8,128)(2,1)S(1)} %collective-permute-done.11.refs_1_.refs_5_), channel_id=1, source_target_pairs={{0,1},{1,0},{2,3},{3,2},{4,5},{5,4},{6,7},{7,6},{8,9},{9,8},{10,11... | collective-permute-start | bytes 307208 | tf_op jit(solution)/shard_map/ppermute | solution.py:79
  38.5 1.4 %copy-start = (bf16[1024,256]{1,0:T(8,128)(2,1)S(1)}, bf16[1024,256]{1,0:T(8,128)(2,1)}, u32[]{:S(2)}) copy-start(bf16[1024,256]{1,0:T(8,128)(2,1)} %refs_1_.1) | copy-start | bytes 1572868

commit v6 on v5

--- a/solution.py
+++ b/solution.py
@@ -18,7 +18,7 @@
     "first_add": 1000000,
     "near_self": 2000000000,
     "near_core": 2000000000,
-    "near_beside": 2000000000,
+    "near_beside": 300000000,
     "add_a": 1000000,
     "add_b": 1000000,
     "sibling": 2000000000,
@@ -32,9 +32,8 @@
 DEADLINES = {
     "add_a": ["sv_8"],
     "sibling": ["sv_10"],
-    "field": ["packs"],
 }
-RELEASES = {"sv_0": "first_add", "halo_next": "near_core", "halo_far": "field"}
+RELEASES = {"sv_0": ["first_add"], "halo_next": ["near_core"], "halo_far": ["field", "packs"]}
 
 
 def vmem():
@@ -191,23 +190,19 @@
     def norms(turned):
         return source_scale * jnp.sum(turned * turned, axis=0, keepdims=True)
 
-    copies[0].wait()
+    for copy in copies:
+        copy.wait()
     one = (
         lax.broadcasted_iota(jnp.int32, (points, skeletons), 0) == rows_ref[...]
     ).astype(F32).astype(BF16)
-    copies[1].wait()
     skeleton = dot_nn(points_ref[...], one)
-    copies[2].wait()
     weights_turned = halo_ref[half : half + points, :].astype(F32).T.astype(BF16)
-    copies[3].wait()
     charges_turned = dot_nn(weights_turned, interp_ref[...]).astype(BF16)
-    copies[4].wait()
     ids = ids_ref[pl.ds(leaf // members, 1), :] - (leaf % members) * skeletons
     chosen = (
         lax.broadcasted_iota(jnp.int32, (skeletons, picked), 0) == ids
     ).astype(F32).astype(BF16)
     cluster = dot_nn(skeleton.astype(BF16), chosen)
-    copies[5].wait()
     sums = dot_nn(charges_turned, ci_ref[...]).T
     part = picked // 2
     rows = sum_ref.shape[0]
@@ -223,7 +218,6 @@
     send_ref[...] = all_ref[pl.ds((1 - core) * rows, rows), :].astype(BF16)
     sk_half, sk_norms = skeletons // 2, norm_rows(skeletons)
     sv_ref[:sk_half, :] = packed(skeleton).astype(BF16)
-    copies[6].wait()
     block = norm_block(norms(skeleton))
     row = lax.broadcasted_iota(jnp.int32, block.shape, 0)
     block = jnp.where(row == sk_norms - 1, flag_row(flags_ref), block)
@@ -297,7 +291,7 @@
 
 
 def sibling_kernel(masks, reduced, features, skeletons, reach, partner_ref, core_ref, *refs):
-    pieces, (own_ref, other_ref, send_ref) = refs[: len(masks)], refs[len(masks) :]
+    pieces, (own_ref, other_ref, send_ref, *form_refs) = refs[: len(masks)], refs[len(masks) :]
     leaf = lax.axis_index("leaf")
     half, points = skeletons // 2, skeletons // 2 + norm_rows(skeletons)
     start = partner_ref.shape[0] - 2 * points
@@ -309,6 +303,8 @@
     ]
     forms = zip(*[target_forms(block[:half], features) for _, block in blocks])
     low, high, parts = [jnp.concatenate(form, axis=0) for form in forms]
+    for ref, form in zip(form_refs, (low, high, parts)):
+        ref[...] = form[:skeletons]
     lane = lax.broadcasted_iota(jnp.int32, (1, LANES), 1)
     fields = [None] * len(blocks)
     for group in grouped(len(masks), half):
@@ -342,10 +338,9 @@
     send_ref[...] = (other_ref[...] + got_ref[rows:, :].astype(F32)).astype(BF16)
 
 
-def final_kernel(count, features, near_ref, interp_ref, sv_ref, own_ref, got_ref, *refs):
+def final_kernel(count, features, near_ref, interp_ref, low_ref, high_ref, parts_ref, own_ref, got_ref, *refs):
     packs, out_ref = refs[:count], refs[count]
-    skeletons = interp_ref.shape[1]
-    low, high, parts = target_forms(sv_ref[: skeletons // 2, :], features)
+    low, high, parts = low_ref[...], high_ref[...], parts_ref[...]
     half = max(r for r in range(1, packs[0].shape[0]) if 3 * r + norm_rows(2 * r) <= packs[0].shape[0])
     field = own_ref[...] + got_ref[...].astype(F32)
     for group in grouped(count, half):
@@ -414,7 +409,7 @@
         if name not in have:
             value = arrive(name)
             if name in RELEASES:
-                value = hand_on(value, done[RELEASES[name]])
+                value = hand_on(value, *[done[x] if x in done else get(x) for x in RELEASES[name]])
             have[name] = value
         return have[name]
 
@@ -500,9 +495,11 @@
             )
             token = near
         elif name == "sibling":
-            *fields, have["field_send"] = call(
+            *fields, have["field_send"], low, high, parts = call(
                 functools.partial(sibling_kernel, piece_masks, reduced, features, skeletons, reach),
-                [((skeletons, columns), F32)] * 2 + [((2 * skeletons, columns), BF16)],
+                [((skeletons, columns), F32)] * 2
+                + [((2 * skeletons, columns), BF16)]
+                + [((skeletons, columns), BF16)] * 3,
                 [have[f"sum_{reduced}"], get("sv_1")] + [get(f"sv_{m}") for m in piece_masks],
                 after=after,
                 work=work,
@@ -525,7 +522,7 @@
             (token,) = call(
                 functools.partial(final_kernel, len(packs), features),
                 [((leaf_points, columns), BF16)],
-                [near, interp, get("sv_0"), field, get("field")] + packs,
+                [near, interp, low, high, parts, field, get("field")] + packs,
                 work=work,
             )
         done[name] = token

time: 41.7 us -> 41.1 us (0.986)
    ppermute x1, waiting for transfers between devices: 4 us -> 2.82 us  [arrive(): packs += [lax.ppermute(pack, 'group', order) for pack in own_group]]
    ppermute x1, waiting for transfers between devices: 0.01 us -> 1.14 us  [arrive(): return lax.ppermute(get('halo_next'), 'leaf', ahead + behind)]
  transfers between devices with their start and end apart: 17 -> 17, of which waited for: 5 -> 6; matrix products, arithmetic and copies ran while one was open for 0% -> 0% of each run, Pallas kernels for 22% -> 22%
where the time goes in v6:
time: 41.1 us; the launch traced here: 41 us
  starting transfers between devices  17.7 us (43%)
  Pallas kernels  12.8 us (31%)
  waiting for transfers between devices  10.4 us (25%)
    ppermute x15, starting transfers between devices, xor_exchange(): lax.ppermute(value, axis, [(i, i ^ mask) for i in range(lax.axis_size(axi...  12.8 us
    pallas_call x13, Pallas kernels, call(): pl.pallas_call(lambda *refs: body(*refs[waits:]), out_shape=[jax.ShapeDty...  10.7 us
    ppermute x15, waiting for transfers between devices, xor_exchange(): lax.ppermute(value, axis, [(i, i ^ mask) for i in range(lax.axis_size(axi...  6.39 us
    ppermute x1, starting transfers between devices, arrive(): return lax.ppermute(get('halo_next'), 'leaf', ahead + behind)  3.26 us
    ppermute x1, waiting for transfers between devices, arrive(): packs += [lax.ppermute(pack, 'group', order) for pack in own_group]  2.82 us
    pallas_call x1, Pallas kernels, on_device(): pl.pallas_call(prepare_kernel, out_shape=[jax.ShapeDtypeStruct(shape, dty...  2.07 us
    ppermute x1, starting transfers between devices, arrive(): packs += [lax.ppermute(pack, 'group', order) for pack in own_group]  1.55 us
    ppermute x1, waiting for transfers between devices, arrive(): return lax.ppermute(get('halo_next'), 'leaf', ahead + behind)  1.14 us
  transfers between devices with their start and end apart: 17, of which 6 were waited for; matrix products, arithmetic and copies ran while one was open for 0% of the time, Pallas kernels for 22%

profile of v6, /device:TPU:0, one launch (start us, length us, event | category | flops | bytes accessed | tf_op | source)
XLA Modules:
  0.0 41.0 jit_solution(596856747321548578)
XLA Ops:
  0.0 2.1 %shard_map.73 = (bf16[1568,128]{1,0:T(8,128)(2,1)S(1)}, bf16[400,128]{1,0:T(8,128)(2,1)S(1)}, f32[400,128]{1,0:T(8,128)S(1)}, bf16[400,128]{1,0:T(8,128)(2,1)S(1)}, s32[1,5]{1,0:T(1,128)S(1)}) custom-call(bf16[64,1024]{1,0:T(8,128)(2,1)} %bitcast.1, bf16[1024,128]{1,0:T(8,128)(2,1)} %weights_hbm.1, bf16[1024,256]{1,0:T(8,128)(2,1)} %refs_1_.1, ...), custom_call_target="tpu_custom_call" | custom-call | flops 1000000 | tf_op jit(solution)/shard_map/pallas_call | solution.py:380
  2.1 0.5 %collective-permute-start.1 = (bf16[1568,128]{1,0:T(8,128)(2,1)S(1)}, bf16[1568,128]{1,0:T(8,128)(2,1)S(1)}, u32[]{:S(2)}, u32[]{:S(2)}) collective-permute-start(bf16[1568,128]{1,0:T(8,128)(2,1)S(1)} %get-tuple-element.32.refs_2_), channel_id=1, source_target_pairs={{0,1},{1,0},{2,3},{3,2},{4,5},{5,4},{6,7},{7,6},{8,9},{9,8},{10,11... | collective-permute-start | bytes 1204232 | tf_op jit(solution)/shard_map/ppermute | solution.py:78
  2.6 0.1 collective-permute-start
  2.7 0.4 %collective-permute-start.5 = (bf16[400,128]{1,0:T(8,128)(2,1)S(1)}, bf16[400,128]{1,0:T(8,128)(2,1)S(1)}, u32[]{:S(2)}, u32[]{:S(2)}) collective-permute-start(bf16[400,128]{1,0:T(8,128)(2,1)S(1)} %get-tuple-element.37.refs_0_), channel_id=1, source_target_pairs={{0,1},{1,0},{2,3},{3,2},{4,5},{5,4},{6,7},{7,6},{8,9},{9,8},{10,11... | collective-permute-start | bytes 307208 | tf_op jit(solution)/shard_map/ppermute | solution.py:78
  3.1 2.6 %collective-permute-start.2 = (bf16[1568,128]{1,0:T(8,128)(2,1)S(1)}, bf16[1568,128]{1,0:T(8,128)(2,1)S(1)}, u32[]{:S(2)}, u32[]{:S(2)}) collective-permute-start(bf16[1568,128]{1,0:T(8,128)(2,1)S(1)} %get-tuple-element.32.refs_2_), channel_id=1, source_target_pairs={{0,2},{1,3},{2,0},{3,1},{4,6},{5,7},{6,4},{7,5},{8,10},{9,11},{10,... | collective-permute-start | bytes 1204232 | tf_op jit(solution)/shard_map/ppermute | solution.py:78
  5.7 0.0 collective-permute-done.refs_1_
  5.7 2.7 %collective-permute-start.4 = (bf16[400,128]{1,0:T(8,128)(2,1)S(1)}, bf16[400,128]{1,0:T(8,128)(2,1)S(1)}, u32[]{:S(2)}, u32[]{:S(2)}) collective-permute-start(bf16[400,128]{1,0:T(8,128)(2,1)S(1)} %get-tuple-element.30.refs_0_.refs_1_), channel_id=1, source_target_pairs={{0,8},{1,9},{2,10},{3,11},{4,12},{5,13},{6,14},{7,15},{8,0},{9,1},... | collective-permute-start | bytes 307208 | tf_op jit(solution)/shard_map/ppermute | solution.py:78
  8.4 0.0 collective-permute-done.5.refs_5_.refs_3_
  8.4 0.3 collective-permute-start.3
  8.7 1.7 %shard_map.75 = (bf16[1024,128]{1,0:T(8,128)(2,1)S(1)}, bf16[1024,128]{1,0:T(8,128)(2,1)S(1)}, bf16[1024,128]{1,0:T(8,128)(2,1)S(1)}, f32[1024,128]{1,0:T(8,128)S(1)}) custom-call(bf16[400,128]{1,0:T(8,128)(2,1)S(1)} %get-tuple-element.30.refs_0_.refs_1_, s32[1,5]{1,0:T(1,128)S(1)} %get-tuple-element.31.refs_1_.refs_2_, ...), custom_call_target="tpu_custom_call" | custom-call | flops 2000000000 | tf_op jit(solution)/shard_map/pallas_call | solution.py:45
  10.5 0.0 collective-permute-done.1.refs_2_
  10.5 1.3 %shard_map.76.refs_1_.refs_0_ = f32[1024,128]{1,0:T(8,128)S(1)} custom-call(f32[1024,128]{1,0:T(8,128)S(1)} %get-tuple-element.33.refs_0_, s32[1,5]{1,0:T(1,128)S(1)} %get-tuple-element.31.refs_1_.refs_2_, bf16[1568,128]{1,0:T(8,128)(2,1)S(1)} %collective-permute-done.1.refs_2_, ...), custom_call_target="tpu_custom_call", output_to_operand_aliasing={{}: (0, {})} | custom-call | flops 2000000000 | tf_op jit(solution)/shard_map/pallas_call | solution.py:45
  11.8 3.8 %collective-permute-done.2.refs_0_ = bf16[1568,128]{1,0:T(8,128)(2,1)S(1)} collective-permute-done((bf16[1568,128]{1,0:T(8,128)(2,1)S(1)}, bf16[1568,128]{1,0:T(8,128)(2,1)S(1)}, u32[]{:S(2)}, u32[]{:S(2)}) %collective-permute-start.2) | collective-permute-done | bytes 401440 | tf_op jit(solution)/shard_map/ppermute | solution.py:78
  15.6 0.0 collective-permute-start.9
  15.6 1.3 %shard_map.78.refs_0_.refs_1_ = f32[1024,128]{1,0:T(8,128)S(1)} custom-call(f32[1024,128]{1,0:T(8,128)S(1)} %shard_map.76.refs_1_.refs_0_, s32[1,5]{1,0:T(1,128)S(1)} %get-tuple-element.31.refs_1_.refs_2_, bf16[1568,128]{1,0:T(8,128)(2,1)S(1)} %shard_map.77.refs_2_, ...), custom_call_target="tpu_custom_call", output_to_operand_aliasing={{}: (0, {})} | custom-call | flops 300000000 | tf_op jit(solution)/shard_map/pallas_call | solution.py:45
  16.9 0.0 collective-permute-done.4.refs_3_
  16.9 1.3 %collective-permute-done.3.refs_1_.refs_6_ = bf16[400,128]{1,0:T(8,128)(2,1)S(1)} collective-permute-done((bf16[400,128]{1,0:T(8,128)(2,1)S(1)}, bf16[400,128]{1,0:T(8,128)(2,1)S(1)}, u32[]{:S(2)}, u32[]{:S(2)}) %collective-permute-start.3) | collective-permute-done | bytes 102432 | tf_op jit(solution)/shard_map/ppermute | solution.py:78
  18.3 0.8 %collective-permute-start.6 = (bf16[688,128]{1,0:T(8,128)(2,1)S(1)}, bf16[688,128]{1,0:T(8,128)(2,1)S(1)}, u32[]{:S(2)}, u32[]{:S(2)}) collective-permute-start(bf16[688,128]{1,0:T(8,128)(2,1)S(1)} %get-tuple-element.39.refs_0_), channel_id=1, source_target_pairs={{0,4},{1,5},{2,6},{3,7},{4,0},{5,1},{6,2},{7,3},{8,12},{9,13},{10,... | collective-permute-start | bytes 528392 | tf_op jit(solution)/shard_map/ppermute | solution.py:78
  19.0 1.4 %collective-permute-start.8 = (bf16[400,128]{1,0:T(8,128)(2,1)S(1)}, bf16[400,128]{1,0:T(8,128)(2,1)S(1)}, u32[]{:S(2)}, u32[]{:S(2)}) collective-permute-start(bf16[400,128]{1,0:T(8,128)(2,1)S(1)} %shard_map.79.refs_4_), channel_id=1, source_target_pairs={{0,2},{1,3},{2,0},{3,1},{4,6},{5,7},{6,4},{7,5},{8,10},{9,11},{10,... | collective-permute-start | bytes 307208 | tf_op jit(solution)/shard_map/ppermute | solution.py:78
  20.4 0.7 %collective-permute-start.7 = (bf16[400,128]{1,0:T(8,128)(2,1)S(1)}, bf16[400,128]{1,0:T(8,128)(2,1)S(1)}, u32[]{:S(2)}, u32[]{:S(2)}) collective-permute-start(bf16[400,128]{1,0:T(8,128)(2,1)S(1)} %collective-permute-done.3.refs_1_.refs_6_), channel_id=1, source_target_pairs={{0,2},{1,3},{2,0},{3,1},{4,6},{5,7},{6,4},{7,5},{8,10},{9,11},{10,... | collective-permute-start | bytes 307208 | tf_op jit(solution)/shard_map/ppermute | solution.py:78
  21.0 3.3 %collective-permute-start.12 = (bf16[1568,128]{1,0:T(8,128)(2,1)S(1)}, bf16[1568,128]{1,0:T(8,128)(2,1)S(1)}, u32[]{:S(2)}, u32[]{:S(2)}) collective-permute-start(bf16[1568,128]{1,0:T(8,128)(2,1)S(1)} %shard_map.77.refs_2_), channel_id=1, source_target_pairs={{0,4},{1,5},{4,8},{5,9},{8,12},{9,13},{6,2},{7,3},{10,6},{11,7},{1... | collective-permute-start | bytes 1204232 | tf_op jit(solution)/shard_map/ppermute | solution.py:434
  24.3 0.0 collective-permute-done.6.refs_2_
  24.4 1.4 %collective-permute-start.10 = (bf16[400,128]{1,0:T(8,128)(2,1)S(1)}, bf16[400,128]{1,0:T(8,128)(2,1)S(1)}, u32[]{:S(2)}, u32[]{:S(2)}) collective-permute-start(bf16[400,128]{1,0:T(8,128)(2,1)S(1)} %get-tuple-element.41.refs_0_), channel_id=1, source_target_pairs={{0,2},{1,3},{2,0},{3,1},{4,6},{5,7},{6,4},{7,5},{8,10},{9,11},{10,... | collective-permute-start | bytes 307208 | tf_op jit(solution)/shard_map/ppermute | solution.py:78
  25.8 0.0 collective-permute-done.8.refs_5_
  25.8 0.8 %collective-permute-done.7.refs_1_.refs_7_ = bf16[400,128]{1,0:T(8,128)(2,1)S(1)} collective-permute-done((bf16[400,128]{1,0:T(8,128)(2,1)S(1)}, bf16[400,128]{1,0:T(8,128)(2,1)S(1)}, u32[]{:S(2)}, u32[]{:S(2)}) %collective-permute-start.7) | collective-permute-done | bytes 102432 | tf_op jit(solution)/shard_map/ppermute | solution.py:78
  26.6 1.9 %shard_map.82 = (f32[256,128]{1,0:T(8,128)S(1)}, f32[256,128]{1,0:T(8,128)S(1)}, bf16[512,128]{1,0:T(8,128)(2,1)S(1)}, bf16[256,128]{1,0:T(8,128)(2,1)S(1)}, bf1...) custom-call(bf16[400,128]{1,0:T(8,128)(2,1)S(1)} %get-tuple-element.41.refs_0_, ...), custom_call_target="tpu_custom_call" | custom-call | flops 2000000000 | tf_op jit(solution)/shard_map/pallas_call | solution.py:45
  28.5 0.1 collective-permute-start.11
  28.6 0.0 collective-permute-done.9.refs_3_
  28.6 0.5 %collective-permute-done.10.refs_2_ = bf16[400,128]{1,0:T(8,128)(2,1)S(1)} collective-permute-done((bf16[400,128]{1,0:T(8,128)(2,1)S(1)}, bf16[400,128]{1,0:T(8,128)(2,1)S(1)}, u32[]{:S(2)}, u32[]{:S(2)}) %collective-permute-start.10) | collective-permute-done | bytes 102432 | tf_op jit(solution)/shard_map/ppermute | solution.py:78
  29.1 1.6 %collective-permute-start.13 = (bf16[400,128]{1,0:T(8,128)(2,1)S(1)}, bf16[400,128]{1,0:T(8,128)(2,1)S(1)}, u32[]{:S(2)}, u32[]{:S(2)}) collective-permute-start(bf16[400,128]{1,0:T(8,128)(2,1)S(1)} %shard_map.84.refs_0_), channel_id=1, source_target_pairs={{0,16},{16,0},{1,17},{17,1},{2,18},{18,2},{3,19},{19,3},{4,20},{20... | collective-permute-start | bytes 307208 | tf_op jit(solution)/shard_map/ppermute | solution.py:450
  30.7 0.0 collective-permute-done.11.refs_3_
  30.7 1.1 %collective-permute-done.12.refs_0_ = bf16[1568,128]{1,0:T(8,128)(2,1)S(1)} collective-permute-done((bf16[1568,128]{1,0:T(8,128)(2,1)S(1)}, bf16[1568,128]{1,0:T(8,128)(2,1)S(1)}, u32[]{:S(2)}, u32[]{:S(2)}) %collective-permute-start.12) | collective-permute-done | bytes 401440 | tf_op jit(solution)/shard_map/ppermute | solution.py:434
  31.8 2.8 %collective-permute-done.13.refs_2_.refs_7_ = bf16[400,128]{1,0:T(8,128)(2,1)S(1)} collective-permute-done((bf16[400,128]{1,0:T(8,128)(2,1)S(1)}, bf16[400,128]{1,0:T(8,128)(2,1)S(1)}, u32[]{:S(2)}, u32[]{:S(2)}) %collective-permute-start.13) | collective-permute-done | bytes 102432 | tf_op jit(solution)/shard_map/ppermute | solution.py:450
  34.7 0.1 collective-permute-start.14
  34.8 1.6 %collective-permute-start.15 = (bf16[256,128]{1,0:T(8,128)(2,1)S(1)}, bf16[256,128]{1,0:T(8,128)(2,1)S(1)}, u32[]{:S(2)}, u32[]{:S(2)}) collective-permute-start(bf16[256,128]{1,0:T(8,128)(2,1)S(1)} %get-tuple-element.50), channel_id=1, source_target_pairs={{0,4},{1,5},{2,6},{3,7},{4,0},{5,1},{6,2},{7,3},{8,12},{9,13},{10,... | collective-permute-start | bytes 196616 | tf_op jit(solution)/shard_map/ppermute | solution.py:78
  36.4 0.2 collective-permute-start.16
  36.6 1.3 %shard_map.87.refs_0_ = f32[1024,128]{1,0:T(8,128)S(1)} custom-call(f32[256,128]{1,0:T(8,128)S(1)} %get-tuple-element.46.refs_1_.refs_0_.refs_5_, f32[1024,128]{1,0:T(8,128)S(1)} %shard_map.83.refs_0_.refs_1_, s32[1,5]{1,0:T(1,128)S(1)} %get-tuple-element.31.refs_1_.refs_2_, ...), custom_call_target="tpu_custom_call", output_to_operand_aliasing={{}: (1, {})} | custom-call | flops 2000000000 | tf_op jit(solution)/shard_map/pallas_call | solution.py:45
  38.0 0.0 copy-start
  38.0 0.0 collective-permute-done.14.refs_2_
  38.0 1.3 %shard_map.88.refs_0_ = f32[1024,128]{1,0:T(8,128)S(1)} custom-call(f32[1024,128]{1,0:T(8,128)S(1)} %shard_map.87.refs_0_, s32[1,5]{1,0:T(1,128)S(1)} %get-tuple-element.31.refs_1_.refs_2_, bf16[1568,128]{1,0:T(8,128)(2,1)S(1)} %collective-permute-done.14.refs_2_, ...), custom_call_target="tpu_custom_call", output_to_operand_aliasing={{}: (0, {})} | custom-call | flops 2000000000 | tf_op jit(solution)/shard_map/pallas_call | solution.py:45
  39.3 0.0 collective-permute-done.15.refs_6_
  39.4 0.0 collective-permute-done.16.refs_8_
  39.4 0.0 copy-done
  39.4 1.6 %shard_map.89 = bf16[1024,128]{1,0:T(8,128)(2,1)} custom-call(f32[1024,128]{1,0:T(8,128)S(1)} %shard_map.88.refs_0_, bf16[1024,256]{1,0:T(8,128)(2,1)S(1)} %copy-done, bf16[256,128]{1,0:T(8,128)(2,1)S(1)} %get-tuple-element.47.refs_2_, bf16[256,128]{1,0:T(8,128)(2,1)S(1)} %get-tuple-element.48.refs_3_, bf16[256,128]{1,0:T(8,128)(2,1)S(1)} %get-tuple-element.49.refs_4_, ...), custom_call_target="tpu_custom_call" | custom-call | flops 2000000000 | tf_op jit(solution)/shard_map/pallas_call | solution.py:45
  (9 shorter events, 0.2 us)
Async XLA Ops:
  2.1 8.4 %collective-permute-start.1 = (bf16[1568,128]{1,0:T(8,128)(2,1)S(1)}, bf16[1568,128]{1,0:T(8,128)(2,1)S(1)}, u32[]{:S(2)}, u32[]{:S(2)}) collective-permute-start(bf16[1568,128]{1,0:T(8,128)(2,1)S(1)} %get-tuple-element.32.refs_2_), channel_id=1, source_target_pairs={{0,1},{1,0},{2,3},{3,2},{4,5},{5,4},{6,7},{7,6},{8,9},{9,8},{10,11... | collective-permute-start | bytes 1204232 | tf_op jit(solution)/shard_map/ppermute | solution.py:78
  2.6 3.1 %collective-permute-start = (bf16[400,128]{1,0:T(8,128)(2,1)S(1)}, bf16[400,128]{1,0:T(8,128)(2,1)S(1)}, u32[]{:S(2)}, u32[]{:S(2)}) collective-permute-start(bf16[400,128]{1,0:T(8,128)(2,1)S(1)} %get-tuple-element.29), channel_id=1, source_target_pairs={{0,1},{1,0},{2,3},{3,2},{4,5},{5,4},{6,7},{7,6},{8,9},{9,8},{10,11... | collective-permute-start | bytes 307208 | tf_op jit(solution)/shard_map/ppermute | solution.py:78
  2.7 5.7 %collective-permute-start.5 = (bf16[400,128]{1,0:T(8,128)(2,1)S(1)}, bf16[400,128]{1,0:T(8,128)(2,1)S(1)}, u32[]{:S(2)}, u32[]{:S(2)}) collective-permute-start(bf16[400,128]{1,0:T(8,128)(2,1)S(1)} %get-tuple-element.37.refs_0_), channel_id=1, source_target_pairs={{0,1},{1,0},{2,3},{3,2},{4,5},{5,4},{6,7},{7,6},{8,9},{9,8},{10,11... | collective-permute-start | bytes 307208 | tf_op jit(solution)/shard_map/ppermute | solution.py:78
  3.1 12.5 %collective-permute-start.2 = (bf16[1568,128]{1,0:T(8,128)(2,1)S(1)}, bf16[1568,128]{1,0:T(8,128)(2,1)S(1)}, u32[]{:S(2)}, u32[]{:S(2)}) collective-permute-start(bf16[1568,128]{1,0:T(8,128)(2,1)S(1)} %get-tuple-element.32.refs_2_), channel_id=1, source_target_pairs={{0,2},{1,3},{2,0},{3,1},{4,6},{5,7},{6,4},{7,5},{8,10},{9,11},{10,... | collective-permute-start | bytes 1204232 | tf_op jit(solution)/shard_map/ppermute | solution.py:78
  5.7 11.2 %collective-permute-start.4 = (bf16[400,128]{1,0:T(8,128)(2,1)S(1)}, bf16[400,128]{1,0:T(8,128)(2,1)S(1)}, u32[]{:S(2)}, u32[]{:S(2)}) collective-permute-start(bf16[400,128]{1,0:T(8,128)(2,1)S(1)} %get-tuple-element.30.refs_0_.refs_1_), channel_id=1, source_target_pairs={{0,8},{1,9},{2,10},{3,11},{4,12},{5,13},{6,14},{7,15},{8,0},{9,1},... | collective-permute-start | bytes 307208 | tf_op jit(solution)/shard_map/ppermute | solution.py:78
  8.4 9.8 %collective-permute-start.3 = (bf16[400,128]{1,0:T(8,128)(2,1)S(1)}, bf16[400,128]{1,0:T(8,128)(2,1)S(1)}, u32[]{:S(2)}, u32[]{:S(2)}) collective-permute-start(bf16[400,128]{1,0:T(8,128)(2,1)S(1)} %shard_map.79.refs_4_), channel_id=1, source_target_pairs={{0,8},{1,9},{2,10},{3,11},{4,12},{5,13},{6,14},{7,15},{8,0},{9,1},... | collective-permute-start | bytes 307208 | tf_op jit(solution)/shard_map/ppermute | solution.py:78
  15.6 13.0 %collective-permute-start.9 = (bf16[1568,128]{1,0:T(8,128)(2,1)S(1)}, bf16[1568,128]{1,0:T(8,128)(2,1)S(1)}, u32[]{:S(2)}, u32[]{:S(2)}) collective-permute-start(bf16[1568,128]{1,0:T(8,128)(2,1)S(1)} %shard_map.77.refs_2_), channel_id=1, source_target_pairs={{0,1},{1,0},{2,3},{3,2},{4,5},{5,4},{6,7},{7,6},{8,9},{9,8},{10,11... | collective-permute-start | bytes 1204232 | tf_op jit(solution)/shard_map/ppermute | solution.py:78
  18.3 6.0 %collective-permute-start.6 = (bf16[688,128]{1,0:T(8,128)(2,1)S(1)}, bf16[688,128]{1,0:T(8,128)(2,1)S(1)}, u32[]{:S(2)}, u32[]{:S(2)}) collective-permute-start(bf16[688,128]{1,0:T(8,128)(2,1)S(1)} %get-tuple-element.39.refs_0_), channel_id=1, source_target_pairs={{0,4},{1,5},{2,6},{3,7},{4,0},{5,1},{6,2},{7,3},{8,12},{9,13},{10,... | collective-permute-start | bytes 528392 | tf_op jit(solution)/shard_map/ppermute | solution.py:78
  19.0 6.8 %collective-permute-start.8 = (bf16[400,128]{1,0:T(8,128)(2,1)S(1)}, bf16[400,128]{1,0:T(8,128)(2,1)S(1)}, u32[]{:S(2)}, u32[]{:S(2)}) collective-permute-start(bf16[400,128]{1,0:T(8,128)(2,1)S(1)} %shard_map.79.refs_4_), channel_id=1, source_target_pairs={{0,2},{1,3},{2,0},{3,1},{4,6},{5,7},{6,4},{7,5},{8,10},{9,11},{10,... | collective-permute-start | bytes 307208 | tf_op jit(solution)/shard_map/ppermute | solution.py:78
  20.4 6.2 %collective-permute-start.7 = (bf16[400,128]{1,0:T(8,128)(2,1)S(1)}, bf16[400,128]{1,0:T(8,128)(2,1)S(1)}, u32[]{:S(2)}, u32[]{:S(2)}) collective-permute-start(bf16[400,128]{1,0:T(8,128)(2,1)S(1)} %collective-permute-done.3.refs_1_.refs_6_), channel_id=1, source_target_pairs={{0,2},{1,3},{2,0},{3,1},{4,6},{5,7},{6,4},{7,5},{8,10},{9,11},{10,... | collective-permute-start | bytes 307208 | tf_op jit(solution)/shard_map/ppermute | solution.py:78
  21.0 10.8 %collective-permute-start.12 = (bf16[1568,128]{1,0:T(8,128)(2,1)S(1)}, bf16[1568,128]{1,0:T(8,128)(2,1)S(1)}, u32[]{:S(2)}, u32[]{:S(2)}) collective-permute-start(bf16[1568,128]{1,0:T(8,128)(2,1)S(1)} %shard_map.77.refs_2_), channel_id=1, source_target_pairs={{0,4},{1,5},{4,8},{5,9},{8,12},{9,13},{6,2},{7,3},{10,6},{11,7},{1... | collective-permute-start | bytes 1204232 | tf_op jit(solution)/shard_map/ppermute | solution.py:434
  24.4 4.7 %collective-permute-start.10 = (bf16[400,128]{1,0:T(8,128)(2,1)S(1)}, bf16[400,128]{1,0:T(8,128)(2,1)S(1)}, u32[]{:S(2)}, u32[]{:S(2)}) collective-permute-start(bf16[400,128]{1,0:T(8,128)(2,1)S(1)} %get-tuple-element.41.refs_0_), channel_id=1, source_target_pairs={{0,2},{1,3},{2,0},{3,1},{4,6},{5,7},{6,4},{7,5},{8,10},{9,11},{10,... | collective-permute-start | bytes 307208 | tf_op jit(solution)/shard_map/ppermute | solution.py:78
  28.5 2.2 %collective-permute-start.11 = (bf16[512,128]{1,0:T(8,128)(2,1)S(1)}, bf16[512,128]{1,0:T(8,128)(2,1)S(1)}, u32[]{:S(2)}, u32[]{:S(2)}) collective-permute-start(bf16[512,128]{1,0:T(8,128)(2,1)S(1)} %get-tuple-element.45), channel_id=1, source_target_pairs={{0,1},{1,0},{2,3},{3,2},{4,5},{5,4},{6,7},{7,6},{8,9},{9,8},{10,11... | collective-permute-start | bytes 393224 | tf_op jit(solution)/shard_map/ppermute | solution.py:78
  29.1 5.6 %collective-permute-start.13 = (bf16[400,128]{1,0:T(8,128)(2,1)S(1)}, bf16[400,128]{1,0:T(8,128)(2,1)S(1)}, u32[]{:S(2)}, u32[]{:S(2)}) collective-permute-start(bf16[400,128]{1,0:T(8,128)(2,1)S(1)} %shard_map.84.refs_0_), channel_id=1, source_target_pairs={{0,16},{16,0},{1,17},{17,1},{2,18},{18,2},{3,19},{19,3},{4,20},{20... | collective-permute-start | bytes 307208 | tf_op jit(solution)/shard_map/ppermute | solution.py:450
  34.7 3.3 %collective-permute-start.14 = (bf16[1568,128]{1,0:T(8,128)(2,1)S(1)}, bf16[1568,128]{1,0:T(8,128)(2,1)S(1)}, u32[]{:S(2)}, u32[]{:S(2)}) collective-permute-start(bf16[1568,128]{1,0:T(8,128)(2,1)S(1)} %shard_map.86.refs_3_), channel_id=1, source_target_pairs={{0,1},{1,0},{2,3},{3,2},{4,5},{5,4},{6,7},{7,6},{8,9},{9,8},{10,11... | collective-permute-start | bytes 1204232 | tf_op jit(solution)/shard_map/ppermute | solution.py:78
  34.8 4.6 %collective-permute-start.15 = (bf16[256,128]{1,0:T(8,128)(2,1)S(1)}, bf16[256,128]{1,0:T(8,128)(2,1)S(1)}, u32[]{:S(2)}, u32[]{:S(2)}) collective-permute-start(bf16[256,128]{1,0:T(8,128)(2,1)S(1)} %get-tuple-element.50), channel_id=1, source_target_pairs={{0,4},{1,5},{2,6},{3,7},{4,0},{5,1},{6,2},{7,3},{8,12},{9,13},{10,... | collective-permute-start | bytes 196616 | tf_op jit(solution)/shard_map/ppermute | solution.py:78
  36.4 2.9 %collective-permute-start.16 = (bf16[400,128]{1,0:T(8,128)(2,1)S(1)}, bf16[400,128]{1,0:T(8,128)(2,1)S(1)}, u32[]{:S(2)}, u32[]{:S(2)}) collective-permute-start(bf16[400,128]{1,0:T(8,128)(2,1)S(1)} %collective-permute-done.13.refs_2_.refs_7_), channel_id=1, source_target_pairs={{0,1},{1,0},{2,3},{3,2},{4,5},{5,4},{6,7},{7,6},{8,9},{9,8},{10,11... | collective-permute-start | bytes 307208 | tf_op jit(solution)/shard_map/ppermute | solution.py:78
  38.0 1.4 %copy-start = (bf16[1024,256]{1,0:T(8,128)(2,1)S(1)}, bf16[1024,256]{1,0:T(8,128)(2,1)}, u32[]{:S(2)}) copy-start(bf16[1024,256]{1,0:T(8,128)(2,1)} %refs_1_.1) | copy-start | bytes 1572868

commit v7 on v6

--- a/solution.py
+++ b/solution.py
@@ -15,23 +15,23 @@
 TARGET_ROWS = 512
 SOURCE_ROWS = 512
 ORDER = {
-    "first_add": 1000000,
+    "first_add": 8000000000,
     "near_self": 2000000000,
     "near_core": 2000000000,
-    "near_beside": 300000000,
+    "near_beside": 4000000000,
     "add_a": 1000000,
     "add_b": 1000000,
     "sibling": 2000000000,
     "near_across": 2000000000,
-    "add_c": 1000000,
+    "add_c": 10000000,
     "field": 1000000,
     "near_far": 2000000000,
     "near_last": 2000000000,
     "final": 2000000000,
 }
 DEADLINES = {
-    "add_a": ["sv_8"],
     "sibling": ["sv_10"],
+    "add_c": ["sv_8"],
 }
 RELEASES = {"sv_0": ["first_add"], "halo_next": ["near_core"], "halo_far": ["field", "packs"]}
 

time: 41.1 us -> 40.3 us (0.981)
  waiting for transfers between devices: 10.4 us -> 8.17 us
  starting transfers between devices: 17.7 us -> 19 us
    ppermute x15, waiting for transfers between devices: 6.39 us -> 4.3 us  [xor_exchange(): lax.ppermute(value, axis, [(i, i ^ mask) for i in range(lax.axis_size(axi...]
    ppermute x15, starting transfers between devices: 12.8 us -> 14.8 us  [xor_exchange(): lax.ppermute(value, axis, [(i, i ^ mask) for i in range(lax.axis_size(axi...]
    ppermute x1, starting transfers between devices: 3.26 us -> 2.52 us  [arrive(): return lax.ppermute(get('halo_next'), 'leaf', ahead + behind)]
  transfers between devices with their start and end apart: 17 -> 17, of which waited for: 6 -> 7; matrix products, arithmetic and copies ran while one was open for 0% -> 0% of each run, Pallas kernels for 22% -> 23%
where the time goes in v7:
time: 40.3 us; the launch traced here: 40.1 us
  starting transfers between devices  19 us (47%)
  Pallas kernels  12.8 us (32%)
  waiting for transfers between devices  8.17 us (20%)
    ppermute x15, starting transfers between devices, xor_exchange(): lax.ppermute(value, axis, [(i, i ^ mask) for i in range(lax.axis_size(axi...  14.8 us
    pallas_call x13, Pallas kernels, call(): pl.pallas_call(lambda *refs: body(*refs[waits:]), out_shape=[jax.ShapeDty...  10.7 us
    ppermute x15, waiting for transfers between devices, xor_exchange(): lax.ppermute(value, axis, [(i, i ^ mask) for i in range(lax.axis_size(axi...  4.3 us
    ppermute x1, waiting for transfers between devices, arrive(): packs += [lax.ppermute(pack, 'group', order) for pack in own_group]  2.56 us
    ppermute x1, starting transfers between devices, arrive(): return lax.ppermute(get('halo_next'), 'leaf', ahead + behind)  2.52 us
    pallas_call x1, Pallas kernels, on_device(): pl.pallas_call(prepare_kernel, out_shape=[jax.ShapeDtypeStruct(shape, dty...  2.07 us
    ppermute x1, starting transfers between devices, arrive(): packs += [lax.ppermute(pack, 'group', order) for pack in own_group]  1.72 us
    ppermute x1, waiting for transfers between devices, arrive(): return lax.ppermute(get('halo_next'), 'leaf', ahead + behind)  1.31 us
  transfers between devices with their start and end apart: 17, of which 7 were waited for; matrix products, arithmetic and copies ran while one was open for 0% of the time, Pallas kernels for 23%

profile of v7, /device:TPU:0, one launch (start us, length us, event | category | flops | bytes accessed | tf_op | source)
XLA Modules:
  0.0 40.1 jit_solution(7622141882652574869)
XLA Ops:
  0.0 2.1 %shard_map.73 = (bf16[1568,128]{1,0:T(8,128)(2,1)S(1)}, bf16[400,128]{1,0:T(8,128)(2,1)S(1)}, f32[400,128]{1,0:T(8,128)S(1)}, bf16[400,128]{1,0:T(8,128)(2,1)S(1)}, s32[1,5]{1,0:T(1,128)S(1)}) custom-call(bf16[64,1024]{1,0:T(8,128)(2,1)} %bitcast.1, bf16[1024,128]{1,0:T(8,128)(2,1)} %weights_hbm.1, bf16[1024,256]{1,0:T(8,128)(2,1)} %refs_1_.1, ...), custom_call_target="tpu_custom_call" | custom-call | flops 1000000 | tf_op jit(solution)/shard_map/pallas_call | solution.py:380
  2.1 0.5 %collective-permute-start = (bf16[400,128]{1,0:T(8,128)(2,1)S(1)}, bf16[400,128]{1,0:T(8,128)(2,1)S(1)}, u32[]{:S(2)}, u32[]{:S(2)}) collective-permute-start(bf16[400,128]{1,0:T(8,128)(2,1)S(1)} %get-tuple-element.29), channel_id=1, source_target_pairs={{0,1},{1,0},{2,3},{3,2},{4,5},{5,4},{6,7},{7,6},{8,9},{9,8},{10,11... | collective-permute-start | bytes 307208 | tf_op jit(solution)/shard_map/ppermute | solution.py:78
  2.6 2.6 %collective-permute-start.2 = (bf16[1568,128]{1,0:T(8,128)(2,1)S(1)}, bf16[1568,128]{1,0:T(8,128)(2,1)S(1)}, u32[]{:S(2)}, u32[]{:S(2)}) collective-permute-start(bf16[1568,128]{1,0:T(8,128)(2,1)S(1)} %get-tuple-element.32.refs_2_), channel_id=1, source_target_pairs={{0,2},{1,3},{2,0},{3,1},{4,6},{5,7},{6,4},{7,5},{8,10},{9,11},{10,... | collective-permute-start | bytes 1204232 | tf_op jit(solution)/shard_map/ppermute | solution.py:78
  5.2 0.2 collective-permute-start.1
  5.4 0.3 collective-permute-start.4
  5.7 0.0 collective-permute-done.refs_1_
  5.7 2.7 %collective-permute-start.3 = (bf16[400,128]{1,0:T(8,128)(2,1)S(1)}, bf16[400,128]{1,0:T(8,128)(2,1)S(1)}, u32[]{:S(2)}, u32[]{:S(2)}) collective-permute-start(bf16[400,128]{1,0:T(8,128)(2,1)S(1)} %get-tuple-element.30.refs_0_.refs_1_), channel_id=1, source_target_pairs={{0,8},{1,9},{2,10},{3,11},{4,12},{5,13},{6,14},{7,15},{8,0},{9,1},... | collective-permute-start | bytes 307208 | tf_op jit(solution)/shard_map/ppermute | solution.py:78
  8.4 0.0 collective-permute-done.4.refs_4_.refs_3_
  8.4 1.3 %collective-permute-start.6 = (bf16[400,128]{1,0:T(8,128)(2,1)S(1)}, bf16[400,128]{1,0:T(8,128)(2,1)S(1)}, u32[]{:S(2)}, u32[]{:S(2)}) collective-permute-start(bf16[400,128]{1,0:T(8,128)(2,1)S(1)} %shard_map.79.refs_3_.refs_4_), channel_id=1, source_target_pairs={{0,8},{1,9},{2,10},{3,11},{4,12},{5,13},{6,14},{7,15},{8,0},{9,1},... | collective-permute-start | bytes 307208 | tf_op jit(solution)/shard_map/ppermute | solution.py:78
  9.7 1.7 %shard_map.75 = (bf16[1024,128]{1,0:T(8,128)(2,1)S(1)}, bf16[1024,128]{1,0:T(8,128)(2,1)S(1)}, bf16[1024,128]{1,0:T(8,128)(2,1)S(1)}, f32[1024,128]{1,0:T(8,128)S(1)}) custom-call(bf16[400,128]{1,0:T(8,128)(2,1)S(1)} %get-tuple-element.30.refs_0_.refs_1_, s32[1,5]{1,0:T(1,128)S(1)} %get-tuple-element.31.refs_1_.refs_2_, ...), custom_call_target="tpu_custom_call" | custom-call | flops 2000000000 | tf_op jit(solution)/shard_map/pallas_call | solution.py:45
  11.4 0.0 collective-permute-done.1.refs_2_
  11.4 1.3 %shard_map.76.refs_1_.refs_0_ = f32[1024,128]{1,0:T(8,128)S(1)} custom-call(f32[1024,128]{1,0:T(8,128)S(1)} %get-tuple-element.33.refs_0_, s32[1,5]{1,0:T(1,128)S(1)} %get-tuple-element.31.refs_1_.refs_2_, bf16[1568,128]{1,0:T(8,128)(2,1)S(1)} %collective-permute-done.1.refs_2_, ...), custom_call_target="tpu_custom_call", output_to_operand_aliasing={{}: (0, {})} | custom-call | flops 2000000000 | tf_op jit(solution)/shard_map/pallas_call | solution.py:45
  12.7 2.3 %collective-permute-done.2.refs_0_ = bf16[1568,128]{1,0:T(8,128)(2,1)S(1)} collective-permute-done((bf16[1568,128]{1,0:T(8,128)(2,1)S(1)}, bf16[1568,128]{1,0:T(8,128)(2,1)S(1)}, u32[]{:S(2)}, u32[]{:S(2)}) %collective-permute-start.2) | collective-permute-done | bytes 401440 | tf_op jit(solution)/shard_map/ppermute | solution.py:78
  15.1 0.0 collective-permute-start.9
  15.1 1.3 %shard_map.78.refs_0_.refs_1_ = f32[1024,128]{1,0:T(8,128)S(1)} custom-call(f32[1024,128]{1,0:T(8,128)S(1)} %shard_map.76.refs_1_.refs_0_, s32[1,5]{1,0:T(1,128)S(1)} %get-tuple-element.31.refs_1_.refs_2_, bf16[1568,128]{1,0:T(8,128)(2,1)S(1)} %shard_map.77.refs_2_, ...), custom_call_target="tpu_custom_call", output_to_operand_aliasing={{}: (0, {})} | custom-call | flops 4000000000 | tf_op jit(solution)/shard_map/pallas_call | solution.py:45
  16.4 0.4 %collective-permute-done.3.refs_2_ = bf16[400,128]{1,0:T(8,128)(2,1)S(1)} collective-permute-done((bf16[400,128]{1,0:T(8,128)(2,1)S(1)}, bf16[400,128]{1,0:T(8,128)(2,1)S(1)}, u32[]{:S(2)}, u32[]{:S(2)}) %collective-permute-start.3) | collective-permute-done | bytes 102432 | tf_op jit(solution)/shard_map/ppermute | solution.py:78
  16.8 1.5 %collective-permute-start.5 = (bf16[688,128]{1,0:T(8,128)(2,1)S(1)}, bf16[688,128]{1,0:T(8,128)(2,1)S(1)}, u32[]{:S(2)}, u32[]{:S(2)}) collective-permute-start(bf16[688,128]{1,0:T(8,128)(2,1)S(1)} %get-tuple-element.39.refs_0_), channel_id=1, source_target_pairs={{0,4},{1,5},{2,6},{3,7},{4,0},{5,1},{6,2},{7,3},{8,12},{9,13},{10,... | collective-permute-start | bytes 528392 | tf_op jit(solution)/shard_map/ppermute | solution.py:78
  18.3 1.5 %collective-permute-start.8 = (bf16[400,128]{1,0:T(8,128)(2,1)S(1)}, bf16[400,128]{1,0:T(8,128)(2,1)S(1)}, u32[]{:S(2)}, u32[]{:S(2)}) collective-permute-start(bf16[400,128]{1,0:T(8,128)(2,1)S(1)} %shard_map.79.refs_3_.refs_4_), channel_id=1, source_target_pairs={{0,2},{1,3},{2,0},{3,1},{4,6},{5,7},{6,4},{7,5},{8,10},{9,11},{10,... | collective-permute-start | bytes 307208 | tf_op jit(solution)/shard_map/ppermute | solution.py:78
  19.8 0.0 collective-permute-done.6.refs_6_.refs_1_
  19.8 0.5 %collective-permute-start.7 = (bf16[400,128]{1,0:T(8,128)(2,1)S(1)}, bf16[400,128]{1,0:T(8,128)(2,1)S(1)}, u32[]{:S(2)}, u32[]{:S(2)}) collective-permute-start(bf16[400,128]{1,0:T(8,128)(2,1)S(1)} %collective-permute-done.6.refs_6_.refs_1_), channel_id=1, source_target_pairs={{0,2},{1,3},{2,0},{3,1},{4,6},{5,7},{6,4},{7,5},{8,10},{9,11},{10,... | collective-permute-start | bytes 307208 | tf_op jit(solution)/shard_map/ppermute | solution.py:78
  20.4 2.5 %collective-permute-start.12 = (bf16[1568,128]{1,0:T(8,128)(2,1)S(1)}, bf16[1568,128]{1,0:T(8,128)(2,1)S(1)}, u32[]{:S(2)}, u32[]{:S(2)}) collective-permute-start(bf16[1568,128]{1,0:T(8,128)(2,1)S(1)} %shard_map.77.refs_2_), channel_id=1, source_target_pairs={{0,4},{1,5},{4,8},{5,9},{8,12},{9,13},{6,2},{7,3},{10,6},{11,7},{1... | collective-permute-start | bytes 1204232 | tf_op jit(solution)/shard_map/ppermute | solution.py:434
  22.9 0.6 %collective-permute-done.5.refs_2_ = bf16[688,128]{1,0:T(8,128)(2,1)S(1)} collective-permute-done((bf16[688,128]{1,0:T(8,128)(2,1)S(1)}, bf16[688,128]{1,0:T(8,128)(2,1)S(1)}, u32[]{:S(2)}, u32[]{:S(2)}) %collective-permute-start.5) | collective-permute-done | bytes 176160 | tf_op jit(solution)/shard_map/ppermute | solution.py:78
  23.5 1.8 %collective-permute-start.10 = (bf16[400,128]{1,0:T(8,128)(2,1)S(1)}, bf16[400,128]{1,0:T(8,128)(2,1)S(1)}, u32[]{:S(2)}, u32[]{:S(2)}) collective-permute-start(bf16[400,128]{1,0:T(8,128)(2,1)S(1)} %get-tuple-element.41.refs_0_), channel_id=1, source_target_pairs={{0,2},{1,3},{2,0},{3,1},{4,6},{5,7},{6,4},{7,5},{8,10},{9,11},{10,... | collective-permute-start | bytes 307208 | tf_op jit(solution)/shard_map/ppermute | solution.py:78
  25.3 0.0 collective-permute-done.8.refs_5_
  25.3 0.3 collective-permute-done.7.refs_1_.refs_7_
  25.5 1.9 %shard_map.82 = (f32[256,128]{1,0:T(8,128)S(1)}, f32[256,128]{1,0:T(8,128)S(1)}, bf16[512,128]{1,0:T(8,128)(2,1)S(1)}, bf16[256,128]{1,0:T(8,128)(2,1)S(1)}, bf1...) custom-call(bf16[400,128]{1,0:T(8,128)(2,1)S(1)} %get-tuple-element.41.refs_0_, ...), custom_call_target="tpu_custom_call" | custom-call | flops 2000000000 | tf_op jit(solution)/shard_map/pallas_call | solution.py:45
  27.4 0.1 collective-permute-start.11
  27.5 0.0 collective-permute-done.9.refs_3_
  27.6 0.7 %collective-permute-done.10.refs_3_ = bf16[400,128]{1,0:T(8,128)(2,1)S(1)} collective-permute-done((bf16[400,128]{1,0:T(8,128)(2,1)S(1)}, bf16[400,128]{1,0:T(8,128)(2,1)S(1)}, u32[]{:S(2)}, u32[]{:S(2)}) %collective-permute-start.10) | collective-permute-done | bytes 102432 | tf_op jit(solution)/shard_map/ppermute | solution.py:78
  28.3 1.7 %collective-permute-start.13 = (bf16[400,128]{1,0:T(8,128)(2,1)S(1)}, bf16[400,128]{1,0:T(8,128)(2,1)S(1)}, u32[]{:S(2)}, u32[]{:S(2)}) collective-permute-start(bf16[400,128]{1,0:T(8,128)(2,1)S(1)} %shard_map.84.refs_0_), channel_id=1, source_target_pairs={{0,16},{16,0},{1,17},{17,1},{2,18},{18,2},{3,19},{19,3},{4,20},{20... | collective-permute-start | bytes 307208 | tf_op jit(solution)/shard_map/ppermute | solution.py:450
  30.0 0.0 collective-permute-done.11.refs_3_
  30.0 1.3 %collective-permute-done.12.refs_0_ = bf16[1568,128]{1,0:T(8,128)(2,1)S(1)} collective-permute-done((bf16[1568,128]{1,0:T(8,128)(2,1)S(1)}, bf16[1568,128]{1,0:T(8,128)(2,1)S(1)}, u32[]{:S(2)}, u32[]{:S(2)}) %collective-permute-start.12) | collective-permute-done | bytes 401440 | tf_op jit(solution)/shard_map/ppermute | solution.py:434
  31.3 2.6 %collective-permute-done.13.refs_2_.refs_7_ = bf16[400,128]{1,0:T(8,128)(2,1)S(1)} collective-permute-done((bf16[400,128]{1,0:T(8,128)(2,1)S(1)}, bf16[400,128]{1,0:T(8,128)(2,1)S(1)}, u32[]{:S(2)}, u32[]{:S(2)}) %collective-permute-start.13) | collective-permute-done | bytes 102432 | tf_op jit(solution)/shard_map/ppermute | solution.py:450
  33.9 0.1 collective-permute-start.14
  34.0 1.6 %collective-permute-start.15 = (bf16[256,128]{1,0:T(8,128)(2,1)S(1)}, bf16[256,128]{1,0:T(8,128)(2,1)S(1)}, u32[]{:S(2)}, u32[]{:S(2)}) collective-permute-start(bf16[256,128]{1,0:T(8,128)(2,1)S(1)} %get-tuple-element.50), channel_id=1, source_target_pairs={{0,4},{1,5},{2,6},{3,7},{4,0},{5,1},{6,2},{7,3},{8,12},{9,13},{10,... | collective-permute-start | bytes 196616 | tf_op jit(solution)/shard_map/ppermute | solution.py:78
  35.6 0.2 collective-permute-start.16
  35.8 1.3 %shard_map.87.refs_0_ = f32[1024,128]{1,0:T(8,128)S(1)} custom-call(f32[256,128]{1,0:T(8,128)S(1)} %get-tuple-element.46.refs_1_.refs_0_.refs_5_, f32[1024,128]{1,0:T(8,128)S(1)} %shard_map.83.refs_0_.refs_1_, s32[1,5]{1,0:T(1,128)S(1)} %get-tuple-element.31.refs_1_.refs_2_, ...), custom_call_target="tpu_custom_call", output_to_operand_aliasing={{}: (1, {})} | custom-call | flops 2000000000 | tf_op jit(solution)/shard_map/pallas_call | solution.py:45
  37.1 0.0 copy-start
  37.1 0.0 collective-permute-done.14.refs_2_
  37.1 1.4 %shard_map.88.refs_0_ = f32[1024,128]{1,0:T(8,128)S(1)} custom-call(f32[1024,128]{1,0:T(8,128)S(1)} %shard_map.87.refs_0_, s32[1,5]{1,0:T(1,128)S(1)} %get-tuple-element.31.refs_1_.refs_2_, bf16[1568,128]{1,0:T(8,128)(2,1)S(1)} %collective-permute-done.14.refs_2_, ...), custom_call_target="tpu_custom_call", output_to_operand_aliasing={{}: (0, {})} | custom-call | flops 2000000000 | tf_op jit(solution)/shard_map/pallas_call | solution.py:45
  38.5 0.0 collective-permute-done.15.refs_6_
  38.5 0.0 collective-permute-done.16.refs_8_
  38.5 0.0 copy-done
  38.6 1.6 %shard_map.89 = bf16[1024,128]{1,0:T(8,128)(2,1)} custom-call(f32[1024,128]{1,0:T(8,128)S(1)} %shard_map.88.refs_0_, bf16[1024,256]{1,0:T(8,128)(2,1)S(1)} %copy-done, bf16[256,128]{1,0:T(8,128)(2,1)S(1)} %get-tuple-element.47.refs_2_, bf16[256,128]{1,0:T(8,128)(2,1)S(1)} %get-tuple-element.48.refs_3_, bf16[256,128]{1,0:T(8,128)(2,1)S(1)} %get-tuple-element.49.refs_4_, ...), custom_call_target="tpu_custom_call" | custom-call | flops 2000000000 | tf_op jit(solution)/shard_map/pallas_call | solution.py:45
  (9 shorter events, 0.2 us)
Async XLA Ops:
  2.1 3.6 %collective-permute-start = (bf16[400,128]{1,0:T(8,128)(2,1)S(1)}, bf16[400,128]{1,0:T(8,128)(2,1)S(1)}, u32[]{:S(2)}, u32[]{:S(2)}) collective-permute-start(bf16[400,128]{1,0:T(8,128)(2,1)S(1)} %get-tuple-element.29), channel_id=1, source_target_pairs={{0,1},{1,0},{2,3},{3,2},{4,5},{5,4},{6,7},{7,6},{8,9},{9,8},{10,11... | collective-permute-start | bytes 307208 | tf_op jit(solution)/shard_map/ppermute | solution.py:78
  2.6 12.5 %collective-permute-start.2 = (bf16[1568,128]{1,0:T(8,128)(2,1)S(1)}, bf16[1568,128]{1,0:T(8,128)(2,1)S(1)}, u32[]{:S(2)}, u32[]{:S(2)}) collective-permute-start(bf16[1568,128]{1,0:T(8,128)(2,1)S(1)} %get-tuple-element.32.refs_2_), channel_id=1, source_target_pairs={{0,2},{1,3},{2,0},{3,1},{4,6},{5,7},{6,4},{7,5},{8,10},{9,11},{10,... | collective-permute-start | bytes 1204232 | tf_op jit(solution)/shard_map/ppermute | solution.py:78
  5.2 6.2 %collective-permute-start.1 = (bf16[1568,128]{1,0:T(8,128)(2,1)S(1)}, bf16[1568,128]{1,0:T(8,128)(2,1)S(1)}, u32[]{:S(2)}, u32[]{:S(2)}) collective-permute-start(bf16[1568,128]{1,0:T(8,128)(2,1)S(1)} %get-tuple-element.32.refs_2_), channel_id=1, source_target_pairs={{0,1},{1,0},{2,3},{3,2},{4,5},{5,4},{6,7},{7,6},{8,9},{9,8},{10,11... | collective-permute-start | bytes 1204232 | tf_op jit(solution)/shard_map/ppermute | solution.py:78
  5.4 3.0 %collective-permute-start.4 = (bf16[400,128]{1,0:T(8,128)(2,1)S(1)}, bf16[400,128]{1,0:T(8,128)(2,1)S(1)}, u32[]{:S(2)}, u32[]{:S(2)}) collective-permute-start(bf16[400,128]{1,0:T(8,128)(2,1)S(1)} %get-tuple-element.38.refs_0_), channel_id=1, source_target_pairs={{0,1},{1,0},{2,3},{3,2},{4,5},{5,4},{6,7},{7,6},{8,9},{9,8},{10,11... | collective-permute-start | bytes 307208 | tf_op jit(solution)/shard_map/ppermute | solution.py:78
  5.7 11.1 %collective-permute-start.3 = (bf16[400,128]{1,0:T(8,128)(2,1)S(1)}, bf16[400,128]{1,0:T(8,128)(2,1)S(1)}, u32[]{:S(2)}, u32[]{:S(2)}) collective-permute-start(bf16[400,128]{1,0:T(8,128)(2,1)S(1)} %get-tuple-element.30.refs_0_.refs_1_), channel_id=1, source_target_pairs={{0,8},{1,9},{2,10},{3,11},{4,12},{5,13},{6,14},{7,15},{8,0},{9,1},... | collective-permute-start | bytes 307208 | tf_op jit(solution)/shard_map/ppermute | solution.py:78
  8.4 11.5 %collective-permute-start.6 = (bf16[400,128]{1,0:T(8,128)(2,1)S(1)}, bf16[400,128]{1,0:T(8,128)(2,1)S(1)}, u32[]{:S(2)}, u32[]{:S(2)}) collective-permute-start(bf16[400,128]{1,0:T(8,128)(2,1)S(1)} %shard_map.79.refs_3_.refs_4_), channel_id=1, source_target_pairs={{0,8},{1,9},{2,10},{3,11},{4,12},{5,13},{6,14},{7,15},{8,0},{9,1},... | collective-permute-start | bytes 307208 | tf_op jit(solution)/shard_map/ppermute | solution.py:78
  15.1 12.4 %collective-permute-start.9 = (bf16[1568,128]{1,0:T(8,128)(2,1)S(1)}, bf16[1568,128]{1,0:T(8,128)(2,1)S(1)}, u32[]{:S(2)}, u32[]{:S(2)}) collective-permute-start(bf16[1568,128]{1,0:T(8,128)(2,1)S(1)} %shard_map.77.refs_2_), channel_id=1, source_target_pairs={{0,1},{1,0},{2,3},{3,2},{4,5},{5,4},{6,7},{7,6},{8,9},{9,8},{10,11... | collective-permute-start | bytes 1204232 | tf_op jit(solution)/shard_map/ppermute | solution.py:78
  16.8 6.6 %collective-permute-start.5 = (bf16[688,128]{1,0:T(8,128)(2,1)S(1)}, bf16[688,128]{1,0:T(8,128)(2,1)S(1)}, u32[]{:S(2)}, u32[]{:S(2)}) collective-permute-start(bf16[688,128]{1,0:T(8,128)(2,1)S(1)} %get-tuple-element.39.refs_0_), channel_id=1, source_target_pairs={{0,4},{1,5},{2,6},{3,7},{4,0},{5,1},{6,2},{7,3},{8,12},{9,13},{10,... | collective-permute-start | bytes 528392 | tf_op jit(solution)/shard_map/ppermute | solution.py:78
  18.3 6.9 %collective-permute-start.8 = (bf16[400,128]{1,0:T(8,128)(2,1)S(1)}, bf16[400,128]{1,0:T(8,128)(2,1)S(1)}, u32[]{:S(2)}, u32[]{:S(2)}) collective-permute-start(bf16[400,128]{1,0:T(8,128)(2,1)S(1)} %shard_map.79.refs_3_.refs_4_), channel_id=1, source_target_pairs={{0,2},{1,3},{2,0},{3,1},{4,6},{5,7},{6,4},{7,5},{8,10},{9,11},{10,... | collective-permute-start | bytes 307208 | tf_op jit(solution)/shard_map/ppermute | solution.py:78
  19.8 5.7 %collective-permute-start.7 = (bf16[400,128]{1,0:T(8,128)(2,1)S(1)}, bf16[400,128]{1,0:T(8,128)(2,1)S(1)}, u32[]{:S(2)}, u32[]{:S(2)}) collective-permute-start(bf16[400,128]{1,0:T(8,128)(2,1)S(1)} %collective-permute-done.6.refs_6_.refs_1_), channel_id=1, source_target_pairs={{0,2},{1,3},{2,0},{3,1},{4,6},{5,7},{6,4},{7,5},{8,10},{9,11},{10,... | collective-permute-start | bytes 307208 | tf_op jit(solution)/shard_map/ppermute | solution.py:78
  20.4 11.0 %collective-permute-start.12 = (bf16[1568,128]{1,0:T(8,128)(2,1)S(1)}, bf16[1568,128]{1,0:T(8,128)(2,1)S(1)}, u32[]{:S(2)}, u32[]{:S(2)}) collective-permute-start(bf16[1568,128]{1,0:T(8,128)(2,1)S(1)} %shard_map.77.refs_2_), channel_id=1, source_target_pairs={{0,4},{1,5},{4,8},{5,9},{8,12},{9,13},{6,2},{7,3},{10,6},{11,7},{1... | collective-permute-start | bytes 1204232 | tf_op jit(solution)/shard_map/ppermute | solution.py:434
  23.5 4.7 %collective-permute-start.10 = (bf16[400,128]{1,0:T(8,128)(2,1)S(1)}, bf16[400,128]{1,0:T(8,128)(2,1)S(1)}, u32[]{:S(2)}, u32[]{:S(2)}) collective-permute-start(bf16[400,128]{1,0:T(8,128)(2,1)S(1)} %get-tuple-element.41.refs_0_), channel_id=1, source_target_pairs={{0,2},{1,3},{2,0},{3,1},{4,6},{5,7},{6,4},{7,5},{8,10},{9,11},{10,... | collective-permute-start | bytes 307208 | tf_op jit(solution)/shard_map/ppermute | solution.py:78
  27.4 2.5 %collective-permute-start.11 = (bf16[512,128]{1,0:T(8,128)(2,1)S(1)}, bf16[512,128]{1,0:T(8,128)(2,1)S(1)}, u32[]{:S(2)}, u32[]{:S(2)}) collective-permute-start(bf16[512,128]{1,0:T(8,128)(2,1)S(1)} %get-tuple-element.45), channel_id=1, source_target_pairs={{0,1},{1,0},{2,3},{3,2},{4,5},{5,4},{6,7},{7,6},{8,9},{9,8},{10,11... | collective-permute-start | bytes 393224 | tf_op jit(solution)/shard_map/ppermute | solution.py:78
  28.3 5.6 %collective-permute-start.13 = (bf16[400,128]{1,0:T(8,128)(2,1)S(1)}, bf16[400,128]{1,0:T(8,128)(2,1)S(1)}, u32[]{:S(2)}, u32[]{:S(2)}) collective-permute-start(bf16[400,128]{1,0:T(8,128)(2,1)S(1)} %shard_map.84.refs_0_), channel_id=1, source_target_pairs={{0,16},{16,0},{1,17},{17,1},{2,18},{18,2},{3,19},{19,3},{4,20},{20... | collective-permute-start | bytes 307208 | tf_op jit(solution)/shard_map/ppermute | solution.py:450
  33.9 3.3 %collective-permute-start.14 = (bf16[1568,128]{1,0:T(8,128)(2,1)S(1)}, bf16[1568,128]{1,0:T(8,128)(2,1)S(1)}, u32[]{:S(2)}, u32[]{:S(2)}) collective-permute-start(bf16[1568,128]{1,0:T(8,128)(2,1)S(1)} %shard_map.86.refs_3_), channel_id=1, source_target_pairs={{0,1},{1,0},{2,3},{3,2},{4,5},{5,4},{6,7},{7,6},{8,9},{9,8},{10,11... | collective-permute-start | bytes 1204232 | tf_op jit(solution)/shard_map/ppermute | solution.py:78
  34.0 4.5 %collective-permute-start.15 = (bf16[256,128]{1,0:T(8,128)(2,1)S(1)}, bf16[256,128]{1,0:T(8,128)(2,1)S(1)}, u32[]{:S(2)}, u32[]{:S(2)}) collective-permute-start(bf16[256,128]{1,0:T(8,128)(2,1)S(1)} %get-tuple-element.50), channel_id=1, source_target_pairs={{0,4},{1,5},{2,6},{3,7},{4,0},{5,1},{6,2},{7,3},{8,12},{9,13},{10,... | collective-permute-start | bytes 196616 | tf_op jit(solution)/shard_map/ppermute | solution.py:78
  35.6 3.0 %collective-permute-start.16 = (bf16[400,128]{1,0:T(8,128)(2,1)S(1)}, bf16[400,128]{1,0:T(8,128)(2,1)S(1)}, u32[]{:S(2)}, u32[]{:S(2)}) collective-permute-start(bf16[400,128]{1,0:T(8,128)(2,1)S(1)} %collective-permute-done.13.refs_2_.refs_7_), channel_id=1, source_target_pairs={{0,1},{1,0},{2,3},{3,2},{4,5},{5,4},{6,7},{7,6},{8,9},{9,8},{10,11... | collective-permute-start | bytes 307208 | tf_op jit(solution)/shard_map/ppermute | solution.py:78
  37.1 1.4 %copy-start = (bf16[1024,256]{1,0:T(8,128)(2,1)S(1)}, bf16[1024,256]{1,0:T(8,128)(2,1)}, u32[]{:S(2)}) copy-start(bf16[1024,256]{1,0:T(8,128)(2,1)} %refs_1_.1) | copy-start | bytes 1572868
